TPU v7x, 1024 devices: a whole 4x4x32 slice. The times are simulated.
1024 devices in a mesh: gx: 16 (over z_lo), gy: 8 (over y, core), gz: 8 (over z_hi, x).
Axes of the slice: x: 4, y: 4, z: 32 (z_hi: 2, z_lo: 16; z = z_hi * 16 + z_lo), core: 2. Of those that a mesh axis runs over, the one named last changes fastest.
Arguments:
- iterate: float32 [4, 128, 64, 1024], P(None, 'gx', 'gy', 'gz'), may hold values from -4 to 4
- forcing: float32 [4, 128, 64, 1024], P(None, 'gx', 'gy', 'gz'), may hold values from -6 to 6
- viscosity: float32 [3, 128, 64, 1024], P(None, 'gx', 'gy', 'gz'), may hold values from 0.1 to 10
Outputs:
- updated: float32 [4, 128, 64, 1024], P(None, 'gx', 'gy', 'gz')
All inputs are finite; a program needn't handle non-finite values.
Results may differ from a plain program's by a relative error of at most 0.00002.
Values sent between devices are 32-bit elements; how exact they have to be, the bound alone decides.
No kernel may reach another device: no remote copies, remote signals or barrier semaphores. Data moves between devices by JAX's collectives and lax.ppermute only.
A program may use at most 64 MiB of HBM per device.

v0:
```python
import jax
import jax.numpy as jnp
from jax import lax
from jax.sharding import PartitionSpec as P

VELOCITY_DAMPING = 0.6
PRESSURE_DAMPING = 0.5


def extended(cells, sides, width):
    for axis, dim in sides:
        count = lax.axis_size(axis)
        ends = count - 1
        head = lax.slice_in_dim(cells, 0, width, axis=dim)
        tail = lax.slice_in_dim(cells, cells.shape[dim] - width, cells.shape[dim], axis=dim)
        cells = jnp.concatenate(
            [
                lax.ppermute(tail, axis, [(i, (i + 1) % count) for i in range(ends)]),
                cells,
                lax.ppermute(head, axis, [((i + 1) % count, i) for i in range(ends)]),
            ],
            axis=dim,
        )
    return cells


def beside(source, axis_num, offset):
    window = [slice(1, source.shape[i] - 1) for i in range(3)]
    window[axis_num] = slice(1 + offset, source.shape[axis_num] - 1 + offset)
    return source[tuple(window)]


def velocity_residual(padded, viscous, forcing, spacing):
    pressure = padded[3]
    residuals = []
    diagonals = []
    for c in range(3):
        moving = padded[c]
        eta_face = viscous[c]
        center = beside(moving, 0, 0)
        eta_center = beside(eta_face, 0, 0)
        summed = jnp.zeros_like(center)
        diagonal = jnp.zeros_like(center)
        for d in range(3):
            for s in (-1, 1):
                weight = 0.5 * (eta_center + beside(eta_face, d, s))
                summed = summed + weight * (center - beside(moving, d, s))
                diagonal = diagonal + weight
        gradient = (beside(pressure, 0, 0) - beside(pressure, c, -1)) / spacing
        residuals.append(forcing[c] - summed / (spacing * spacing) - gradient)
        diagonals.append(diagonal / (spacing * spacing))
    return (jnp.stack(residuals), jnp.stack(diagonals))


def divergence(padded_velocity, spacing):
    summed = beside(padded_velocity[0], 0, 1) - beside(padded_velocity[0], 0, 0)
    for c in range(1, 3):
        summed = summed + (beside(padded_velocity[c], c, 1) - beside(padded_velocity[c], 0, 0))
    return summed / spacing


def cell_viscosity(viscous):
    summed = beside(viscous[0], 0, 0) + beside(viscous[0], 0, 1)
    for c in range(1, 3):
        summed = summed + beside(viscous[c], 0, 0) + beside(viscous[c], c, 1)
    return summed / 6.0


def restrict(values):
    extents = values.shape
    blocks = values.reshape(extents[0], extents[1] // 2, 2, extents[2] // 2, 2, extents[3] // 2, 2)
    return blocks.mean(axis=(2, 4, 6))


def prolong(values):
    return jnp.repeat(jnp.repeat(jnp.repeat(values, 2, axis=1), 2, axis=2), 2, axis=3)


def rims(values, width):
    return extended(values, (("gx", 1), ("gy", 2), ("gz", 3)), width)


def level_viscosity(viscosity, padder):
    viscous = padder(viscosity, 1)
    return viscous


def smooth_level(iterate, forcing, viscous, spacing, padder):
    extent = forcing.shape[1:]
    if iterate is None:
        padded = jnp.zeros((4, extent[0] + 2, extent[1] + 2, extent[2] + 2), jnp.float32)
    else:
        padded = padder(iterate, 1)
    residuals, diagonals = velocity_residual(padded, viscous, forcing, spacing)
    velocity = padded[:3, 1:-1, 1:-1, 1:-1] + VELOCITY_DAMPING * residuals / diagonals
    outflow = divergence(padder(velocity, 1), spacing)
    mass_resid = forcing[3] + outflow
    old_pressure = jnp.zeros_like(forcing[3]) if iterate is None else iterate[3]
    pressure = old_pressure - PRESSURE_DAMPING * cell_viscosity(viscous) * mass_resid
    return jnp.concatenate([velocity, pressure[None]], axis=0)


def level_residual(iterate, forcing, viscous, spacing, padder):
    padded = padder(iterate, 1)
    residuals = velocity_residual(padded, viscous, forcing, spacing)[0]
    mass_resid = forcing[3] + divergence(padded[:3], spacing)
    return jnp.concatenate([residuals, mass_resid[None]], axis=0)


def per_device(iterate, forcing, viscosity):
    viscous_mid = restrict(viscosity)
    viscous_low = restrict(viscous_mid)
    eta_fine = level_viscosity(viscosity, rims)
    finest = smooth_level(iterate, forcing, eta_fine, 1.0, rims)
    forcing_mid = restrict(level_residual(finest, forcing, eta_fine, 1.0, rims))
    eta_mid = level_viscosity(viscous_mid, rims)
    middle = smooth_level(None, forcing_mid, eta_mid, 2.0, rims)
    forcing_low = restrict(level_residual(middle, forcing_mid, eta_mid, 2.0, rims))
    eta_low = level_viscosity(viscous_low, rims)
    lowest = smooth_level(None, forcing_low, eta_low, 4.0, rims)
    middle = smooth_level(middle + prolong(lowest), forcing_mid, eta_mid, 2.0, rims)
    finest = smooth_level(finest + prolong(middle), forcing, eta_fine, 1.0, rims)
    return finest


def solution(mesh):
    placed = (P(None, "gx", "gy", "gz"), P(None, "gx", "gy", "gz"), P(None, "gx", "gy", "gz"))
    return jax.shard_map(
        per_device, mesh=mesh, in_specs=placed, out_specs=P(None, "gx", "gy", "gz"), check_vma=False
    )
```

profile of v0, /device:TPU:39, one launch (start us, length us, event | category | flops | bytes accessed | tf_op | source)
XLA Modules:
  0.0 778.9 jit_solution(4542226846115220792)
XLA Ops:
  10.5 8.5 %reshape.43 = f32[3,4,2,4,2,64,2]{6,5,4,3,2,1,0:T(8,128)} reshape(f32[3,8,8,128]{3,2,1,0:T(8,128)} %param.5) | data formatting | bytes 196608 | tf_op jit(solution)/shard_map/reshape | solution.py:71
  56.6 25.9 %collective-permute-start.4 = (f32[3,10,10,1]{3,0,2,1:T(4,128)S(1)}, f32[3,10,10,1]{3,0,2,1:T(4,128)S(1)}, u32[]{:S(2)}, u32[]{:S(2)}) collective-permute-start(f32[3,10,10,1]{3,0,2,1:T(4,128)S(1)} %get-tuple-element.86), channel_id=1, source_target_pairs={{0,1},{1,2},{2,3},{3,4},{4,5},{5,6},{6,7},{8,9},{9,10},{10,11},{11... | collective-permute-start | bytes 3608 | tf_op jit(solution)/shard_map/ppermute | solution.py:18
  84.5 32.8 %collective-permute-done.4 = f32[3,10,10,1]{3,0,2,1:T(4,128)S(1)} collective-permute-done((f32[3,10,10,1]{3,0,2,1:T(4,128)S(1)}, f32[3,10,10,1]{3,0,2,1:T(4,128)S(1)}, u32[]{:S(2)}, u32[]{:S(2)}) %collective-permute-start.4) | collective-permute-done | bytes 1232 | tf_op jit(solution)/shard_map/ppermute | solution.py:18
  121.6 20.4 %collective-permute-done.5 = f32[3,10,10,1]{3,0,2,1:T(4,128)S(1)} collective-permute-done((f32[3,10,10,1]{3,0,2,1:T(4,128)S(1)}, f32[3,10,10,1]{3,0,2,1:T(4,128)S(1)}, u32[]{:S(2)}, u32[]{:S(2)}) %collective-permute-start.5) | collective-permute-done | bytes 1232 | tf_op jit(solution)/shard_map/ppermute | solution.py:20
  153.9 6.2 collective-permute-done.10
  162.3 22.5 %collective-permute-done.11 = f32[4,10,10,1]{3,0,2,1:T(4,128)S(1)} collective-permute-done((f32[4,10,10,1]{3,0,2,1:T(4,128)S(1)}, f32[4,10,10,1]{3,0,2,1:T(4,128)S(1)}, u32[]{:S(2)}, u32[]{:S(2)}) %collective-permute-start.11) | collective-permute-done | bytes 1632 | tf_op jit(solution)/shard_map/ppermute | solution.py:20
  192.5 6.5 collective-permute-start.14
  209.7 22.4 %collective-permute-start.16 = (f32[3,10,10,1]{3,0,2,1:T(4,128)S(1)}, f32[3,10,10,1]{3,0,2,1:T(4,128)S(1)}, u32[]{:S(2)}, u32[]{:S(2)}) collective-permute-start(f32[3,10,10,1]{3,0,2,1:T(4,128)S(1)} %get-tuple-element.84), channel_id=1, source_target_pairs={{0,1},{1,2},{2,3},{3,4},{4,5},{5,6},{6,7},{8,9},{9,10},{10,11},{11... | collective-permute-start | bytes 3608 | tf_op jit(solution)/shard_map/ppermute | solution.py:18
  234.2 22.6 %collective-permute-done.16 = f32[3,10,10,1]{3,0,2,1:T(4,128)S(1)} collective-permute-done((f32[3,10,10,1]{3,0,2,1:T(4,128)S(1)}, f32[3,10,10,1]{3,0,2,1:T(4,128)S(1)}, u32[]{:S(2)}, u32[]{:S(2)}) %collective-permute-start.16) | collective-permute-done | bytes 1232 | tf_op jit(solution)/shard_map/ppermute | solution.py:18
  256.8 24.6 %collective-permute-done.17 = f32[3,10,10,1]{3,0,2,1:T(4,128)S(1)} collective-permute-done((f32[3,10,10,1]{3,0,2,1:T(4,128)S(1)}, f32[3,10,10,1]{3,0,2,1:T(4,128)S(1)}, u32[]{:S(2)}, u32[]{:S(2)}) %collective-permute-start.17) | collective-permute-done | bytes 1232 | tf_op jit(solution)/shard_map/ppermute | solution.py:20
  288.6 7.0 collective-permute-done.19
  311.1 16.7 %collective-permute-done.22 = f32[4,10,10,1]{3,0,2,1:T(4,128)S(1)} collective-permute-done((f32[4,10,10,1]{3,0,2,1:T(4,128)S(1)}, f32[4,10,10,1]{3,0,2,1:T(4,128)S(1)}, u32[]{:S(2)}, u32[]{:S(2)}) %collective-permute-start.22) | collective-permute-done | bytes 1632 | tf_op jit(solution)/shard_map/ppermute | solution.py:18
  327.8 24.6 %collective-permute-done.23 = f32[4,10,10,1]{3,0,2,1:T(4,128)S(1)} collective-permute-done((f32[4,10,10,1]{3,0,2,1:T(4,128)S(1)}, f32[4,10,10,1]{3,0,2,1:T(4,128)S(1)}, u32[]{:S(2)}, u32[]{:S(2)}) %collective-permute-start.23) | collective-permute-done | bytes 1632 | tf_op jit(solution)/shard_map/ppermute | solution.py:20
  388.8 22.4 %collective-permute-start.34 = (f32[3,6,6,1]{3,2,1,0:T(8,128)S(1)}, f32[3,6,6,1]{3,2,1,0:T(8,128)S(1)}, u32[]{:S(2)}, u32[]{:S(2)}) collective-permute-start(f32[3,6,6,1]{3,2,1,0:T(8,128)S(1)} %get-tuple-element.134), channel_id=1, source_target_pairs={{0,1},{1,2},{2,3},{3,4},{4,5},{5,6},{6,7},{8,9},{9,10},{10,11},{11... | collective-permute-start | bytes 1304 | tf_op jit(solution)/shard_map/ppermute | solution.py:18
  413.3 23.5 %collective-permute-done.35 = f32[3,6,6,1]{3,2,1,0:T(8,128)S(1)} collective-permute-done((f32[3,6,6,1]{3,2,1,0:T(8,128)S(1)}, f32[3,6,6,1]{3,2,1,0:T(8,128)S(1)}, u32[]{:S(2)}, u32[]{:S(2)}) %collective-permute-start.35) | collective-permute-done | bytes 464 | tf_op jit(solution)/shard_map/ppermute | solution.py:20
  443.5 7.1 collective-permute-start.38
  461.2 23.8 %collective-permute-done.41 = f32[4,6,6,1]{3,0,2,1:T(4,128)S(1)} collective-permute-done((f32[4,6,6,1]{3,0,2,1:T(4,128)S(1)}, f32[4,6,6,1]{3,0,2,1:T(4,128)S(1)}, u32[]{:S(2)}, u32[]{:S(2)}) %collective-permute-start.41) | collective-permute-done | bytes 608 | tf_op jit(solution)/shard_map/ppermute | solution.py:20
  508.6 21.6 %collective-permute-done.53 = f32[3,4,4,1]{3,2,1,0:T(4,128)S(1)} collective-permute-done((f32[3,4,4,1]{3,2,1,0:T(4,128)S(1)}, f32[3,4,4,1]{3,2,1,0:T(4,128)S(1)}, u32[]{:S(2)}, u32[]{:S(2)}) %collective-permute-start.53) | collective-permute-done | bytes 224 | tf_op jit(solution)/shard_map/ppermute | solution.py:20
  552.3 23.4 %collective-permute-done.59 = f32[4,6,6,1]{3,0,2,1:T(4,128)S(1)} collective-permute-done((f32[4,6,6,1]{3,0,2,1:T(4,128)S(1)}, f32[4,6,6,1]{3,0,2,1:T(4,128)S(1)}, u32[]{:S(2)}, u32[]{:S(2)}) %collective-permute-start.59) | collective-permute-done | bytes 608 | tf_op jit(solution)/shard_map/ppermute | solution.py:20
  599.4 24.8 %collective-permute-done.65 = f32[3,6,6,1]{3,2,1,0:T(8,128)S(1)} collective-permute-done((f32[3,6,6,1]{3,2,1,0:T(8,128)S(1)}, f32[3,6,6,1]{3,2,1,0:T(8,128)S(1)}, u32[]{:S(2)}, u32[]{:S(2)}) %collective-permute-start.65) | collective-permute-done | bytes 464 | tf_op jit(solution)/shard_map/ppermute | solution.py:20
  646.7 30.8 %collective-permute-done.70 = f32[4,10,10,1]{3,0,2,1:T(4,128)S(1)} collective-permute-done((f32[4,10,10,1]{3,0,2,1:T(4,128)S(1)}, f32[4,10,10,1]{3,0,2,1:T(4,128)S(1)}, u32[]{:S(2)}, u32[]{:S(2)}) %collective-permute-start.70) | collective-permute-done | bytes 1632 | tf_op jit(solution)/shard_map/ppermute | solution.py:18
  677.6 24.8 %collective-permute-done.71 = f32[4,10,10,1]{3,0,2,1:T(4,128)S(1)} collective-permute-done((f32[4,10,10,1]{3,0,2,1:T(4,128)S(1)}, f32[4,10,10,1]{3,0,2,1:T(4,128)S(1)}, u32[]{:S(2)}, u32[]{:S(2)}) %collective-permute-start.71) | collective-permute-done | bytes 1632 | tf_op jit(solution)/shard_map/ppermute | solution.py:20
  724.3 28.1 %collective-permute-done.76 = f32[3,10,10,1]{3,0,2,1:T(4,128)S(1)} collective-permute-done((f32[3,10,10,1]{3,0,2,1:T(4,128)S(1)}, f32[3,10,10,1]{3,0,2,1:T(4,128)S(1)}, u32[]{:S(2)}, u32[]{:S(2)}) %collective-permute-start.76) | collective-permute-done | bytes 1232 | tf_op jit(solution)/shard_map/ppermute | solution.py:18
  752.4 24.6 %collective-permute-done.77 = f32[3,10,10,1]{3,0,2,1:T(4,128)S(1)} collective-permute-done((f32[3,10,10,1]{3,0,2,1:T(4,128)S(1)}, f32[3,10,10,1]{3,0,2,1:T(4,128)S(1)}, u32[]{:S(2)}, u32[]{:S(2)}) %collective-permute-start.77) | collective-permute-done | bytes 1232 | tf_op jit(solution)/shard_map/ppermute | solution.py:20
  (425 shorter events, 280.2 us)
Async XLA Ops:
  0.7 45.4 %collective-permute-start.1 = (f32[3,1,8,128]{3,2,1,0:T(8,128)S(1)}, f32[3,1,8,128]{3,2,1,0:T(8,128)S(1)}, u32[]{:S(2)}, u32[]{:S(2)}) collective-permute-start(f32[3,1,8,128]{3,2,1,0:T(8,128)S(1)} %get-tuple-element.112), channel_id=1, source_target_pairs={{64,0},{128,64},{192,128},{256,192},{320,256},{384,320},{448,384},... | collective-permute-start | bytes 36872 | tf_op jit(solution)/shard_map/ppermute | solution.py:20
  2.6 41.5 %collective-permute-start = (f32[3,1,8,128]{3,2,1,0:T(8,128)S(1)}, f32[3,1,8,128]{3,2,1,0:T(8,128)S(1)}, u32[]{:S(2)}, u32[]{:S(2)}) collective-permute-start(f32[3,1,8,128]{3,2,1,0:T(8,128)S(1)} %get-tuple-element.113), channel_id=1, source_target_pairs={{0,64},{64,128},{128,192},{192,256},{256,320},{320,384},{384,448},... | collective-permute-start | bytes 36872 | tf_op jit(solution)/shard_map/ppermute | solution.py:18
  6.9 42.9 %collective-permute-start.6 = (f32[4,1,8,128]{3,2,1,0:T(8,128)S(1)}, f32[4,1,8,128]{3,2,1,0:T(8,128)S(1)}, u32[]{:S(2)}, u32[]{:S(2)}) collective-permute-start(f32[4,1,8,128]{3,2,1,0:T(8,128)S(1)} %get-tuple-element.100), channel_id=1, source_target_pairs={{0,64},{64,128},{128,192},{192,256},{256,320},{320,384},{384,448},... | collective-permute-start | bytes 49160 | tf_op jit(solution)/shard_map/ppermute | solution.py:18
  38.1 337.0 %collective-permute-start.44 = (f32[3,4,1,32]{3,2,1,0:T(1,128)S(1)}, f32[3,4,1,32]{3,2,1,0:T(1,128)S(1)}, u32[]{:S(2)}, u32[]{:S(2)}) collective-permute-start(f32[3,4,1,32]{3,2,1,0:T(1,128)S(1)} %get-tuple-element.175), channel_id=1, source_target_pairs={{0,8},{8,16},{16,24},{24,32},{32,40},{40,48},{48,56},{1,9},{9,17},... | collective-permute-start | bytes 4616 | tf_op jit(solution)/shard_map/ppermute | solution.py:18
  44.2 330.9 %collective-permute-start.45 = (f32[3,4,1,32]{3,2,1,0:T(1,128)S(1)}, f32[3,4,1,32]{3,2,1,0:T(1,128)S(1)}, u32[]{:S(2)}, u32[]{:S(2)}) collective-permute-start(f32[3,4,1,32]{3,2,1,0:T(1,128)S(1)} %get-tuple-element.176), channel_id=1, source_target_pairs={{8,0},{16,8},{24,16},{32,24},{40,32},{48,40},{56,48},{9,1},{17,9},... | collective-permute-start | bytes 4616 | tf_op jit(solution)/shard_map/ppermute | solution.py:20
  46.2 141.9 %collective-permute-start.26 = (f32[3,6,1,64]{3,2,1,0:T(1,128)S(1)}, f32[3,6,1,64]{3,2,1,0:T(1,128)S(1)}, u32[]{:S(2)}, u32[]{:S(2)}) collective-permute-start(f32[3,6,1,64]{3,2,1,0:T(1,128)S(1)} %get-tuple-element.149), channel_id=1, source_target_pairs={{0,8},{8,16},{16,24},{24,32},{32,40},{40,48},{48,56},{1,9},{9,17},... | collective-permute-start | bytes 13832 | tf_op jit(solution)/shard_map/ppermute | solution.py:18
  56.6 60.8 %collective-permute-start.4 = (f32[3,10,10,1]{3,0,2,1:T(4,128)S(1)}, f32[3,10,10,1]{3,0,2,1:T(4,128)S(1)}, u32[]{:S(2)}, u32[]{:S(2)}) collective-permute-start(f32[3,10,10,1]{3,0,2,1:T(4,128)S(1)} %get-tuple-element.86), channel_id=1, source_target_pairs={{0,1},{1,2},{2,3},{3,4},{4,5},{5,6},{6,7},{8,9},{9,10},{10,11},{11... | collective-permute-start | bytes 3608 | tf_op jit(solution)/shard_map/ppermute | solution.py:18
  82.5 59.6 %collective-permute-start.5 = (f32[3,10,10,1]{3,0,2,1:T(4,128)S(1)}, f32[3,10,10,1]{3,0,2,1:T(4,128)S(1)}, u32[]{:S(2)}, u32[]{:S(2)}) collective-permute-start(f32[3,10,10,1]{3,0,2,1:T(4,128)S(1)} %get-tuple-element.87), channel_id=1, source_target_pairs={{1,0},{2,1},{3,2},{4,3},{5,4},{6,5},{7,6},{9,8},{10,9},{11,10},{12... | collective-permute-start | bytes 3608 | tf_op jit(solution)/shard_map/ppermute | solution.py:20
  117.4 28.3 %collective-permute-start.8 = (f32[4,10,1,128]{3,0,2,1:T(4,128)S(1)}, f32[4,10,1,128]{3,0,2,1:T(4,128)S(1)}, u32[]{:S(2)}, u32[]{:S(2)}) collective-permute-start(f32[4,10,1,128]{3,0,2,1:T(4,128)S(1)} %copy.576), channel_id=1, source_target_pairs={{0,8},{8,16},{16,24},{24,32},{32,40},{40,48},{48,56},{1,9},{9,17},... | collective-permute-start | bytes 61448 | tf_op jit(solution)/shard_map/ppermute | solution.py:18
  151.8 33.0 %collective-permute-start.11 = (f32[4,10,10,1]{3,0,2,1:T(4,128)S(1)}, f32[4,10,10,1]{3,0,2,1:T(4,128)S(1)}, u32[]{:S(2)}, u32[]{:S(2)}) collective-permute-start(f32[4,10,10,1]{3,0,2,1:T(4,128)S(1)} %get-tuple-element.89), channel_id=1, source_target_pairs={{1,0},{2,1},{3,2},{4,3},{5,4},{6,5},{7,6},{9,8},{10,9},{11,10},{12... | collective-permute-start | bytes 4808 | tf_op jit(solution)/shard_map/ppermute | solution.py:20
  160.2 31.2 %collective-permute-start.27 = (f32[3,6,1,64]{3,2,1,0:T(1,128)S(1)}, f32[3,6,1,64]{3,2,1,0:T(1,128)S(1)}, u32[]{:S(2)}, u32[]{:S(2)}) collective-permute-start(f32[3,6,1,64]{3,2,1,0:T(1,128)S(1)} %get-tuple-element.150), channel_id=1, source_target_pairs={{8,0},{16,8},{24,16},{32,24},{40,32},{48,40},{56,48},{9,1},{17,9},... | collective-permute-start | bytes 13832 | tf_op jit(solution)/shard_map/ppermute | solution.py:20
  199.1 32.9 %collective-permute-start.28 = (f32[3,6,6,1]{3,2,1,0:T(8,128)S(1)}, f32[3,6,6,1]{3,2,1,0:T(8,128)S(1)}, u32[]{:S(2)}, u32[]{:S(2)}) collective-permute-start(f32[3,6,6,1]{3,2,1,0:T(8,128)S(1)} %get-tuple-element.139), channel_id=1, source_target_pairs={{0,1},{1,2},{2,3},{3,4},{4,5},{5,6},{6,7},{8,9},{9,10},{10,11},{11... | collective-permute-start | bytes 1304 | tf_op jit(solution)/shard_map/ppermute | solution.py:18
  201.1 32.9 %collective-permute-start.29 = (f32[3,6,6,1]{3,2,1,0:T(8,128)S(1)}, f32[3,6,6,1]{3,2,1,0:T(8,128)S(1)}, u32[]{:S(2)}, u32[]{:S(2)}) collective-permute-start(f32[3,6,6,1]{3,2,1,0:T(8,128)S(1)} %get-tuple-element.140), channel_id=1, source_target_pairs={{1,0},{2,1},{3,2},{4,3},{5,4},{6,5},{7,6},{9,8},{10,9},{11,10},{12... | collective-permute-start | bytes 1304 | tf_op jit(solution)/shard_map/ppermute | solution.py:20
  209.7 47.1 %collective-permute-start.16 = (f32[3,10,10,1]{3,0,2,1:T(4,128)S(1)}, f32[3,10,10,1]{3,0,2,1:T(4,128)S(1)}, u32[]{:S(2)}, u32[]{:S(2)}) collective-permute-start(f32[3,10,10,1]{3,0,2,1:T(4,128)S(1)} %get-tuple-element.84), channel_id=1, source_target_pairs={{0,1},{1,2},{2,3},{3,4},{4,5},{5,6},{6,7},{8,9},{9,10},{10,11},{11... | collective-permute-start | bytes 3608 | tf_op jit(solution)/shard_map/ppermute | solution.py:18
  232.1 49.4 %collective-permute-start.17 = (f32[3,10,10,1]{3,0,2,1:T(4,128)S(1)}, f32[3,10,10,1]{3,0,2,1:T(4,128)S(1)}, u32[]{:S(2)}, u32[]{:S(2)}) collective-permute-start(f32[3,10,10,1]{3,0,2,1:T(4,128)S(1)} %get-tuple-element.85), channel_id=1, source_target_pairs={{1,0},{2,1},{3,2},{4,3},{5,4},{6,5},{7,6},{9,8},{10,9},{11,10},{12... | collective-permute-start | bytes 3608 | tf_op jit(solution)/shard_map/ppermute | solution.py:20
  307.4 45.0 %collective-permute-start.23 = (f32[4,10,10,1]{3,0,2,1:T(4,128)S(1)}, f32[4,10,10,1]{3,0,2,1:T(4,128)S(1)}, u32[]{:S(2)}, u32[]{:S(2)}) collective-permute-start(f32[4,10,10,1]{3,0,2,1:T(4,128)S(1)} %get-tuple-element.83), channel_id=1, source_target_pairs={{1,0},{2,1},{3,2},{4,3},{5,4},{6,5},{7,6},{9,8},{10,9},{11,10},{12... | collective-permute-start | bytes 4808 | tf_op jit(solution)/shard_map/ppermute | solution.py:20
  383.4 29.7 %collective-permute-start.46 = (f32[3,4,4,1]{3,2,1,0:T(4,128)S(1)}, f32[3,4,4,1]{3,2,1,0:T(4,128)S(1)}, u32[]{:S(2)}, u32[]{:S(2)}) collective-permute-start(f32[3,4,4,1]{3,2,1,0:T(4,128)S(1)} %get-tuple-element.167), channel_id=1, source_target_pairs={{0,1},{1,2},{2,3},{3,4},{4,5},{5,6},{6,7},{8,9},{9,10},{10,11},{11... | collective-permute-start | bytes 584 | tf_op jit(solution)/shard_map/ppermute | solution.py:18
  385.3 27.8 %collective-permute-start.47 = (f32[3,4,4,1]{3,2,1,0:T(4,128)S(1)}, f32[3,4,4,1]{3,2,1,0:T(4,128)S(1)}, u32[]{:S(2)}, u32[]{:S(2)}) collective-permute-start(f32[3,4,4,1]{3,2,1,0:T(4,128)S(1)} %get-tuple-element.168), channel_id=1, source_target_pairs={{1,0},{2,1},{3,2},{4,3},{5,4},{6,5},{7,6},{9,8},{10,9},{11,10},{12... | collective-permute-start | bytes 584 | tf_op jit(solution)/shard_map/ppermute | solution.py:20
  457.8 27.3 %collective-permute-start.41 = (f32[4,6,6,1]{3,0,2,1:T(4,128)S(1)}, f32[4,6,6,1]{3,0,2,1:T(4,128)S(1)}, u32[]{:S(2)}, u32[]{:S(2)}) collective-permute-start(f32[4,6,6,1]{3,0,2,1:T(4,128)S(1)} %get-tuple-element.130), channel_id=1, source_target_pairs={{1,0},{2,1},{3,2},{4,3},{5,4},{6,5},{7,6},{9,8},{10,9},{11,10},{12... | collective-permute-start | bytes 1736 | tf_op jit(solution)/shard_map/ppermute | solution.py:20
  548.9 26.8 %collective-permute-start.59 = (f32[4,6,6,1]{3,0,2,1:T(4,128)S(1)}, f32[4,6,6,1]{3,0,2,1:T(4,128)S(1)}, u32[]{:S(2)}, u32[]{:S(2)}) collective-permute-start(f32[4,6,6,1]{3,0,2,1:T(4,128)S(1)} %get-tuple-element.124), channel_id=1, source_target_pairs={{1,0},{2,1},{3,2},{4,3},{5,4},{6,5},{7,6},{9,8},{10,9},{11,10},{12... | collective-permute-start | bytes 1736 | tf_op jit(solution)/shard_map/ppermute | solution.py:20
  641.1 36.4 %collective-permute-start.70 = (f32[4,10,10,1]{3,0,2,1:T(4,128)S(1)}, f32[4,10,10,1]{3,0,2,1:T(4,128)S(1)}, u32[]{:S(2)}, u32[]{:S(2)}) collective-permute-start(f32[4,10,10,1]{3,0,2,1:T(4,128)S(1)} %get-tuple-element.80), channel_id=1, source_target_pairs={{0,1},{1,2},{2,3},{3,4},{4,5},{5,6},{6,7},{8,9},{9,10},{10,11},{11... | collective-permute-start | bytes 4808 | tf_op jit(solution)/shard_map/ppermute | solution.py:18
  643.5 58.9 %collective-permute-start.71 = (f32[4,10,10,1]{3,0,2,1:T(4,128)S(1)}, f32[4,10,10,1]{3,0,2,1:T(4,128)S(1)}, u32[]{:S(2)}, u32[]{:S(2)}) collective-permute-start(f32[4,10,10,1]{3,0,2,1:T(4,128)S(1)} %get-tuple-element.81), channel_id=1, source_target_pairs={{1,0},{2,1},{3,2},{4,3},{5,4},{6,5},{7,6},{9,8},{10,9},{11,10},{12... | collective-permute-start | bytes 4808 | tf_op jit(solution)/shard_map/ppermute | solution.py:20
  719.0 33.4 %collective-permute-start.76 = (f32[3,10,10,1]{3,0,2,1:T(4,128)S(1)}, f32[3,10,10,1]{3,0,2,1:T(4,128)S(1)}, u32[]{:S(2)}, u32[]{:S(2)}) collective-permute-start(f32[3,10,10,1]{3,0,2,1:T(4,128)S(1)} %get-tuple-element.78), channel_id=1, source_target_pairs={{0,1},{1,2},{2,3},{3,4},{4,5},{5,6},{6,7},{8,9},{9,10},{10,11},{11... | collective-permute-start | bytes 3608 | tf_op jit(solution)/shard_map/ppermute | solution.py:18
  721.0 56.1 %collective-permute-start.77 = (f32[3,10,10,1]{3,0,2,1:T(4,128)S(1)}, f32[3,10,10,1]{3,0,2,1:T(4,128)S(1)}, u32[]{:S(2)}, u32[]{:S(2)}) collective-permute-start(f32[3,10,10,1]{3,0,2,1:T(4,128)S(1)} %get-tuple-element.79), channel_id=1, source_target_pairs={{1,0},{2,1},{3,2},{4,3},{5,4},{6,5},{7,6},{9,8},{10,9},{11,10},{12... | collective-permute-start | bytes 3608 | tf_op jit(solution)/shard_map/ppermute | solution.py:20
  (92 other events, 4481.0 us)
where the time goes:
time: 782 us; the launch traced here: 779 us
  waiting for transfers between devices  439 us (56%)
  starting transfers between devices  288 us (37%)
  local copies, waits for them, and re-layouts  31.1 us (4%)
  other arithmetic  17.3 us (2%)
    ppermute x39, waiting for transfers between devices, extended(): lax.ppermute(head, axis, [((i + 1) % count, i) for i in range(ends)])  301 us
    ppermute x39, starting transfers between devices, extended(): lax.ppermute(tail, axis, [(i, (i + 1) % count) for i in range(ends)])  189 us
    ppermute x39, waiting for transfers between devices, extended(): lax.ppermute(tail, axis, [(i, (i + 1) % count) for i in range(ends)])  138 us
    ppermute x39, starting transfers between devices, extended(): lax.ppermute(head, axis, [((i + 1) % count, i) for i in range(ends)])  99.8 us
  transfers between devices with their start and end apart: 78, of which 37 were waited for; matrix products, arithmetic and copies ran while one was open for 5% of the time, Pallas kernels for 0%

commit v1 on v0

v1 whole, which is shorter than its diff:
```python
import functools

import jax
import jax.numpy as jnp
from jax import lax
from jax.experimental import pallas as pl
from jax.experimental.pallas import tpu as pltpu
from jax.sharding import PartitionSpec as P

F32 = jnp.float32
BX, BY, BZ = 8, 8, 128
XL, XH = 2, 4
NL = BX + XL + XH
ROWS, LANES = 16, 256
ML = 14
VMEM = pl.BlockSpec(memory_space=pltpu.VMEM)
SMEM = pl.BlockSpec(memory_space=pltpu.SMEM)
PARAMS = pltpu.CompilerParams(vmem_limit_bytes=20 * 1024 * 1024)


def call(kernel, outs, scratch, *args):
    specs = [SMEM if a.dtype == jnp.int32 else VMEM for a in args]
    return pl.pallas_call(
        kernel,
        out_shape=[jax.ShapeDtypeStruct(s, F32) for s in outs],
        in_specs=specs,
        out_specs=[VMEM] * len(outs),
        scratch_shapes=[pltpu.VMEM(s, F32) for s in scratch],
        compiler_params=PARAMS,
    )(*args)


def iota(shape, dim):
    return lax.broadcasted_iota(jnp.int32, shape, dim)


def up(a, dim, by=1):
    return pltpu.roll(a, a.shape[dim] - by, dim)


def down(a, dim, by=1):
    return pltpu.roll(a, by, dim)


def lane_roll(a, by):
    by = by % a.shape[1]
    return pltpu.roll(a, by, 1) if by else a


def pack_z(place, iterate, forcing, viscosity, own, first, second):
    lane = iota((BY, BZ), 1) // 16
    odd = jnp.full((BY, BZ), place[3], jnp.int32) == 1
    at = 0
    for source, count in ((iterate, 4), (forcing, 4), (viscosity, 3)):
        for f in range(count):
            low = jnp.zeros((BY, BZ), F32)
            high = jnp.zeros((BY, BZ), F32)
            for x in range(BX):
                a = source[f, x]
                own[at, x] = a
                mine = lane == x
                low = jnp.where(mine, lane_roll(a, 16 * x - 112), low)
                high = jnp.where(mine, lane_roll(a, 16 * x), high)
            first[at] = jnp.where(odd, low, high)
            second[at] = jnp.where(odd, high, low)
            at += 1


def strips(place, first, second, f):
    odd = jnp.full((BY, BZ), place[3], jnp.int32) == 1
    a, b = first[f], second[f]
    return jnp.where(odd, b, a), jnp.where(odd, a, b)


def pack_x(place, own, first, second, to_up, to_down):
    lane = iota((BY, BZ), 1)

    def field(f, carry):
        low, high = strips(place, first, second, f)
        for i in range(XL):
            to_up[f, i] = own[f, BX - XL + i]
        to_up[f, XL] = jnp.where(lane >= 96, low, lane_roll(high, -32))
        for i in range(XH):
            to_down[f, i] = own[f, i]
        to_down[f, XH] = jnp.where(lane < 64, low, lane_roll(high, 64))
        return carry

    lax.fori_loop(0, 11, field, 0)


def pack_y(place, own, first, second, from_low, from_high, to_up, to_down):
    def field(f, carry):
        low, high = strips(place, first, second, f)
        tiles = [from_low[f, i] for i in range(XL)]
        tiles += [own[f, i] for i in range(BX)]
        tiles += [from_high[f, i] for i in range(XH)]
        tiles += [low, high, from_low[f, XL], from_high[f, XH]]
        for i, tile in enumerate(tiles):
            to_up[f, i] = tile[BY - XL :, :]
            to_down[f, i] = tile[:XH, :]
        return carry

    lax.fori_loop(0, 11, field, 0)


def inside_yz(place, rows, lanes, ny, nz, end_y, low_y, end_z, low_z, by, bz):
    y = iota((rows, lanes), 0)
    z = iota((rows, lanes), 1)
    held = ((y < end_y) | (y >= rows - low_y)) & ((z < end_z) | (z >= lanes - low_z))
    y = jnp.where(y < end_y, y, y - rows) + place[1] * by
    z = jnp.where(z < end_z, z, z - lanes) + place[2] * bz
    good = held & (y >= 0) & (y < ny) & (z >= 0) & (z < nz)
    return jnp.where(good, 1, 0)


def inside(yz, x, nx):
    ok = jnp.where((x >= 0) & (x < nx), 1, 0)
    return (yz * ok) != 0


def neighbours(low, mid, high, by=1):
    return (low, high, down(mid, 0, by), up(mid, 0, by), down(mid, 1, by), up(mid, 1, by))


def total(values):
    out = values[0]
    for v in values[1:]:
        out = out + v
    return out


def couple(e, es, vs):
    return e * total(vs) + total([a * b for a, b in zip(es, vs)])


def fine_mask_args(place, sizes):
    return inside_yz(place, ROWS, LANES, sizes[1], sizes[2], BY + XH, XL, BZ + 16, 16, BY, BZ)


def compact_matrix():
    a = iota((LANES, BZ), 0) // 2
    return jnp.where(a == iota((LANES, BZ), 1), 0.125, 0.0).astype(jnp.bfloat16)


def spread_matrix():
    a = iota((BZ, LANES), 1) // 2
    return jnp.where(a == iota((BZ, LANES), 0), 1.0, 0.0).astype(jnp.bfloat16)


def exact_dot(a, matrix):
    high = a.astype(jnp.bfloat16)
    rest = a - high.astype(F32)
    mid = rest.astype(jnp.bfloat16)
    low = (rest - mid.astype(F32)).astype(jnp.bfloat16)
    dot = functools.partial(jnp.dot, preferred_element_type=F32)
    return dot(high, matrix) + (dot(mid, matrix) + dot(low, matrix))


def fine_level(sizes, place, own, first, second, from_low, from_high, y_low, y_high, full, to_down, to_up, it, packed, rsum, tsum):
    lane = iota((ROWS, BZ), 1)

    def assemble(dest, at, f):
        low, high = strips(place, first, second, f)
        packed[0, 0:BY] = low
        packed[1, 0:BY] = high
        packed[2, 0:BY] = from_low[f, XL]
        packed[3, 0:BY] = from_high[f, XH]
        blank = jnp.zeros((2, BZ), F32)
        for i in range(4):
            packed[i, BY : BY + XH] = y_high[f, NL + i]
            packed[i, 12:14] = blank
            packed[i, 14:16] = y_low[f, NL + i]
        tiles = [packed[i] for i in range(4)]
        for l in range(NL):
            x = l - XL
            if x < 0:
                body = from_low[f, l]
                a, b = lane_roll(tiles[2], 16 - 16 * l), lane_roll(tiles[2], -(64 + 16 * l))
            elif x < BX:
                body = own[f, x]
                a, b = lane_roll(tiles[0], 112 - 16 * x), lane_roll(tiles[1], -16 * x)
            else:
                body = from_high[f, x - BX]
                a, b = lane_roll(tiles[3], 112 - 16 * (x - BX)), lane_roll(tiles[3], -(64 + 16 * (x - BX)))
            dest[at, l, 0:BY, 0:BZ] = body
            dest[at, l, BY : BY + XH, 0:BZ] = y_high[f, l]
            dest[at, l, 12:14, 0:BZ] = blank
            dest[at, l, 14:16, 0:BZ] = y_low[f, l]
            dest[at, l, :, BZ:] = jnp.where(lane >= 112, a, jnp.where(lane < 16, b, 0.0))

    def first_fields(f, carry):
        assemble(it, f, f)
        return carry

    def other_fields(f, carry):
        assemble(full, f, f)
        return carry

    lax.fori_loop(0, 4, first_fields, 0)
    lax.fori_loop(4, 11, other_fields, 0)

    yz = fine_mask_args(place, sizes)
    for i in range(4):
        full[i, 0] = jnp.zeros((ROWS, LANES), F32)
        full[i, NL - 1] = jnp.zeros((ROWS, LANES), F32)
    full[3, NL - 2] = jnp.zeros((ROWS, LANES), F32)

    def velocities(l, carry):
        good = inside(yz, place[0] * BX + l - XL, sizes[0])
        p = it[3, l]
        for c in range(3):
            u, e = it[c, l], full[8 + c, l]
            us = neighbours(it[c, l - 1], u, it[c, l + 1])
            es = neighbours(full[8 + c, l - 1], e, full[8 + c, l + 1])
            diag = 6.0 * e + total(es)
            before = it[3, l - 1] if c == 0 else down(p, c - 1)
            push = 1.2 * (full[4 + c, l] - (p - before)) + 0.6 * couple(e, es, us)
            full[c, l] = jnp.where(good, 0.4 * u + push / diag, 0.0)
        return carry

    lax.fori_loop(1, NL - 1, velocities, 0)

    def outflow(l):
        v, w = full[1, l], full[2, l]
        return (full[0, l + 1] - full[0, l]) + (up(v, 0) - v) + (up(w, 1) - w)

    def pressures(l, carry):
        good = inside(yz, place[0] * BX + l - XL, sizes[0])
        ev, ew = full[9, l], full[10, l]
        cell = (full[8, l] + full[8, l + 1]) + (ev + up(ev, 0)) + (ew + up(ew, 1))
        full[3, l] = jnp.where(good, it[3, l] - (0.5 / 6.0) * cell * (full[7, l] + outflow(l)), 0.0)
        return carry

    lax.fori_loop(1, NL - 2, pressures, 0)

    def layer_residual(c, l):
        u, e = full[c, l], full[8 + c, l]
        us = neighbours(full[c, l - 1], u, full[c, l + 1])
        es = neighbours(full[8 + c, l - 1], e, full[8 + c, l + 1])
        diag = 6.0 * e + total(es)
        p = full[3, l]
        before = full[3, l - 1] if c == 0 else down(p, c - 1)
        return full[4 + c, l] - (p - before) - 0.5 * (diag * u - couple(e, es, us))

    def residuals(m, carry):
        l = XL + 2 * m
        for c in range(3):
            rsum[c, m] = layer_residual(c, l) + layer_residual(c, l + 1)
        rsum[3, m] = (full[7, l] + outflow(l)) + (full[7, l + 1] + outflow(l + 1))
        return carry

    lax.fori_loop(0, 5, residuals, 0)
    for i in range(4):
        rsum[i, 5] = jnp.zeros((ROWS, LANES), F32)
    for c in range(3):
        for m in range(6):
            rsum[4 + c, m] = full[8 + c, XL + 2 * m] + full[8 + c, XL + 2 * m + 1]

    matrix = compact_matrix()
    for f in range(7):
        tsum[6 * f : 6 * f + 6] = exact_dot(rsum[f].reshape(6 * ROWS, LANES), matrix).reshape(6, ROWS, BZ)
    for f in range(7):
        for m in range(6):
            i = 6 * f + m
            a = tsum[i, pl.ds(0, 8, stride=2), :] + tsum[i, pl.ds(1, 8, stride=2), :]
            to_down[f, m] = a
            if m < 4:
                to_up[f, m] = a


def pack_y_mid(own, from_low, from_high, to_down, to_up):
    def field(f, carry):
        tiles = [from_low[f, i] for i in range(4)]
        tiles += [own[f, i] for i in range(4)]
        tiles += [from_high[f, i] for i in range(6)]
        for i, tile in enumerate(tiles):
            to_down[f, i] = tile
            to_up[f, i] = tile[:4, :]
        return carry

    lax.fori_loop(0, 7, field, 0)


def coarse_levels(sizes, place, fine, own, y_low, y_high, out, mid, um, dm, f2, e2, low, sm, twice, spread, g, un):
    blank = jnp.zeros((2, BZ), F32)

    def assemble(f, carry):
        for l in range(ML):
            mid[f, l, 0:4] = own[f, l, 0:4]
            mid[f, l, 4:10] = y_high[f, l, 0:6]
            mid[f, l, 10:12] = blank
            mid[f, l, 12:16] = y_low[f, l]
        return carry

    lax.fori_loop(0, 7, assemble, 0)

    shape = (ROWS, BZ)
    yz = inside_yz(place, ROWS, BZ, sizes[1] // 2, sizes[2] // 2, 10, 4, BZ // 2 + 8, 8, BY // 2, BZ // 2)
    row_even = iota(shape, 0) % 2 == 0
    lane_even = iota(shape, 1) % 2 == 0

    def mid_inside(l):
        return inside(yz, place[0] * (BX // 2) + l - 4, sizes[0] // 2)

    def first_velocities(l, carry):
        good = mid_inside(l)
        for c in range(3):
            e = mid[4 + c, l]
            diag = 6.0 * e + total(neighbours(mid[4 + c, l - 1], e, mid[4 + c, l + 1]))
            dm[c, l] = diag
            um[c, l] = jnp.where(good, 4.8 * mid[c, l] / diag, 0.0)
        return carry

    lax.fori_loop(1, 13, first_velocities, 0)

    def outflow(v, l):
        b, w = v[1, l], v[2, l]
        return (v[0, l + 1] - v[0, l]) + (up(b, 0) - b) + (up(w, 1) - w)

    def mid_cell(l):
        ev, ew = mid[5, l], mid[6, l]
        return (mid[4, l] + mid[4, l + 1]) + (ev + up(ev, 0)) + (ew + up(ew, 1))

    def first_pressures(l, carry):
        q = mid[3, l] + 0.5 * outflow(um, l)
        um[3, l] = jnp.where(mid_inside(l), (-0.5 / 6.0) * mid_cell(l) * q, 0.0)
        return carry

    lax.fori_loop(1, 12, first_pressures, 0)

    def expand(a):
        a = a + up(a, 0)
        a = jnp.where(row_even, a, down(a, 0))
        a = a + up(a, 1)
        return 0.125 * jnp.where(lane_even, a, down(a, 1))

    def layer_residual(c, l):
        u, e = um[c, l], mid[4 + c, l]
        us = neighbours(um[c, l - 1], u, um[c, l + 1])
        es = neighbours(mid[4 + c, l - 1], e, mid[4 + c, l + 1])
        p = um[3, l]
        before = um[3, l - 1] if c == 0 else down(p, c - 1)
        return mid[c, l] - 0.5 * (p - before) - 0.125 * (dm[c, l] * u - couple(e, es, us))

    def residuals(k, carry):
        l = 2 + 2 * k
        for c in range(3):
            f2[c, k] = expand(layer_residual(c, l) + layer_residual(c, l + 1))
        f2[3, k] = expand((mid[3, l] + 0.5 * outflow(um, l)) + (mid[3, l + 1] + 0.5 * outflow(um, l + 1)))
        return carry

    lax.fori_loop(0, 5, residuals, 0)

    def low_viscosity(k, carry):
        for c in range(3):
            e2[c, k] = expand(mid[4 + c, 2 * k] + mid[4 + c, 2 * k + 1])
        return carry

    lax.fori_loop(0, 7, low_viscosity, 0)

    def low_inside(k):
        return inside(yz, place[0] * (BX // 4) + k - 1, sizes[0] // 4)

    def low_velocities(k, carry):
        good = low_inside(k)
        for c in range(3):
            e = e2[c, k + 1]
            diag = 6.0 * e + total(neighbours(e2[c, k], e, e2[c, k + 2], 2))
            low[c, k] = jnp.where(good, 19.2 * f2[c, k] / diag, 0.0)
        return carry

    lax.fori_loop(0, 5, low_velocities, 0)

    def low_pressures(k, carry):
        v, w, ev, ew = low[1, k], low[2, k], e2[1, k + 1], e2[2, k + 1]
        flow = (low[0, k + 1] - low[0, k]) + (up(v, 0, 2) - v) + (up(w, 1, 2) - w)
        cell = (e2[0, k + 1] + e2[0, k + 2]) + (ev + up(ev, 0, 2)) + (ew + up(ew, 1, 2))
        low[3, k] = jnp.where(low_inside(k), (-0.5 / 6.0) * cell * (f2[3, k] + 0.25 * flow), 0.0)
        return carry

    lax.fori_loop(0, 4, low_pressures, 0)

    def corrected(k, carry):
        for i in range(3):
            um[i, 2 * k + 2] = um[i, 2 * k + 2] + low[i, k]
            um[i, 2 * k + 3] = um[i, 2 * k + 3] + low[i, k]
        return carry

    lax.fori_loop(0, 5, corrected, 0)
    for k in range(4):
        um[3, 2 * k + 2] = um[3, 2 * k + 2] + low[3, k]
        um[3, 2 * k + 3] = um[3, 2 * k + 3] + low[3, k]

    def second_velocities(l, carry):
        good = mid_inside(l)
        p = um[3, l]
        for c in range(3):
            u, e = um[c, l], mid[4 + c, l]
            us = neighbours(um[c, l - 1], u, um[c, l + 1])
            es = neighbours(mid[4 + c, l - 1], e, mid[4 + c, l + 1])
            before = um[3, l - 1] if c == 0 else down(p, c - 1)
            push = 4.8 * (mid[c, l] - 0.5 * (p - before)) + 0.6 * couple(e, es, us)
            sm[c, l] = jnp.where(good, 0.4 * u + push / dm[c, l], 0.0)
        return carry

    lax.fori_loop(3, 10, second_velocities, 0)

    def second_pressures(l, carry):
        q = mid[3, l] + 0.5 * outflow(sm, l)
        sm[3, l] = jnp.where(mid_inside(l), um[3, l] - (0.5 / 6.0) * mid_cell(l) * q, 0.0)
        return carry

    lax.fori_loop(3, 9, second_pressures, 0)

    last_row = iota((8, BZ), 0) == 7
    for i in range(4):
        for m in range(6):
            a = sm[i, 3 + m]
            a = jnp.where(last_row, a[8:16], a[0:8])
            twice[6 * i + m, pl.ds(0, 8, stride=2), :] = a
            twice[6 * i + m, pl.ds(1, 8, stride=2), :] = a
    matrix = spread_matrix()
    for i in range(4):
        wide = exact_dot(twice[6 * i : 6 * i + 6].reshape(6 * ROWS, BZ), matrix)
        spread[i] = wide.reshape(6, ROWS, LANES)

    for i in range(4):
        for j in range(11):
            g[i, j] = fine[i, j + 1] + spread[i, (j + 1) // 2]

    fyz = fine_mask_args(place, sizes)

    def last_velocities(x, carry):
        good = inside(fyz, place[0] * BX + x, sizes[0])
        p = g[3, x + 1]
        for c in range(3):
            u, e = g[c, x + 1], fine[8 + c, x + XL]
            us = neighbours(g[c, x], u, g[c, x + 2])
            es = neighbours(fine[8 + c, x + XL - 1], e, fine[8 + c, x + XL + 1])
            diag = 6.0 * e + total(es)
            before = g[3, x] if c == 0 else down(p, c - 1)
            push = 1.2 * (fine[4 + c, x + XL] - (p - before)) + 0.6 * couple(e, es, us)
            un[c, x] = jnp.where(good, 0.4 * u + push / diag, 0.0)
        return carry

    lax.fori_loop(0, 9, last_velocities, 0)

    def last_pressures(x, carry):
        l = x + XL
        ev, ew = fine[9, l], fine[10, l]
        cell = (fine[8, l] + fine[8, l + 1]) + (ev + up(ev, 0)) + (ew + up(ew, 1))
        p = g[3, x + 1] - (0.5 / 6.0) * cell * (fine[7, l] + outflow(un, x))
        out[3, x] = p[0:BY, 0:BZ]
        for c in range(3):
            out[c, x] = un[c, x, 0:BY, 0:BZ]
        return carry

    lax.fori_loop(0, BX, last_pressures, 0)


def per_device(sizes, iterate, forcing, viscosity):
    nx, ny, nz = (lax.axis_size(a) for a in ("gx", "gy", "gz"))
    at = [lax.axis_index(a) for a in ("gx", "gy", "gz")]
    place = jnp.stack(at + [at[2] % 2]).astype(jnp.int32)

    def swap(a, axis, count, start):
        pairs = []
        for i in range(start, count - 1, 2):
            pairs += [(i, i + 1), (i + 1, i)]
        return lax.ppermute(a, axis, pairs)

    def to_next(a, axis, count):
        return lax.ppermute(a, axis, [(i, i + 1) for i in range(count - 1)])

    def to_previous(a, axis, count):
        return lax.ppermute(a, axis, [(i + 1, i) for i in range(count - 1)])

    tile = (BY, BZ)
    own, first, second = call(
        pack_z, [(11, BX) + tile, (11,) + tile, (11,) + tile], [], place, iterate, forcing, viscosity
    )
    first = swap(first, "gz", nz, 1)
    second = swap(second, "gz", nz, 0)

    upward, downward = call(pack_x, [(11, XL + 1) + tile, (11, XH + 1) + tile], [], place, own, first, second)
    x_low = to_next(upward, "gx", nx)
    x_high = to_previous(downward, "gx", nx)

    upward, downward = call(
        pack_y, [(11, NL + 4, XL, BZ), (11, NL + 4, XH, BZ)], [], place, own, first, second, x_low, x_high
    )
    y_low = to_next(upward, "gy", ny)
    y_high = to_previous(downward, "gy", ny)

    fine, downward, upward = call(
        functools.partial(fine_level, sizes),
        [(11, NL, ROWS, LANES), (7, 6) + tile, (7, 4) + tile],
        [(4, NL, ROWS, LANES), (4, ROWS, BZ), (7, 6, ROWS, LANES), (42, ROWS, BZ)],
        place, own, first, second, x_low, x_high, y_low, y_high,
    )
    x_low = to_next(upward, "gx", nx)
    x_high = to_previous(downward, "gx", nx)

    downward, upward = call(pack_y_mid, [(7, ML) + tile, (7, ML, 4, BZ)], [], downward, x_low, x_high)
    y_low = to_next(upward, "gy", ny)
    y_high = to_previous(downward, "gy", ny)

    wide = (ROWS, BZ)
    (updated,) = call(
        functools.partial(coarse_levels, sizes),
        [(4, BX) + tile],
        [
            (7, ML) + wide, (4, ML) + wide, (3, ML) + wide, (4, 5) + wide, (3, 7) + wide, (4, 5) + wide,
            (4, ML) + wide, (24,) + wide, (4, 6, ROWS, LANES), (4, 11, ROWS, LANES), (3, 9, ROWS, LANES),
        ],
        place, fine, downward, y_low, y_high,
    )
    return updated


def solution(mesh):
    spec = P(None, "gx", "gy", "gz")
    sizes = (mesh.shape["gx"] * BX, mesh.shape["gy"] * BY, mesh.shape["gz"] * BZ)
    return jax.shard_map(
        functools.partial(per_device, sizes), mesh=mesh, in_specs=(spec,) * 3, out_specs=spec, check_vma=False
    )
```

time: 782 us -> 95.2 us (0.12)
  the two profiles are of different devices: /device:TPU:39 before, /device:TPU:641 now
where the time goes in v1:
time: 95.2 us; the launch traced here: 94.8 us
  starting transfers between devices  38 us (40%)
  waiting for transfers between devices  34.7 us (36%)
  Pallas kernels  19.2 us (20%)
  local copies, waits for them, and re-layouts  2.7 us (3%)
    pallas_call x6, Pallas kernels, call(): pl.pallas_call(kernel, out_shape=[jax.ShapeDtypeStruct(s, F32) for s in o...  19.2 us
    ppermute x2, waiting for transfers between devices, swap(): return lax.ppermute(a, axis, pairs)  19.1 us
    ppermute x4, starting transfers between devices, to_previous(): return lax.ppermute(a, axis, [(i + 1, i) for i in range(count - 1)])  18.3 us
    ppermute x4, waiting for transfers between devices, to_next(): return lax.ppermute(a, axis, [(i, i + 1) for i in range(count - 1)])  13.7 us
    ppermute x4, starting transfers between devices, to_next(): return lax.ppermute(a, axis, [(i, i + 1) for i in range(count - 1)])  13.4 us
    ppermute x2, starting transfers between devices, swap(): return lax.ppermute(a, axis, pairs)  6.24 us
    unnamed x6, local copies, waits for them, and re-layouts  2.7 us
    ppermute x4, waiting for transfers between devices, to_previous(): return lax.ppermute(a, axis, [(i + 1, i) for i in range(count - 1)])  1.96 us
  transfers between devices with their start and end apart: 10, of which 7 were waited for; matrix products, arithmetic and copies ran while one was open for 0% of the time, Pallas kernels for 0%

profile of v1, /device:TPU:641, one launch (start us, length us, event | category | flops | bytes accessed | tf_op | source)
XLA Modules:
  0.0 94.8 jit_solution(12986406638743254331)
XLA Ops:
  0.1 0.9 copy-done
  1.0 0.9 copy-done.1
  1.9 0.9 copy-done.2
  2.8 0.8 shard_map.37
  3.6 1.9 %collective-permute-start = (f32[11,8,128]{2,1,0:T(8,128)S(1)}, f32[11,8,128]{2,1,0:T(8,128)S(1)}, u32[]{:S(2)}, u32[]{:S(2)}) collective-permute-start(f32[11,8,128]{2,1,0:T(8,128)S(1)} %get-tuple-element.18), channel_id=1, source_target_pairs={{1,2},{2,1},{3,4},{4,3},{5,6},{6,5},{9,10},{10,9},{11,12},{12,11},... | collective-permute-start | bytes 135176 | tf_op jit(solution)/shard_map/ppermute | solution.py:470
  5.5 4.3 %collective-permute-start.1 = (f32[11,8,128]{2,1,0:T(8,128)S(1)}, f32[11,8,128]{2,1,0:T(8,128)S(1)}, u32[]{:S(2)}, u32[]{:S(2)}) collective-permute-start(f32[11,8,128]{2,1,0:T(8,128)S(1)} %get-tuple-element.19), channel_id=1, source_target_pairs={{0,1},{1,0},{2,3},{3,2},{4,5},{5,4},{6,7},{7,6},{8,9},{9,8},{10,11... | collective-permute-start | bytes 135176 | tf_op jit(solution)/shard_map/ppermute | solution.py:470
  9.8 19.1 %collective-permute-done.first = f32[11,8,128]{2,1,0:T(8,128)S(1)} collective-permute-done((f32[11,8,128]{2,1,0:T(8,128)S(1)}, f32[11,8,128]{2,1,0:T(8,128)S(1)}, u32[]{:S(2)}, u32[]{:S(2)}) %collective-permute-start) | collective-permute-done | bytes 45088 | tf_op jit(solution)/shard_map/ppermute | solution.py:470
  28.9 1.4 %shard_map.38 = (f32[11,3,8,128]{3,2,1,0:T(8,128)S(1)}, f32[11,5,8,128]{3,2,1,0:T(8,128)S(1)}) custom-call(s32[4]{0:T(128)S(1)} %pad_add_fusion.place, f32[11,8,8,128]{3,2,1,0:T(8,128)S(1)} %get-tuple-element.17.own, f32[11,8,128]{2,1,0:T(8,128)S(1)} %collective-permute-done.first, f32[11,8,128]{2,1,0:T(8,128)S(1)} %collective-permute-done.1.second), custom_call_target="tpu_custom_call" | custom-call | tf_op jit(solution)/shard_map/pallas_call | solution.py:23
  30.2 3.8 %collective-permute-start.3 = (f32[11,5,8,128]{3,2,1,0:T(8,128)S(1)}, f32[11,5,8,128]{3,2,1,0:T(8,128)S(1)}, u32[]{:S(2)}, u32[]{:S(2)}) collective-permute-start(f32[11,5,8,128]{3,2,1,0:T(8,128)S(1)} %get-tuple-element.21), channel_id=1, source_target_pairs={{64,0},{128,64},{192,128},{256,192},{320,256},{384,320},{448,384},... | collective-permute-start | bytes 675848 | tf_op jit(solution)/shard_map/ppermute | solution.py:476
  34.0 1.9 %collective-permute-start.2 = (f32[11,3,8,128]{3,2,1,0:T(8,128)S(1)}, f32[11,3,8,128]{3,2,1,0:T(8,128)S(1)}, u32[]{:S(2)}, u32[]{:S(2)}) collective-permute-start(f32[11,3,8,128]{3,2,1,0:T(8,128)S(1)} %get-tuple-element.20), channel_id=1, source_target_pairs={{0,64},{64,128},{128,192},{192,256},{256,320},{320,384},{384,448},... | collective-permute-start | bytes 405512 | tf_op jit(solution)/shard_map/ppermute | solution.py:473
  35.9 5.0 %collective-permute-done.2.from_low = f32[11,3,8,128]{3,2,1,0:T(8,128)S(1)} collective-permute-done((f32[11,3,8,128]{3,2,1,0:T(8,128)S(1)}, f32[11,3,8,128]{3,2,1,0:T(8,128)S(1)}, u32[]{:S(2)}, u32[]{:S(2)}) %collective-permute-start.2) | collective-permute-done | bytes 135200 | tf_op jit(solution)/shard_map/ppermute | solution.py:473
  41.7 10.7 %collective-permute-start.5 = (f32[11,18,4,128]{3,2,1,0:T(4,128)S(1)}, f32[11,18,4,128]{3,2,1,0:T(4,128)S(1)}, u32[]{:S(2)}, u32[]{:S(2)}) collective-permute-start(f32[11,18,4,128]{3,2,1,0:T(4,128)S(1)} %get-tuple-element.23), channel_id=1, source_target_pairs={{8,0},{16,8},{24,16},{32,24},{40,32},{48,40},{56,48},{9,1},{17,9},... | collective-permute-start | bytes 1216520 | tf_op jit(solution)/shard_map/ppermute | solution.py:476
  52.4 3.1 %collective-permute-start.4 = (f32[11,18,2,128]{3,2,1,0:T(2,128)S(1)}, f32[11,18,2,128]{3,2,1,0:T(2,128)S(1)}, u32[]{:S(2)}, u32[]{:S(2)}) collective-permute-start(f32[11,18,2,128]{3,2,1,0:T(2,128)S(1)} %get-tuple-element.22), channel_id=1, source_target_pairs={{0,8},{8,16},{16,24},{24,32},{32,40},{40,48},{48,56},{1,9},{9,17},... | collective-permute-start | bytes 608264 | tf_op jit(solution)/shard_map/ppermute | solution.py:473
  55.5 2.7 %collective-permute-done.4.y_low = f32[11,18,2,128]{3,2,1,0:T(2,128)S(1)} collective-permute-done((f32[11,18,2,128]{3,2,1,0:T(2,128)S(1)}, f32[11,18,2,128]{3,2,1,0:T(2,128)S(1)}, u32[]{:S(2)}, u32[]{:S(2)}) %collective-permute-start.4) | collective-permute-done | bytes 202784 | tf_op jit(solution)/shard_map/ppermute | solution.py:473
  58.2 1.0 %collective-permute-done.5.y_high = f32[11,18,4,128]{3,2,1,0:T(4,128)S(1)} collective-permute-done((f32[11,18,4,128]{3,2,1,0:T(4,128)S(1)}, f32[11,18,4,128]{3,2,1,0:T(4,128)S(1)}, u32[]{:S(2)}, u32[]{:S(2)}) %collective-permute-start.5) | collective-permute-done | bytes 405536 | tf_op jit(solution)/shard_map/ppermute | solution.py:476
  59.1 6.3 %shard_map.40 = (f32[11,14,16,256]{3,2,1,0:T(8,128)S(1)}, f32[7,6,8,128]{3,2,1,0:T(8,128)S(1)}, f32[7,4,8,128]{3,2,1,0:T(8,128)S(1)}) custom-call(s32[4]{0:T(128)S(1)} %pad_add_fusion.place, f32[11,8,8,128]{3,2,1,0:T(8,128)S(1)} %get-tuple-element.17.own, f32[11,8,128]{2,1,0:T(8,128)S(1)} %collective-permute-done.first, ...), custom_call_target="tpu_custom_call" | custom-call | tf_op jit(solution)/shard_map/pallas_call | solution.py:23
  65.5 1.9 %collective-permute-start.7 = (f32[7,6,8,128]{3,2,1,0:T(8,128)S(1)}, f32[7,6,8,128]{3,2,1,0:T(8,128)S(1)}, u32[]{:S(2)}, u32[]{:S(2)}) collective-permute-start(f32[7,6,8,128]{3,2,1,0:T(8,128)S(1)} %get-tuple-element.25.own), channel_id=1, source_target_pairs={{64,0},{128,64},{192,128},{256,192},{320,256},{384,320},{448,384},... | collective-permute-start | bytes 516104 | tf_op jit(solution)/shard_map/ppermute | solution.py:476
  67.4 3.4 %collective-permute-start.6 = (f32[7,4,8,128]{3,2,1,0:T(8,128)S(1)}, f32[7,4,8,128]{3,2,1,0:T(8,128)S(1)}, u32[]{:S(2)}, u32[]{:S(2)}) collective-permute-start(f32[7,4,8,128]{3,2,1,0:T(8,128)S(1)} %get-tuple-element.26), channel_id=1, source_target_pairs={{0,64},{64,128},{128,192},{192,256},{256,320},{320,384},{384,448},... | collective-permute-start | bytes 344072 | tf_op jit(solution)/shard_map/ppermute | solution.py:473
  70.8 3.4 %collective-permute-done.6.from_low = f32[7,4,8,128]{3,2,1,0:T(8,128)S(1)} collective-permute-done((f32[7,4,8,128]{3,2,1,0:T(8,128)S(1)}, f32[7,4,8,128]{3,2,1,0:T(8,128)S(1)}, u32[]{:S(2)}, u32[]{:S(2)}) %collective-permute-start.6) | collective-permute-done | bytes 114720 | tf_op jit(solution)/shard_map/ppermute | solution.py:473
  74.2 1.9 %collective-permute-start.9 = (f32[7,14,8,128]{3,2,1,0:T(8,128)S(1)}, f32[7,14,8,128]{3,2,1,0:T(8,128)S(1)}, u32[]{:S(2)}, u32[]{:S(2)}) collective-permute-start(f32[7,14,8,128]{3,2,1,0:T(8,128)S(1)} %get-tuple-element.27.own), channel_id=1, source_target_pairs={{8,0},{16,8},{24,16},{32,24},{40,32},{48,40},{56,48},{9,1},{17,9},... | collective-permute-start | bytes 1204232 | tf_op jit(solution)/shard_map/ppermute | solution.py:476
  76.1 5.0 %collective-permute-start.8 = (f32[7,14,4,128]{3,2,1,0:T(4,128)S(1)}, f32[7,14,4,128]{3,2,1,0:T(4,128)S(1)}, u32[]{:S(2)}, u32[]{:S(2)}) collective-permute-start(f32[7,14,4,128]{3,2,1,0:T(4,128)S(1)} %get-tuple-element.28), channel_id=1, source_target_pairs={{0,8},{8,16},{16,24},{24,32},{32,40},{40,48},{48,56},{1,9},{9,17},... | collective-permute-start | bytes 602120 | tf_op jit(solution)/shard_map/ppermute | solution.py:473
  81.2 2.6 %collective-permute-done.8.y_low = f32[7,14,4,128]{3,2,1,0:T(4,128)S(1)} collective-permute-done((f32[7,14,4,128]{3,2,1,0:T(4,128)S(1)}, f32[7,14,4,128]{3,2,1,0:T(4,128)S(1)}, u32[]{:S(2)}, u32[]{:S(2)}) %collective-permute-start.8) | collective-permute-done | bytes 200736 | tf_op jit(solution)/shard_map/ppermute | solution.py:473
  83.8 1.0 %collective-permute-done.9.y_high = f32[7,14,8,128]{3,2,1,0:T(8,128)S(1)} collective-permute-done((f32[7,14,8,128]{3,2,1,0:T(8,128)S(1)}, f32[7,14,8,128]{3,2,1,0:T(8,128)S(1)}, u32[]{:S(2)}, u32[]{:S(2)}) %collective-permute-start.9) | collective-permute-done | bytes 401440 | tf_op jit(solution)/shard_map/ppermute | solution.py:476
  84.8 10.0 %shard_map.42 = f32[4,8,8,128]{3,2,1,0:T(8,128)} custom-call(s32[4]{0:T(128)S(1)} %pad_add_fusion.place, f32[11,14,16,256]{3,2,1,0:T(8,128)S(1)} %get-tuple-element.24.fine, f32[7,14,8,128]{3,2,1,0:T(8,128)S(1)} %get-tuple-element.27.own, f32[7,14,4,128]{3,2,1,0:T(4,128)S(1)} %collective-permute-done.8.y_low, f32[7,14,8,128]{3,2,1,0:T(8,128)S(1)} %collective-permute-done.9.y_high), custom_call_target="tpu_custom_call" | custom-call | tf_op jit(solution)/shard_map/pallas_call | solution.py:23
  (9 shorter events, 0.8 us)
Async XLA Ops:
  0.1 0.9 copy-start
  1.0 0.9 copy-start.1
  1.9 0.9 copy-start.2
  3.6 25.3 %collective-permute-start = (f32[11,8,128]{2,1,0:T(8,128)S(1)}, f32[11,8,128]{2,1,0:T(8,128)S(1)}, u32[]{:S(2)}, u32[]{:S(2)}) collective-permute-start(f32[11,8,128]{2,1,0:T(8,128)S(1)} %get-tuple-element.18), channel_id=1, source_target_pairs={{1,2},{2,1},{3,4},{4,3},{5,6},{6,5},{9,10},{10,9},{11,12},{12,11},... | collective-permute-start | bytes 135176 | tf_op jit(solution)/shard_map/ppermute | solution.py:470
  5.5 23.4 %collective-permute-start.1 = (f32[11,8,128]{2,1,0:T(8,128)S(1)}, f32[11,8,128]{2,1,0:T(8,128)S(1)}, u32[]{:S(2)}, u32[]{:S(2)}) collective-permute-start(f32[11,8,128]{2,1,0:T(8,128)S(1)} %get-tuple-element.19), channel_id=1, source_target_pairs={{0,1},{1,0},{2,3},{3,2},{4,5},{5,4},{6,7},{7,6},{8,9},{9,8},{10,11... | collective-permute-start | bytes 135176 | tf_op jit(solution)/shard_map/ppermute | solution.py:470
  30.2 10.8 %collective-permute-start.3 = (f32[11,5,8,128]{3,2,1,0:T(8,128)S(1)}, f32[11,5,8,128]{3,2,1,0:T(8,128)S(1)}, u32[]{:S(2)}, u32[]{:S(2)}) collective-permute-start(f32[11,5,8,128]{3,2,1,0:T(8,128)S(1)} %get-tuple-element.21), channel_id=1, source_target_pairs={{64,0},{128,64},{192,128},{256,192},{320,256},{384,320},{448,384},... | collective-permute-start | bytes 675848 | tf_op jit(solution)/shard_map/ppermute | solution.py:476
  34.0 7.0 %collective-permute-start.2 = (f32[11,3,8,128]{3,2,1,0:T(8,128)S(1)}, f32[11,3,8,128]{3,2,1,0:T(8,128)S(1)}, u32[]{:S(2)}, u32[]{:S(2)}) collective-permute-start(f32[11,3,8,128]{3,2,1,0:T(8,128)S(1)} %get-tuple-element.20), channel_id=1, source_target_pairs={{0,64},{64,128},{128,192},{192,256},{256,320},{320,384},{384,448},... | collective-permute-start | bytes 405512 | tf_op jit(solution)/shard_map/ppermute | solution.py:473
  41.7 17.5 %collective-permute-start.5 = (f32[11,18,4,128]{3,2,1,0:T(4,128)S(1)}, f32[11,18,4,128]{3,2,1,0:T(4,128)S(1)}, u32[]{:S(2)}, u32[]{:S(2)}) collective-permute-start(f32[11,18,4,128]{3,2,1,0:T(4,128)S(1)} %get-tuple-element.23), channel_id=1, source_target_pairs={{8,0},{16,8},{24,16},{32,24},{40,32},{48,40},{56,48},{9,1},{17,9},... | collective-permute-start | bytes 1216520 | tf_op jit(solution)/shard_map/ppermute | solution.py:476
  52.4 5.8 %collective-permute-start.4 = (f32[11,18,2,128]{3,2,1,0:T(2,128)S(1)}, f32[11,18,2,128]{3,2,1,0:T(2,128)S(1)}, u32[]{:S(2)}, u32[]{:S(2)}) collective-permute-start(f32[11,18,2,128]{3,2,1,0:T(2,128)S(1)} %get-tuple-element.22), channel_id=1, source_target_pairs={{0,8},{8,16},{16,24},{24,32},{32,40},{40,48},{48,56},{1,9},{9,17},... | collective-permute-start | bytes 608264 | tf_op jit(solution)/shard_map/ppermute | solution.py:473
  65.5 8.7 %collective-permute-start.7 = (f32[7,6,8,128]{3,2,1,0:T(8,128)S(1)}, f32[7,6,8,128]{3,2,1,0:T(8,128)S(1)}, u32[]{:S(2)}, u32[]{:S(2)}) collective-permute-start(f32[7,6,8,128]{3,2,1,0:T(8,128)S(1)} %get-tuple-element.25.own), channel_id=1, source_target_pairs={{64,0},{128,64},{192,128},{256,192},{320,256},{384,320},{448,384},... | collective-permute-start | bytes 516104 | tf_op jit(solution)/shard_map/ppermute | solution.py:476
  67.4 6.7 %collective-permute-start.6 = (f32[7,4,8,128]{3,2,1,0:T(8,128)S(1)}, f32[7,4,8,128]{3,2,1,0:T(8,128)S(1)}, u32[]{:S(2)}, u32[]{:S(2)}) collective-permute-start(f32[7,4,8,128]{3,2,1,0:T(8,128)S(1)} %get-tuple-element.26), channel_id=1, source_target_pairs={{0,64},{64,128},{128,192},{192,256},{256,320},{320,384},{384,448},... | collective-permute-start | bytes 344072 | tf_op jit(solution)/shard_map/ppermute | solution.py:473
  74.2 10.6 %collective-permute-start.9 = (f32[7,14,8,128]{3,2,1,0:T(8,128)S(1)}, f32[7,14,8,128]{3,2,1,0:T(8,128)S(1)}, u32[]{:S(2)}, u32[]{:S(2)}) collective-permute-start(f32[7,14,8,128]{3,2,1,0:T(8,128)S(1)} %get-tuple-element.27.own), channel_id=1, source_target_pairs={{8,0},{16,8},{24,16},{32,24},{40,32},{48,40},{56,48},{9,1},{17,9},... | collective-permute-start | bytes 1204232 | tf_op jit(solution)/shard_map/ppermute | solution.py:476
  76.1 7.7 %collective-permute-start.8 = (f32[7,14,4,128]{3,2,1,0:T(4,128)S(1)}, f32[7,14,4,128]{3,2,1,0:T(4,128)S(1)}, u32[]{:S(2)}, u32[]{:S(2)}) collective-permute-start(f32[7,14,4,128]{3,2,1,0:T(4,128)S(1)} %get-tuple-element.28), channel_id=1, source_target_pairs={{0,8},{8,16},{16,24},{24,32},{32,40},{40,48},{48,56},{1,9},{9,17},... | collective-permute-start | bytes 602120 | tf_op jit(solution)/shard_map/ppermute | solution.py:473

commit v2 on v1

--- a/solution.py
+++ b/solution.py
@@ -15,19 +15,25 @@
 ML = 14
 VMEM = pl.BlockSpec(memory_space=pltpu.VMEM)
 SMEM = pl.BlockSpec(memory_space=pltpu.SMEM)
+HBM = pl.BlockSpec(memory_space=pltpu.HBM)
+UNROLL = True
 PARAMS = pltpu.CompilerParams(vmem_limit_bytes=20 * 1024 * 1024)
 
 
-def call(kernel, outs, scratch, *args):
-    specs = [SMEM if a.dtype == jnp.int32 else VMEM for a in args]
+def call(kernel, outs, scratch, *args, space=VMEM):
+    specs = [SMEM if a.dtype == jnp.int32 else space for a in args]
     return pl.pallas_call(
         kernel,
         out_shape=[jax.ShapeDtypeStruct(s, F32) for s in outs],
         in_specs=specs,
         out_specs=[VMEM] * len(outs),
-        scratch_shapes=[pltpu.VMEM(s, F32) for s in scratch],
+        scratch_shapes=[pltpu.VMEM(s, F32) if isinstance(s, tuple) else s for s in scratch],
         compiler_params=PARAMS,
     )(*args)
+
+
+def loop(start, stop, body, carry):
+    return lax.fori_loop(start, stop, body, carry, unroll=UNROLL)
 
 
 def iota(shape, dim):
@@ -47,23 +53,28 @@
     return pltpu.roll(a, by, 1) if by else a
 
 
-def pack_z(place, iterate, forcing, viscosity, own, first, second):
+def pack_z(place, iterate, forcing, viscosity, own, first, second, sems):
+    parts = ((iterate, 0, 4), (forcing, 4, 4), (viscosity, 8, 3))
+    copies = [
+        pltpu.make_async_copy(source, own.at[at : at + count], sems.at[i])
+        for i, (source, at, count) in enumerate(parts)
+    ]
+    for copy in copies:
+        copy.start()
     lane = iota((BY, BZ), 1) // 16
     odd = jnp.full((BY, BZ), place[3], jnp.int32) == 1
-    at = 0
-    for source, count in ((iterate, 4), (forcing, 4), (viscosity, 3)):
-        for f in range(count):
+    for copy, (_, at, count) in zip(copies, parts):
+        copy.wait()
+        for f in range(at, at + count):
             low = jnp.zeros((BY, BZ), F32)
             high = jnp.zeros((BY, BZ), F32)
             for x in range(BX):
-                a = source[f, x]
-                own[at, x] = a
+                a = own[f, x]
                 mine = lane == x
                 low = jnp.where(mine, lane_roll(a, 16 * x - 112), low)
                 high = jnp.where(mine, lane_roll(a, 16 * x), high)
-            first[at] = jnp.where(odd, low, high)
-            second[at] = jnp.where(odd, high, low)
-            at += 1
+            first[f] = jnp.where(odd, low, high)
+            second[f] = jnp.where(odd, high, low)
 
 
 def strips(place, first, second, f):
@@ -74,8 +85,7 @@
 
 def pack_x(place, own, first, second, to_up, to_down):
     lane = iota((BY, BZ), 1)
-
-    def field(f, carry):
+    for f in range(11):
         low, high = strips(place, first, second, f)
         for i in range(XL):
             to_up[f, i] = own[f, BX - XL + i]
@@ -83,9 +93,6 @@
         for i in range(XH):
             to_down[f, i] = own[f, i]
         to_down[f, XH] = jnp.where(lane < 64, low, lane_roll(high, 64))
-        return carry
-
-    lax.fori_loop(0, 11, field, 0)
 
 
 def pack_y(place, own, first, second, from_low, from_high, to_up, to_down):
@@ -100,7 +107,7 @@
             to_down[f, i] = tile[:XH, :]
         return carry
 
-    lax.fori_loop(0, 11, field, 0)
+    loop(0, 11, field, 0)
 
 
 def inside_yz(place, rows, lanes, ny, nz, end_y, low_y, end_z, low_z, by, bz):
@@ -156,48 +163,56 @@
     return dot(high, matrix) + (dot(mid, matrix) + dot(low, matrix))
 
 
-def fine_level(sizes, place, own, first, second, from_low, from_high, y_low, y_high, full, to_down, to_up, it, packed, rsum, tsum):
-    lane = iota((ROWS, BZ), 1)
-
-    def assemble(dest, at, f):
+def kept(place, sizes):
+    low = jnp.where(place[1] > 0, 1.0, 0.0).astype(F32)
+    high = jnp.where(place[1] < sizes[1] // BY - 1, 1.0, 0.0).astype(F32)
+    return low, high
+
+
+def side_lanes(l, tiles):
+    lane = iota((BY, BZ), 1)
+    x = l - XL
+    if x < 0:
+        a, b = lane_roll(tiles[2], 16 - 16 * l), lane_roll(tiles[2], -(64 + 16 * l))
+    elif x < BX:
+        a, b = lane_roll(tiles[0], 112 - 16 * x), lane_roll(tiles[1], -16 * x)
+    else:
+        a, b = lane_roll(tiles[3], 112 - 16 * (x - BX)), lane_roll(tiles[3], -(64 + 16 * (x - BX)))
+    return jnp.where(lane >= 112, a, jnp.where(lane < 16, b, 0.0))
+
+
+def assemble_own(place, own, first, second, from_low, from_high, half):
+    for f in range(11):
         low, high = strips(place, first, second, f)
-        packed[0, 0:BY] = low
-        packed[1, 0:BY] = high
-        packed[2, 0:BY] = from_low[f, XL]
-        packed[3, 0:BY] = from_high[f, XH]
-        blank = jnp.zeros((2, BZ), F32)
-        for i in range(4):
-            packed[i, BY : BY + XH] = y_high[f, NL + i]
-            packed[i, 12:14] = blank
-            packed[i, 14:16] = y_low[f, NL + i]
-        tiles = [packed[i] for i in range(4)]
+        tiles = [low, high, from_low[f, XL], from_high[f, XH]]
         for l in range(NL):
             x = l - XL
             if x < 0:
                 body = from_low[f, l]
-                a, b = lane_roll(tiles[2], 16 - 16 * l), lane_roll(tiles[2], -(64 + 16 * l))
             elif x < BX:
                 body = own[f, x]
-                a, b = lane_roll(tiles[0], 112 - 16 * x), lane_roll(tiles[1], -16 * x)
             else:
                 body = from_high[f, x - BX]
-                a, b = lane_roll(tiles[3], 112 - 16 * (x - BX)), lane_roll(tiles[3], -(64 + 16 * (x - BX)))
-            dest[at, l, 0:BY, 0:BZ] = body
-            dest[at, l, BY : BY + XH, 0:BZ] = y_high[f, l]
-            dest[at, l, 12:14, 0:BZ] = blank
-            dest[at, l, 14:16, 0:BZ] = y_low[f, l]
-            dest[at, l, :, BZ:] = jnp.where(lane >= 112, a, jnp.where(lane < 16, b, 0.0))
-
-    def first_fields(f, carry):
-        assemble(it, f, f)
-        return carry
-
-    def other_fields(f, carry):
-        assemble(full, f, f)
-        return carry
-
-    lax.fori_loop(0, 4, first_fields, 0)
-    lax.fori_loop(4, 11, other_fields, 0)
+            half[f, l, :, 0:BZ] = body
+            half[f, l, :, BZ:] = side_lanes(l, tiles)
+
+
+def fine_level(sizes, place, half, y_low, y_high, grid, full, to_down, to_up, rows, rsum, tsum):
+    keep_low, keep_high = kept(place, sizes)
+
+    def halo_rows(f, carry):
+        for i in range(NL + 4):
+            rows[i, 0:XH] = y_high[f, i] * keep_high
+            rows[i, XH:6] = jnp.zeros((2, BZ), F32)
+            rows[i, 6:8] = y_low[f, i] * keep_low
+        tiles = [rows[NL + i] for i in range(4)]
+        for l in range(NL):
+            grid[f, l, 0:BY] = half[f, l]
+            grid[f, l, BY:, 0:BZ] = rows[l]
+            grid[f, l, BY:, BZ:] = side_lanes(l, tiles)
+        return carry
+
+    loop(0, 11, halo_rows, 0)
 
     yz = fine_mask_args(place, sizes)
     for i in range(4):
@@ -207,18 +222,18 @@
 
     def velocities(l, carry):
         good = inside(yz, place[0] * BX + l - XL, sizes[0])
-        p = it[3, l]
-        for c in range(3):
-            u, e = it[c, l], full[8 + c, l]
-            us = neighbours(it[c, l - 1], u, it[c, l + 1])
-            es = neighbours(full[8 + c, l - 1], e, full[8 + c, l + 1])
+        p = grid[3, l]
+        for c in range(3):
+            u, e = grid[c, l], grid[8 + c, l]
+            us = neighbours(grid[c, l - 1], u, grid[c, l + 1])
+            es = neighbours(grid[8 + c, l - 1], e, grid[8 + c, l + 1])
             diag = 6.0 * e + total(es)
-            before = it[3, l - 1] if c == 0 else down(p, c - 1)
-            push = 1.2 * (full[4 + c, l] - (p - before)) + 0.6 * couple(e, es, us)
+            before = grid[3, l - 1] if c == 0 else down(p, c - 1)
+            push = 1.2 * (grid[4 + c, l] - (p - before)) + 0.6 * couple(e, es, us)
             full[c, l] = jnp.where(good, 0.4 * u + push / diag, 0.0)
         return carry
 
-    lax.fori_loop(1, NL - 1, velocities, 0)
+    loop(1, NL - 1, velocities, 0)
 
     def outflow(l):
         v, w = full[1, l], full[2, l]
@@ -226,35 +241,35 @@
 
     def pressures(l, carry):
         good = inside(yz, place[0] * BX + l - XL, sizes[0])
-        ev, ew = full[9, l], full[10, l]
-        cell = (full[8, l] + full[8, l + 1]) + (ev + up(ev, 0)) + (ew + up(ew, 1))
-        full[3, l] = jnp.where(good, it[3, l] - (0.5 / 6.0) * cell * (full[7, l] + outflow(l)), 0.0)
-        return carry
-
-    lax.fori_loop(1, NL - 2, pressures, 0)
+        ev, ew = grid[9, l], grid[10, l]
+        cell = (grid[8, l] + grid[8, l + 1]) + (ev + up(ev, 0)) + (ew + up(ew, 1))
+        full[3, l] = jnp.where(good, grid[3, l] - (0.5 / 6.0) * cell * (grid[7, l] + outflow(l)), 0.0)
+        return carry
+
+    loop(1, NL - 2, pressures, 0)
 
     def layer_residual(c, l):
-        u, e = full[c, l], full[8 + c, l]
+        u, e = full[c, l], grid[8 + c, l]
         us = neighbours(full[c, l - 1], u, full[c, l + 1])
-        es = neighbours(full[8 + c, l - 1], e, full[8 + c, l + 1])
+        es = neighbours(grid[8 + c, l - 1], e, grid[8 + c, l + 1])
         diag = 6.0 * e + total(es)
         p = full[3, l]
         before = full[3, l - 1] if c == 0 else down(p, c - 1)
-        return full[4 + c, l] - (p - before) - 0.5 * (diag * u - couple(e, es, us))
+        return grid[4 + c, l] - (p - before) - 0.5 * (diag * u - couple(e, es, us))
 
     def residuals(m, carry):
         l = XL + 2 * m
         for c in range(3):
             rsum[c, m] = layer_residual(c, l) + layer_residual(c, l + 1)
-        rsum[3, m] = (full[7, l] + outflow(l)) + (full[7, l + 1] + outflow(l + 1))
-        return carry
-
-    lax.fori_loop(0, 5, residuals, 0)
+        rsum[3, m] = (grid[7, l] + outflow(l)) + (grid[7, l + 1] + outflow(l + 1))
+        return carry
+
+    loop(0, 5, residuals, 0)
     for i in range(4):
         rsum[i, 5] = jnp.zeros((ROWS, LANES), F32)
     for c in range(3):
         for m in range(6):
-            rsum[4 + c, m] = full[8 + c, XL + 2 * m] + full[8 + c, XL + 2 * m + 1]
+            rsum[4 + c, m] = grid[8 + c, XL + 2 * m] + grid[8 + c, XL + 2 * m + 1]
 
     matrix = compact_matrix()
     for f in range(7):
@@ -269,30 +284,29 @@
 
 
 def pack_y_mid(own, from_low, from_high, to_down, to_up):
-    def field(f, carry):
+    for f in range(7):
         tiles = [from_low[f, i] for i in range(4)]
         tiles += [own[f, i] for i in range(4)]
         tiles += [from_high[f, i] for i in range(6)]
         for i, tile in enumerate(tiles):
-            to_down[f, i] = tile
+            to_down[f, 6 * i : 6 * i + 6] = tile[:6, :]
             to_up[f, i] = tile[:4, :]
-        return carry
-
-    lax.fori_loop(0, 7, field, 0)
-
-
-def coarse_levels(sizes, place, fine, own, y_low, y_high, out, mid, um, dm, f2, e2, low, sm, twice, spread, g, un):
+        to_down[f, 6 * ML :] = jnp.zeros((4, BZ), F32)
+
+
+def coarse_levels(sizes, place, grid, fine, own, y_low, y_high, out, mid, um, dm, f2, e2, low, sm, twice, spread, g, un):
     blank = jnp.zeros((2, BZ), F32)
+    keep_low, keep_high = kept(place, sizes)
 
     def assemble(f, carry):
         for l in range(ML):
-            mid[f, l, 0:4] = own[f, l, 0:4]
-            mid[f, l, 4:10] = y_high[f, l, 0:6]
+            mid[f, l, 0:4] = own[f, l]
+            mid[f, l, 4:10] = y_high[f, 6 * l : 6 * l + 6] * keep_high
             mid[f, l, 10:12] = blank
-            mid[f, l, 12:16] = y_low[f, l]
-        return carry
-
-    lax.fori_loop(0, 7, assemble, 0)
+            mid[f, l, 12:16] = y_low[f, l] * keep_low
+        return carry
+
+    loop(0, 7, assemble, 0)
 
     shape = (ROWS, BZ)
     yz = inside_yz(place, ROWS, BZ, sizes[1] // 2, sizes[2] // 2, 10, 4, BZ // 2 + 8, 8, BY // 2, BZ // 2)
@@ -311,7 +325,7 @@
             um[c, l] = jnp.where(good, 4.8 * mid[c, l] / diag, 0.0)
         return carry
 
-    lax.fori_loop(1, 13, first_velocities, 0)
+    loop(1, 13, first_velocities, 0)
 
     def outflow(v, l):
         b, w = v[1, l], v[2, l]
@@ -326,7 +340,7 @@
         um[3, l] = jnp.where(mid_inside(l), (-0.5 / 6.0) * mid_cell(l) * q, 0.0)
         return carry
 
-    lax.fori_loop(1, 12, first_pressures, 0)
+    loop(1, 12, first_pressures, 0)
 
     def expand(a):
         a = a + up(a, 0)
@@ -349,14 +363,14 @@
         f2[3, k] = expand((mid[3, l] + 0.5 * outflow(um, l)) + (mid[3, l + 1] + 0.5 * outflow(um, l + 1)))
         return carry
 
-    lax.fori_loop(0, 5, residuals, 0)
+    loop(0, 5, residuals, 0)
 
     def low_viscosity(k, carry):
         for c in range(3):
             e2[c, k] = expand(mid[4 + c, 2 * k] + mid[4 + c, 2 * k + 1])
         return carry
 
-    lax.fori_loop(0, 7, low_viscosity, 0)
+    loop(0, 7, low_viscosity, 0)
 
     def low_inside(k):
         return inside(yz, place[0] * (BX // 4) + k - 1, sizes[0] // 4)
@@ -369,7 +383,7 @@
             low[c, k] = jnp.where(good, 19.2 * f2[c, k] / diag, 0.0)
         return carry
 
-    lax.fori_loop(0, 5, low_velocities, 0)
+    loop(0, 5, low_velocities, 0)
 
     def low_pressures(k, carry):
         v, w, ev, ew = low[1, k], low[2, k], e2[1, k + 1], e2[2, k + 1]
@@ -378,7 +392,7 @@
         low[3, k] = jnp.where(low_inside(k), (-0.5 / 6.0) * cell * (f2[3, k] + 0.25 * flow), 0.0)
         return carry
 
-    lax.fori_loop(0, 4, low_pressures, 0)
+    loop(0, 4, low_pressures, 0)
 
     def corrected(k, carry):
         for i in range(3):
@@ -386,7 +400,7 @@
             um[i, 2 * k + 3] = um[i, 2 * k + 3] + low[i, k]
         return carry
 
-    lax.fori_loop(0, 5, corrected, 0)
+    loop(0, 5, corrected, 0)
     for k in range(4):
         um[3, 2 * k + 2] = um[3, 2 * k + 2] + low[3, k]
         um[3, 2 * k + 3] = um[3, 2 * k + 3] + low[3, k]
@@ -403,14 +417,14 @@
             sm[c, l] = jnp.where(good, 0.4 * u + push / dm[c, l], 0.0)
         return carry
 
-    lax.fori_loop(3, 10, second_velocities, 0)
+    loop(3, 10, second_velocities, 0)
 
     def second_pressures(l, carry):
         q = mid[3, l] + 0.5 * outflow(sm, l)
         sm[3, l] = jnp.where(mid_inside(l), um[3, l] - (0.5 / 6.0) * mid_cell(l) * q, 0.0)
         return carry
 
-    lax.fori_loop(3, 9, second_pressures, 0)
+    loop(3, 9, second_pressures, 0)
 
     last_row = iota((8, BZ), 0) == 7
     for i in range(4):
@@ -434,28 +448,38 @@
         good = inside(fyz, place[0] * BX + x, sizes[0])
         p = g[3, x + 1]
         for c in range(3):
-            u, e = g[c, x + 1], fine[8 + c, x + XL]
+            u, e = g[c, x + 1], grid[8 + c, x + XL]
             us = neighbours(g[c, x], u, g[c, x + 2])
-            es = neighbours(fine[8 + c, x + XL - 1], e, fine[8 + c, x + XL + 1])
+            es = neighbours(grid[8 + c, x + XL - 1], e, grid[8 + c, x + XL + 1])
             diag = 6.0 * e + total(es)
             before = g[3, x] if c == 0 else down(p, c - 1)
-            push = 1.2 * (fine[4 + c, x + XL] - (p - before)) + 0.6 * couple(e, es, us)
+            push = 1.2 * (grid[4 + c, x + XL] - (p - before)) + 0.6 * couple(e, es, us)
             un[c, x] = jnp.where(good, 0.4 * u + push / diag, 0.0)
         return carry
 
-    lax.fori_loop(0, 9, last_velocities, 0)
+    loop(0, 9, last_velocities, 0)
 
     def last_pressures(x, carry):
         l = x + XL
-        ev, ew = fine[9, l], fine[10, l]
-        cell = (fine[8, l] + fine[8, l + 1]) + (ev + up(ev, 0)) + (ew + up(ew, 1))
-        p = g[3, x + 1] - (0.5 / 6.0) * cell * (fine[7, l] + outflow(un, x))
+        ev, ew = grid[9, l], grid[10, l]
+        cell = (grid[8, l] + grid[8, l + 1]) + (ev + up(ev, 0)) + (ew + up(ew, 1))
+        p = g[3, x + 1] - (0.5 / 6.0) * cell * (grid[7, l] + outflow(un, x))
         out[3, x] = p[0:BY, 0:BZ]
         for c in range(3):
             out[c, x] = un[c, x, 0:BY, 0:BZ]
         return carry
 
-    lax.fori_loop(0, BX, last_pressures, 0)
+    loop(0, BX, last_pressures, 0)
+
+
+GRID = (11, NL, ROWS, LANES)
+FINE_OUT = [GRID, (4, NL, ROWS, LANES), (7, 6, BY, BZ), (7, 4, BY, BZ)]
+FINE_SCRATCH = [(NL + 4, BY, BZ), (7, 6, ROWS, LANES), (42, ROWS, BZ)]
+WIDE = (ROWS, BZ)
+COARSE_SCRATCH = [
+    (7, ML) + WIDE, (4, ML) + WIDE, (3, ML) + WIDE, (4, 5) + WIDE, (3, 7) + WIDE, (4, 5) + WIDE,
+    (4, ML) + WIDE, (24,) + WIDE, (4, 6, ROWS, LANES), (4, 11, ROWS, LANES), (3, 9, ROWS, LANES),
+]
 
 
 def per_device(sizes, iterate, forcing, viscosity):
@@ -469,15 +493,22 @@
             pairs += [(i, i + 1), (i + 1, i)]
         return lax.ppermute(a, axis, pairs)
 
+    def around(a, axis, count, by):
+        return lax.ppermute(a, axis, [(i, (i + by) % count) for i in range(count)])
+
     def to_next(a, axis, count):
         return lax.ppermute(a, axis, [(i, i + 1) for i in range(count - 1)])
 
     def to_previous(a, axis, count):
         return lax.ppermute(a, axis, [(i + 1, i) for i in range(count - 1)])
 
+    iterate, forcing, viscosity = (
+        pltpu.with_memory_space_constraint(a, pltpu.HBM) for a in (iterate, forcing, viscosity)
+    )
     tile = (BY, BZ)
     own, first, second = call(
-        pack_z, [(11, BX) + tile, (11,) + tile, (11,) + tile], [], place, iterate, forcing, viscosity
+        pack_z, [(11, BX) + tile, (11,) + tile, (11,) + tile], [pltpu.SemaphoreType.DMA((3,))],
+        place, iterate, forcing, viscosity, space=HBM,
     )
     first = swap(first, "gz", nz, 1)
     second = swap(second, "gz", nz, 0)
@@ -489,31 +520,23 @@
     upward, downward = call(
         pack_y, [(11, NL + 4, XL, BZ), (11, NL + 4, XH, BZ)], [], place, own, first, second, x_low, x_high
     )
-    y_low = to_next(upward, "gy", ny)
-    y_high = to_previous(downward, "gy", ny)
-
-    fine, downward, upward = call(
-        functools.partial(fine_level, sizes),
-        [(11, NL, ROWS, LANES), (7, 6) + tile, (7, 4) + tile],
-        [(4, NL, ROWS, LANES), (4, ROWS, BZ), (7, 6, ROWS, LANES), (42, ROWS, BZ)],
-        place, own, first, second, x_low, x_high, y_low, y_high,
+    y_low = around(upward, "gy", ny, 1)
+    y_high = around(downward, "gy", ny, -1)
+    (half,) = call(assemble_own, [(11, NL, BY, LANES)], [], place, own, first, second, x_low, x_high)
+
+    grid, fine, downward, upward = call(
+        functools.partial(fine_level, sizes), FINE_OUT, FINE_SCRATCH, place, half, y_low, y_high
     )
     x_low = to_next(upward, "gx", nx)
     x_high = to_previous(downward, "gx", nx)
 
-    downward, upward = call(pack_y_mid, [(7, ML) + tile, (7, ML, 4, BZ)], [], downward, x_low, x_high)
-    y_low = to_next(upward, "gy", ny)
-    y_high = to_previous(downward, "gy", ny)
-
-    wide = (ROWS, BZ)
+    downward, upward = call(pack_y_mid, [(7, 6 * ML + 4, BZ), (7, ML, 4, BZ)], [], downward, x_low, x_high)
+    y_low = around(upward, "gy", ny, 1)
+    y_high = around(downward, "gy", ny, -1)
+
     (updated,) = call(
-        functools.partial(coarse_levels, sizes),
-        [(4, BX) + tile],
-        [
-            (7, ML) + wide, (4, ML) + wide, (3, ML) + wide, (4, 5) + wide, (3, 7) + wide, (4, 5) + wide,
-            (4, ML) + wide, (24,) + wide, (4, 6, ROWS, LANES), (4, 11, ROWS, LANES), (3, 9, ROWS, LANES),
-        ],
-        place, fine, downward, y_low, y_high,
+        functools.partial(coarse_levels, sizes), [(4, BX) + tile], COARSE_SCRATCH,
+        place, grid, fine, upward, y_low, y_high,
     )
     return updated
 

time: 95.2 us -> 82.6 us (0.87)
  starting transfers between devices: 38 us -> 29 us
  Pallas kernels: 19.2 us -> 14.2 us
  waiting for transfers between devices: 34.7 us -> 38.3 us
  local copies, waits for them, and re-layouts: 2.7 us -> 0 us
    ppermute x4 -> x2, starting transfers between devices: 18.3 us -> 5.7 us  [to_previous(): return lax.ppermute(a, axis, [(i + 1, i) for i in range(count - 1)])]
    ppermute x0 -> x4, starting transfers between devices: none -> 11.8 us  [around(): return lax.ppermute(a, axis, [(i, (i + by) % count) for i in range(count)])]
    ppermute x0 -> x4, waiting for transfers between devices: none -> 9.59 us  [around(): return lax.ppermute(a, axis, [(i, (i + by) % count) for i in range(count)])]
    ppermute x4 -> x2, starting transfers between devices: 13.4 us -> 5.28 us  [to_next(): return lax.ppermute(a, axis, [(i, i + 1) for i in range(count - 1)])]
    pallas_call x6 -> x7, Pallas kernels: 19.2 us -> 14.2 us  [call(): pl.pallas_call(kernel, out_shape=[jax.ShapeDtypeStruct(s, F32) for s in o...]
    ppermute x4 -> x2, waiting for transfers between devices: 13.7 us -> 9.7 us  [to_next(): return lax.ppermute(a, axis, [(i, i + 1) for i in range(count - 1)])]
    unnamed x6 -> x0, local copies, waits for them, and re-layouts: 2.7 us -> none
    ppermute x4 -> x2, waiting for transfers between devices: 1.96 us -> 0.01 us  [to_previous(): return lax.ppermute(a, axis, [(i + 1, i) for i in range(count - 1)])]
  transfers between devices with their start and end apart: 10 -> 10, of which waited for: 7 -> 7; matrix products, arithmetic and copies ran while one was open for 0% -> 0% of each run, Pallas kernels for 0% -> 1%
where the time goes in v2:
time: 82.6 us; the launch traced here: 81.7 us
  waiting for transfers between devices  38.3 us (46%)
  starting transfers between devices  29 us (35%)
  Pallas kernels  14.2 us (17%)
    ppermute x2, waiting for transfers between devices, swap(): return lax.ppermute(a, axis, pairs)  19.1 us
    pallas_call x7, Pallas kernels, call(): pl.pallas_call(kernel, out_shape=[jax.ShapeDtypeStruct(s, F32) for s in o...  14.2 us
    ppermute x4, starting transfers between devices, around(): return lax.ppermute(a, axis, [(i, (i + by) % count) for i in range(count)])  11.8 us
    ppermute x2, waiting for transfers between devices, to_next(): return lax.ppermute(a, axis, [(i, i + 1) for i in range(count - 1)])  9.7 us
    ppermute x4, waiting for transfers between devices, around(): return lax.ppermute(a, axis, [(i, (i + by) % count) for i in range(count)])  9.59 us
    ppermute x2, starting transfers between devices, swap(): return lax.ppermute(a, axis, pairs)  6.24 us
    ppermute x2, starting transfers between devices, to_previous(): return lax.ppermute(a, axis, [(i + 1, i) for i in range(count - 1)])  5.7 us
    ppermute x2, starting transfers between devices, to_next(): return lax.ppermute(a, axis, [(i, i + 1) for i in range(count - 1)])  5.28 us
  transfers between devices with their start and end apart: 10, of which 7 were waited for; matrix products, arithmetic and copies ran while one was open for 0% of the time, Pallas kernels for 1%

profile of v2, /device:TPU:641, one launch (start us, length us, event | category | flops | bytes accessed | tf_op | source)
XLA Modules:
  0.0 81.7 jit_solution(14808042222675486663)
XLA Ops:
  0.0 0.1 pad_add_fusion.place
  0.1 1.8 %shard_map.37 = (f32[11,8,8,128]{3,2,1,0:T(8,128)S(1)}, f32[11,8,128]{2,1,0:T(8,128)S(1)}, f32[11,8,128]{2,1,0:T(8,128)S(1)}) custom-call(s32[4]{0:T(128)S(1)} %pad_add_fusion.place, f32[4,8,8,128]{3,2,1,0:T(8,128)} %iterate.1, f32[4,8,8,128]{3,2,1,0:T(8,128)} %forcing.1, f32[3,8,8,128]{3,2,1,0:T(8,128)} %viscosity.1), custom_call_target="tpu_custom_call" | custom-call | tf_op jit(solution)/shard_map/pallas_call | solution.py:25
  1.9 1.9 %collective-permute-start = (f32[11,8,128]{2,1,0:T(8,128)S(1)}, f32[11,8,128]{2,1,0:T(8,128)S(1)}, u32[]{:S(2)}, u32[]{:S(2)}) collective-permute-start(f32[11,8,128]{2,1,0:T(8,128)S(1)} %get-tuple-element.19), channel_id=1, source_target_pairs={{1,2},{2,1},{3,4},{4,3},{5,6},{6,5},{9,10},{10,9},{11,12},{12,11},... | collective-permute-start | bytes 135176 | tf_op jit(solution)/shard_map/ppermute | solution.py:494
  3.9 4.3 %collective-permute-start.1 = (f32[11,8,128]{2,1,0:T(8,128)S(1)}, f32[11,8,128]{2,1,0:T(8,128)S(1)}, u32[]{:S(2)}, u32[]{:S(2)}) collective-permute-start(f32[11,8,128]{2,1,0:T(8,128)S(1)} %get-tuple-element.20), channel_id=1, source_target_pairs={{0,1},{1,0},{2,3},{3,2},{4,5},{5,4},{6,7},{7,6},{8,9},{9,8},{10,11... | collective-permute-start | bytes 135176 | tf_op jit(solution)/shard_map/ppermute | solution.py:494
  8.2 19.1 %collective-permute-done.first = f32[11,8,128]{2,1,0:T(8,128)S(1)} collective-permute-done((f32[11,8,128]{2,1,0:T(8,128)S(1)}, f32[11,8,128]{2,1,0:T(8,128)S(1)}, u32[]{:S(2)}, u32[]{:S(2)}) %collective-permute-start) | collective-permute-done | bytes 45088 | tf_op jit(solution)/shard_map/ppermute | solution.py:494
  27.2 0.6 shard_map.38
  27.9 3.8 %collective-permute-start.3 = (f32[11,5,8,128]{3,2,1,0:T(8,128)S(1)}, f32[11,5,8,128]{3,2,1,0:T(8,128)S(1)}, u32[]{:S(2)}, u32[]{:S(2)}) collective-permute-start(f32[11,5,8,128]{3,2,1,0:T(8,128)S(1)} %get-tuple-element.22), channel_id=1, source_target_pairs={{64,0},{128,64},{192,128},{256,192},{320,256},{384,320},{448,384},... | collective-permute-start | bytes 675848 | tf_op jit(solution)/shard_map/ppermute | solution.py:503
  31.7 1.9 %collective-permute-start.2 = (f32[11,3,8,128]{3,2,1,0:T(8,128)S(1)}, f32[11,3,8,128]{3,2,1,0:T(8,128)S(1)}, u32[]{:S(2)}, u32[]{:S(2)}) collective-permute-start(f32[11,3,8,128]{3,2,1,0:T(8,128)S(1)} %get-tuple-element.21), channel_id=1, source_target_pairs={{0,64},{64,128},{128,192},{192,256},{256,320},{320,384},{384,448},... | collective-permute-start | bytes 405512 | tf_op jit(solution)/shard_map/ppermute | solution.py:500
  33.6 5.0 %collective-permute-done.2.from_low = f32[11,3,8,128]{3,2,1,0:T(8,128)S(1)} collective-permute-done((f32[11,3,8,128]{3,2,1,0:T(8,128)S(1)}, f32[11,3,8,128]{3,2,1,0:T(8,128)S(1)}, u32[]{:S(2)}, u32[]{:S(2)}) %collective-permute-start.2) | collective-permute-done | bytes 135200 | tf_op jit(solution)/shard_map/ppermute | solution.py:500
  38.6 0.7 shard_map.40
  39.3 8.8 %collective-permute-start.5 = (f32[11,18,4,128]{3,2,1,0:T(4,128)S(1)}, f32[11,18,4,128]{3,2,1,0:T(4,128)S(1)}, u32[]{:S(2)}, u32[]{:S(2)}) collective-permute-start(f32[11,18,4,128]{3,2,1,0:T(4,128)S(1)} %get-tuple-element.24), channel_id=1, source_target_pairs={{0,56},{8,0},{16,8},{24,16},{32,24},{40,32},{48,40},{56,48},{1,57}... | collective-permute-start | bytes 1216520 | tf_op jit(solution)/shard_map/ppermute | solution.py:497
  48.1 1.2 %collective-permute-start.4 = (f32[11,18,2,128]{3,2,1,0:T(2,128)S(1)}, f32[11,18,2,128]{3,2,1,0:T(2,128)S(1)}, u32[]{:S(2)}, u32[]{:S(2)}) collective-permute-start(f32[11,18,2,128]{3,2,1,0:T(2,128)S(1)} %get-tuple-element.23), channel_id=1, source_target_pairs={{0,8},{8,16},{16,24},{24,32},{32,40},{40,48},{48,56},{56,0},{1,9},... | collective-permute-start | bytes 608264 | tf_op jit(solution)/shard_map/ppermute | solution.py:497
  49.3 0.9 %shard_map.39.half = f32[11,14,8,256]{3,2,1,0:T(8,128)S(1)} custom-call(s32[4]{0:T(128)S(1)} %pad_add_fusion.place, f32[11,8,8,128]{3,2,1,0:T(8,128)S(1)} %get-tuple-element.18.own, f32[11,8,128]{2,1,0:T(8,128)S(1)} %collective-permute-done.first, f32[11,8,128]{2,1,0:T(8,128)S(1)} %collective-permute-done.1.second, ...), custom_call_target="tpu_custom_call" | custom-call | tf_op jit(solution)/shard_map/pallas_call | solution.py:25
  50.2 1.8 %collective-permute-done.4.y_low = f32[11,18,2,128]{3,2,1,0:T(2,128)S(1)} collective-permute-done((f32[11,18,2,128]{3,2,1,0:T(2,128)S(1)}, f32[11,18,2,128]{3,2,1,0:T(2,128)S(1)}, u32[]{:S(2)}, u32[]{:S(2)}) %collective-permute-start.4) | collective-permute-done | bytes 202784 | tf_op jit(solution)/shard_map/ppermute | solution.py:497
  52.0 2.9 %collective-permute-done.5.y_high = f32[11,18,4,128]{3,2,1,0:T(4,128)S(1)} collective-permute-done((f32[11,18,4,128]{3,2,1,0:T(4,128)S(1)}, f32[11,18,4,128]{3,2,1,0:T(4,128)S(1)}, u32[]{:S(2)}, u32[]{:S(2)}) %collective-permute-start.5) | collective-permute-done | bytes 405536 | tf_op jit(solution)/shard_map/ppermute | solution.py:497
  54.9 3.7 %shard_map.41 = (f32[11,14,16,256]{3,2,1,0:T(8,128)S(1)}, f32[4,14,16,256]{3,2,1,0:T(8,128)S(1)}, f32[7,6,8,128]{3,2,1,0:T(8,128)S(1)}, f32[7,4,8,128]{3,2,1,0:T(8,128)S(1)}) custom-call(s32[4]{0:T(128)S(1)} %pad_add_fusion.place, f32[11,14,8,256]{3,2,1,0:T(8,128)S(1)} %shard_map.39.half, f32[11,18,2,128]{3,2,1,0:T(2,128)S(1)} %collective-permute-done.4.y_low, ...), custom_call_target="tpu_custom_call" | custom-call | tf_op jit(solution)/shard_map/pallas_call | solution.py:25
  58.5 1.9 %collective-permute-start.7 = (f32[7,6,8,128]{3,2,1,0:T(8,128)S(1)}, f32[7,6,8,128]{3,2,1,0:T(8,128)S(1)}, u32[]{:S(2)}, u32[]{:S(2)}) collective-permute-start(f32[7,6,8,128]{3,2,1,0:T(8,128)S(1)} %get-tuple-element.27.own), channel_id=1, source_target_pairs={{64,0},{128,64},{192,128},{256,192},{320,256},{384,320},{448,384},... | collective-permute-start | bytes 516104 | tf_op jit(solution)/shard_map/ppermute | solution.py:503
  60.5 3.4 %collective-permute-start.6 = (f32[7,4,8,128]{3,2,1,0:T(8,128)S(1)}, f32[7,4,8,128]{3,2,1,0:T(8,128)S(1)}, u32[]{:S(2)}, u32[]{:S(2)}) collective-permute-start(f32[7,4,8,128]{3,2,1,0:T(8,128)S(1)} %get-tuple-element.28), channel_id=1, source_target_pairs={{0,64},{64,128},{128,192},{192,256},{256,320},{320,384},{384,448},... | collective-permute-start | bytes 344072 | tf_op jit(solution)/shard_map/ppermute | solution.py:500
  63.8 4.7 %collective-permute-done.6.from_low = f32[7,4,8,128]{3,2,1,0:T(8,128)S(1)} collective-permute-done((f32[7,4,8,128]{3,2,1,0:T(8,128)S(1)}, f32[7,4,8,128]{3,2,1,0:T(8,128)S(1)}, u32[]{:S(2)}, u32[]{:S(2)}) %collective-permute-start.6) | collective-permute-done | bytes 114720 | tf_op jit(solution)/shard_map/ppermute | solution.py:500
  68.6 0.6 collective-permute-start.9
  69.2 1.1 %collective-permute-start.8 = (f32[7,14,4,128]{3,2,1,0:T(4,128)S(1)}, f32[7,14,4,128]{3,2,1,0:T(4,128)S(1)}, u32[]{:S(2)}, u32[]{:S(2)}) collective-permute-start(f32[7,14,4,128]{3,2,1,0:T(4,128)S(1)} %get-tuple-element.29.own), channel_id=1, source_target_pairs={{0,8},{8,16},{16,24},{24,32},{32,40},{40,48},{48,56},{56,0},{1,9},... | collective-permute-start | bytes 602120 | tf_op jit(solution)/shard_map/ppermute | solution.py:497
  70.3 2.7 %collective-permute-done.8.y_low = f32[7,14,4,128]{3,2,1,0:T(4,128)S(1)} collective-permute-done((f32[7,14,4,128]{3,2,1,0:T(4,128)S(1)}, f32[7,14,4,128]{3,2,1,0:T(4,128)S(1)}, u32[]{:S(2)}, u32[]{:S(2)}) %collective-permute-start.8) | collective-permute-done | bytes 200736 | tf_op jit(solution)/shard_map/ppermute | solution.py:497
  73.0 2.3 %collective-permute-done.9.y_high = f32[7,88,128]{2,1,0:T(8,128)S(1)} collective-permute-done((f32[7,88,128]{2,1,0:T(8,128)S(1)}, f32[7,88,128]{2,1,0:T(8,128)S(1)}, u32[]{:S(2)}, u32[]{:S(2)}) %collective-permute-start.9) | collective-permute-done | bytes 315424 | tf_op jit(solution)/shard_map/ppermute | solution.py:497
  75.2 6.5 %shard_map.43 = f32[4,8,8,128]{3,2,1,0:T(8,128)} custom-call(s32[4]{0:T(128)S(1)} %pad_add_fusion.place, f32[11,14,16,256]{3,2,1,0:T(8,128)S(1)} %get-tuple-element.25.grid, f32[4,14,16,256]{3,2,1,0:T(8,128)S(1)} %get-tuple-element.26.fine, f32[7,14,4,128]{3,2,1,0:T(4,128)S(1)} %get-tuple-element.29.own, f32[7,14,4,128]{3,2,1,0:T(4,128)S(1)} %collective-permute-done.8.y_low, ...), custom_call_target="tpu_custom_call" | custom-call | tf_op jit(solution)/shard_map/pallas_call | solution.py:25
  (4 shorter events, 0.1 us)
Async XLA Ops:
  1.9 25.3 %collective-permute-start = (f32[11,8,128]{2,1,0:T(8,128)S(1)}, f32[11,8,128]{2,1,0:T(8,128)S(1)}, u32[]{:S(2)}, u32[]{:S(2)}) collective-permute-start(f32[11,8,128]{2,1,0:T(8,128)S(1)} %get-tuple-element.19), channel_id=1, source_target_pairs={{1,2},{2,1},{3,4},{4,3},{5,6},{6,5},{9,10},{10,9},{11,12},{12,11},... | collective-permute-start | bytes 135176 | tf_op jit(solution)/shard_map/ppermute | solution.py:494
  3.9 23.4 %collective-permute-start.1 = (f32[11,8,128]{2,1,0:T(8,128)S(1)}, f32[11,8,128]{2,1,0:T(8,128)S(1)}, u32[]{:S(2)}, u32[]{:S(2)}) collective-permute-start(f32[11,8,128]{2,1,0:T(8,128)S(1)} %get-tuple-element.20), channel_id=1, source_target_pairs={{0,1},{1,0},{2,3},{3,2},{4,5},{5,4},{6,7},{7,6},{8,9},{9,8},{10,11... | collective-permute-start | bytes 135176 | tf_op jit(solution)/shard_map/ppermute | solution.py:494
  27.9 10.8 %collective-permute-start.3 = (f32[11,5,8,128]{3,2,1,0:T(8,128)S(1)}, f32[11,5,8,128]{3,2,1,0:T(8,128)S(1)}, u32[]{:S(2)}, u32[]{:S(2)}) collective-permute-start(f32[11,5,8,128]{3,2,1,0:T(8,128)S(1)} %get-tuple-element.22), channel_id=1, source_target_pairs={{64,0},{128,64},{192,128},{256,192},{320,256},{384,320},{448,384},... | collective-permute-start | bytes 675848 | tf_op jit(solution)/shard_map/ppermute | solution.py:503
  31.7 7.0 %collective-permute-start.2 = (f32[11,3,8,128]{3,2,1,0:T(8,128)S(1)}, f32[11,3,8,128]{3,2,1,0:T(8,128)S(1)}, u32[]{:S(2)}, u32[]{:S(2)}) collective-permute-start(f32[11,3,8,128]{3,2,1,0:T(8,128)S(1)} %get-tuple-element.21), channel_id=1, source_target_pairs={{0,64},{64,128},{128,192},{192,256},{256,320},{320,384},{384,448},... | collective-permute-start | bytes 405512 | tf_op jit(solution)/shard_map/ppermute | solution.py:500
  39.3 15.6 %collective-permute-start.5 = (f32[11,18,4,128]{3,2,1,0:T(4,128)S(1)}, f32[11,18,4,128]{3,2,1,0:T(4,128)S(1)}, u32[]{:S(2)}, u32[]{:S(2)}) collective-permute-start(f32[11,18,4,128]{3,2,1,0:T(4,128)S(1)} %get-tuple-element.24), channel_id=1, source_target_pairs={{0,56},{8,0},{16,8},{24,16},{32,24},{40,32},{48,40},{56,48},{1,57}... | collective-permute-start | bytes 1216520 | tf_op jit(solution)/shard_map/ppermute | solution.py:497
  48.1 3.9 %collective-permute-start.4 = (f32[11,18,2,128]{3,2,1,0:T(2,128)S(1)}, f32[11,18,2,128]{3,2,1,0:T(2,128)S(1)}, u32[]{:S(2)}, u32[]{:S(2)}) collective-permute-start(f32[11,18,2,128]{3,2,1,0:T(2,128)S(1)} %get-tuple-element.23), channel_id=1, source_target_pairs={{0,8},{8,16},{16,24},{24,32},{32,40},{40,48},{48,56},{56,0},{1,9},... | collective-permute-start | bytes 608264 | tf_op jit(solution)/shard_map/ppermute | solution.py:497
  58.5 10.0 %collective-permute-start.7 = (f32[7,6,8,128]{3,2,1,0:T(8,128)S(1)}, f32[7,6,8,128]{3,2,1,0:T(8,128)S(1)}, u32[]{:S(2)}, u32[]{:S(2)}) collective-permute-start(f32[7,6,8,128]{3,2,1,0:T(8,128)S(1)} %get-tuple-element.27.own), channel_id=1, source_target_pairs={{64,0},{128,64},{192,128},{256,192},{320,256},{384,320},{448,384},... | collective-permute-start | bytes 516104 | tf_op jit(solution)/shard_map/ppermute | solution.py:503
  60.5 8.0 %collective-permute-start.6 = (f32[7,4,8,128]{3,2,1,0:T(8,128)S(1)}, f32[7,4,8,128]{3,2,1,0:T(8,128)S(1)}, u32[]{:S(2)}, u32[]{:S(2)}) collective-permute-start(f32[7,4,8,128]{3,2,1,0:T(8,128)S(1)} %get-tuple-element.28), channel_id=1, source_target_pairs={{0,64},{64,128},{128,192},{192,256},{256,320},{320,384},{384,448},... | collective-permute-start | bytes 344072 | tf_op jit(solution)/shard_map/ppermute | solution.py:500
  68.6 6.7 %collective-permute-start.9 = (f32[7,88,128]{2,1,0:T(8,128)S(1)}, f32[7,88,128]{2,1,0:T(8,128)S(1)}, u32[]{:S(2)}, u32[]{:S(2)}) collective-permute-start(f32[7,88,128]{2,1,0:T(8,128)S(1)} %get-tuple-element.30), channel_id=1, source_target_pairs={{0,56},{8,0},{16,8},{24,16},{32,24},{40,32},{48,40},{56,48},{1,57}... | collective-permute-start | bytes 946184 | tf_op jit(solution)/shard_map/ppermute | solution.py:497
  69.2 3.8 %collective-permute-start.8 = (f32[7,14,4,128]{3,2,1,0:T(4,128)S(1)}, f32[7,14,4,128]{3,2,1,0:T(4,128)S(1)}, u32[]{:S(2)}, u32[]{:S(2)}) collective-permute-start(f32[7,14,4,128]{3,2,1,0:T(4,128)S(1)} %get-tuple-element.29.own), channel_id=1, source_target_pairs={{0,8},{8,16},{16,24},{24,32},{32,40},{40,48},{48,56},{56,0},{1,9},... | collective-permute-start | bytes 602120 | tf_op jit(solution)/shard_map/ppermute | solution.py:497

commit v3 on v2

--- a/solution.py
+++ b/solution.py
@@ -197,7 +197,15 @@
             half[f, l, :, BZ:] = side_lanes(l, tiles)
 
 
-def fine_level(sizes, place, half, y_low, y_high, grid, full, to_down, to_up, rows, rsum, tsum):
+def pair_sums(e, high):
+    return e + high, e + down(e, 0), e + up(e, 0), e + down(e, 1), e + up(e, 1)
+
+
+def weigh(weights, values):
+    return total([a * b for a, b in zip(weights, values)])
+
+
+def fine_level(sizes, place, half, y_low, y_high, whole, full, to_down, to_up, rows, rsum, tsum):
     keep_low, keep_high = kept(place, sizes)
 
     def halo_rows(f, carry):
@@ -207,12 +215,15 @@
             rows[i, 6:8] = y_low[f, i] * keep_low
         tiles = [rows[NL + i] for i in range(4)]
         for l in range(NL):
-            grid[f, l, 0:BY] = half[f, l]
-            grid[f, l, BY:, 0:BZ] = rows[l]
-            grid[f, l, BY:, BZ:] = side_lanes(l, tiles)
+            whole[f, l, 0:BY] = half[f, l]
+            whole[f, l, BY:, 0:BZ] = rows[l]
+            whole[f, l, BY:, BZ:] = side_lanes(l, tiles)
         return carry
 
     loop(0, 11, halo_rows, 0)
+
+    def grid(f, l):
+        return whole[f, l]
 
     yz = fine_mask_args(place, sizes)
     for i in range(4):
@@ -220,17 +231,20 @@
         full[i, NL - 1] = jnp.zeros((ROWS, LANES), F32)
     full[3, NL - 2] = jnp.zeros((ROWS, LANES), F32)
 
+    def weights(c, l):
+        e = grid(8 + c, l)
+        return (e + grid(8 + c, l - 1),) + pair_sums(e, grid(8 + c, l + 1))
+
     def velocities(l, carry):
         good = inside(yz, place[0] * BX + l - XL, sizes[0])
-        p = grid[3, l]
-        for c in range(3):
-            u, e = grid[c, l], grid[8 + c, l]
-            us = neighbours(grid[c, l - 1], u, grid[c, l + 1])
-            es = neighbours(grid[8 + c, l - 1], e, grid[8 + c, l + 1])
-            diag = 6.0 * e + total(es)
-            before = grid[3, l - 1] if c == 0 else down(p, c - 1)
-            push = 1.2 * (grid[4 + c, l] - (p - before)) + 0.6 * couple(e, es, us)
-            full[c, l] = jnp.where(good, 0.4 * u + push / diag, 0.0)
+        p = grid(3, l)
+        for c in range(3):
+            u = grid(c, l)
+            us = neighbours(grid(c, l - 1), u, grid(c, l + 1))
+            ks = weights(c, l)
+            before = grid(3, l - 1) if c == 0 else down(p, c - 1)
+            push = 1.2 * (grid(4 + c, l) - (p - before)) + 0.6 * weigh(ks, us)
+            full[c, l] = jnp.where(good, 0.4 * u + push / total(ks), 0.0)
         return carry
 
     loop(1, NL - 1, velocities, 0)
@@ -241,27 +255,26 @@
 
     def pressures(l, carry):
         good = inside(yz, place[0] * BX + l - XL, sizes[0])
-        ev, ew = grid[9, l], grid[10, l]
-        cell = (grid[8, l] + grid[8, l + 1]) + (ev + up(ev, 0)) + (ew + up(ew, 1))
-        full[3, l] = jnp.where(good, grid[3, l] - (0.5 / 6.0) * cell * (grid[7, l] + outflow(l)), 0.0)
+        ev, ew = grid(9, l), grid(10, l)
+        cell = (grid(8, l) + grid(8, l + 1)) + (ev + up(ev, 0)) + (ew + up(ew, 1))
+        full[3, l] = jnp.where(good, grid(3, l) - (0.5 / 6.0) * cell * (grid(7, l) + outflow(l)), 0.0)
         return carry
 
     loop(1, NL - 2, pressures, 0)
 
     def layer_residual(c, l):
-        u, e = full[c, l], grid[8 + c, l]
+        u = full[c, l]
         us = neighbours(full[c, l - 1], u, full[c, l + 1])
-        es = neighbours(grid[8 + c, l - 1], e, grid[8 + c, l + 1])
-        diag = 6.0 * e + total(es)
+        ks = weights(c, l)
         p = full[3, l]
         before = full[3, l - 1] if c == 0 else down(p, c - 1)
-        return grid[4 + c, l] - (p - before) - 0.5 * (diag * u - couple(e, es, us))
+        return grid(4 + c, l) - (p - before) - 0.5 * (total(ks) * u - weigh(ks, us))
 
     def residuals(m, carry):
         l = XL + 2 * m
         for c in range(3):
             rsum[c, m] = layer_residual(c, l) + layer_residual(c, l + 1)
-        rsum[3, m] = (grid[7, l] + outflow(l)) + (grid[7, l + 1] + outflow(l + 1))
+        rsum[3, m] = (grid(7, l) + outflow(l)) + (grid(7, l + 1) + outflow(l + 1))
         return carry
 
     loop(0, 5, residuals, 0)
@@ -269,7 +282,7 @@
         rsum[i, 5] = jnp.zeros((ROWS, LANES), F32)
     for c in range(3):
         for m in range(6):
-            rsum[4 + c, m] = grid[8 + c, XL + 2 * m] + grid[8 + c, XL + 2 * m + 1]
+            rsum[4 + c, m] = grid(8 + c, XL + 2 * m) + grid(8 + c, XL + 2 * m + 1)
 
     matrix = compact_matrix()
     for f in range(7):
@@ -283,6 +296,43 @@
                 to_up[f, m] = a
 
 
+def sizes_of(c):
+    return (ROWS if c == 1 else BY), (LANES if c == 2 else BZ)
+
+
+def last_terms(sizes, place, whole, fine, sums, base, inv, cells, pbase):
+    fyz = fine_mask_args(place, sizes)
+
+    def grid(f, l):
+        return whole[f, l]
+
+    for x in range(9):
+        l = x + XL
+        good = inside(fyz, place[0] * BX + x, sizes[0])
+        p = fine[3, l]
+        for c in range(3):
+            u, e = fine[c, l], grid(8 + c, l)
+            us = neighbours(fine[c, l - 1], u, fine[c, l + 1])
+            xp, ym, yp, zm, zp = pair_sums(e, grid(8 + c, l + 1))
+            ks = (e + grid(8 + c, l - 1), xp, ym, yp, zm, zp)
+            before = fine[3, l - 1] if c == 0 else down(p, c - 1)
+            push = 1.2 * (grid(4 + c, l) - (p - before)) + 0.6 * weigh(ks, us)
+            over = 1.0 / total(ks)
+            rows, lanes = sizes_of(c)
+            for i, k in enumerate(ks):
+                sums[c, i, x, 0:rows, 0:lanes] = (0.6 * k)[0:rows, 0:lanes]
+            base[c, x, 0:rows, 0:lanes] = jnp.where(good, 0.4 * u + push * over, 0.0)[0:rows, 0:lanes]
+            inv[c, x, 0:rows, 0:lanes] = jnp.where(good, over, 0.0)[0:rows, 0:lanes]
+            if x < BX and c == 0:
+                cell = e + grid(8, l + 1)
+            elif x < BX:
+                cell = cell + (yp if c == 1 else zp)
+        if x < BX:
+            cell = (0.5 / 6.0) * cell
+            cells[x] = cell[0:BY, 0:BZ]
+            pbase[x] = (p - cell * grid(7, l))[0:BY, 0:BZ]
+
+
 def pack_y_mid(own, from_low, from_high, to_down, to_up):
     for f in range(7):
         tiles = [from_low[f, i] for i in range(4)]
@@ -294,7 +344,10 @@
         to_down[f, 6 * ML :] = jnp.zeros((4, BZ), F32)
 
 
-def coarse_levels(sizes, place, grid, fine, own, y_low, y_high, out, mid, um, dm, f2, e2, low, sm, twice, spread, g, un):
+def coarse_levels(
+    sizes, place, last_sums, base, inv, cells, pbase, own, y_low, y_high, out,
+    mid, sums, um, over, dm, f2, e2, low, sm, twice, spread, un,
+):
     blank = jnp.zeros((2, BZ), F32)
     keep_low, keep_high = kept(place, sizes)
 
@@ -316,24 +369,36 @@
     def mid_inside(l):
         return inside(yz, place[0] * (BX // 2) + l - 4, sizes[0] // 2)
 
+    for c in range(3):
+        sums[c, 0, 1] = mid[4 + c, 0] + mid[4 + c, 1]
+
     def first_velocities(l, carry):
         good = mid_inside(l)
         for c in range(3):
-            e = mid[4 + c, l]
-            diag = 6.0 * e + total(neighbours(mid[4 + c, l - 1], e, mid[4 + c, l + 1]))
+            xp, ym, yp, zm, zp = pair_sums(mid[4 + c, l], mid[4 + c, l + 1])
+            diag = total([sums[c, 0, l], xp, ym, yp, zm, zp])
+            sums[c, 0, l + 1] = xp
+            sums[c, 1, l] = ym
+            sums[c, 2, l] = yp
+            sums[c, 3, l] = zm
+            sums[c, 4, l] = zp
             dm[c, l] = diag
-            um[c, l] = jnp.where(good, 4.8 * mid[c, l] / diag, 0.0)
+            inverse = 1.0 / diag
+            over[c, l] = inverse
+            um[c, l] = jnp.where(good, 4.8 * mid[c, l] * inverse, 0.0)
         return carry
 
     loop(1, 13, first_velocities, 0)
+
+    def weights(c, l):
+        return (sums[c, 0, l], sums[c, 0, l + 1]) + tuple(sums[c, i, l] for i in range(1, 5))
 
     def outflow(v, l):
         b, w = v[1, l], v[2, l]
         return (v[0, l + 1] - v[0, l]) + (up(b, 0) - b) + (up(w, 1) - w)
 
     def mid_cell(l):
-        ev, ew = mid[5, l], mid[6, l]
-        return (mid[4, l] + mid[4, l + 1]) + (ev + up(ev, 0)) + (ew + up(ew, 1))
+        return sums[0, 0, l + 1] + sums[1, 2, l] + sums[2, 4, l]
 
     def first_pressures(l, carry):
         q = mid[3, l] + 0.5 * outflow(um, l)
@@ -349,12 +414,11 @@
         return 0.125 * jnp.where(lane_even, a, down(a, 1))
 
     def layer_residual(c, l):
-        u, e = um[c, l], mid[4 + c, l]
+        u = um[c, l]
         us = neighbours(um[c, l - 1], u, um[c, l + 1])
-        es = neighbours(mid[4 + c, l - 1], e, mid[4 + c, l + 1])
         p = um[3, l]
         before = um[3, l - 1] if c == 0 else down(p, c - 1)
-        return mid[c, l] - 0.5 * (p - before) - 0.125 * (dm[c, l] * u - couple(e, es, us))
+        return mid[c, l] - 0.5 * (p - before) - 0.125 * (dm[c, l] * u - weigh(weights(c, l), us))
 
     def residuals(k, carry):
         l = 2 + 2 * k
@@ -409,12 +473,11 @@
         good = mid_inside(l)
         p = um[3, l]
         for c in range(3):
-            u, e = um[c, l], mid[4 + c, l]
+            u = um[c, l]
             us = neighbours(um[c, l - 1], u, um[c, l + 1])
-            es = neighbours(mid[4 + c, l - 1], e, mid[4 + c, l + 1])
             before = um[3, l - 1] if c == 0 else down(p, c - 1)
-            push = 4.8 * (mid[c, l] - 0.5 * (p - before)) + 0.6 * couple(e, es, us)
-            sm[c, l] = jnp.where(good, 0.4 * u + push / dm[c, l], 0.0)
+            push = 4.8 * (mid[c, l] - 0.5 * (p - before)) + 0.6 * weigh(weights(c, l), us)
+            sm[c, l] = jnp.where(good, 0.4 * u + push * over[c, l], 0.0)
         return carry
 
     loop(3, 10, second_velocities, 0)
@@ -438,47 +501,41 @@
         wide = exact_dot(twice[6 * i : 6 * i + 6].reshape(6 * ROWS, BZ), matrix)
         spread[i] = wide.reshape(6, ROWS, LANES)
 
-    for i in range(4):
-        for j in range(11):
-            g[i, j] = fine[i, j + 1] + spread[i, (j + 1) // 2]
-
-    fyz = fine_mask_args(place, sizes)
-
-    def last_velocities(x, carry):
-        good = inside(fyz, place[0] * BX + x, sizes[0])
-        p = g[3, x + 1]
-        for c in range(3):
-            u, e = g[c, x + 1], grid[8 + c, x + XL]
-            us = neighbours(g[c, x], u, g[c, x + 2])
-            es = neighbours(grid[8 + c, x + XL - 1], e, grid[8 + c, x + XL + 1])
-            diag = 6.0 * e + total(es)
-            before = g[3, x] if c == 0 else down(p, c - 1)
-            push = 1.2 * (grid[4 + c, x + XL] - (p - before)) + 0.6 * couple(e, es, us)
-            un[c, x] = jnp.where(good, 0.4 * u + push / diag, 0.0)
-        return carry
-
-    loop(0, 9, last_velocities, 0)
-
-    def last_pressures(x, carry):
-        l = x + XL
-        ev, ew = grid[9, l], grid[10, l]
-        cell = (grid[8, l] + grid[8, l + 1]) + (ev + up(ev, 0)) + (ew + up(ew, 1))
-        p = g[3, x + 1] - (0.5 / 6.0) * cell * (grid[7, l] + outflow(un, x))
-        out[3, x] = p[0:BY, 0:BZ]
-        for c in range(3):
-            out[c, x] = un[c, x, 0:BY, 0:BZ]
-        return carry
-
-    loop(0, BX, last_pressures, 0)
-
-
-GRID = (11, NL, ROWS, LANES)
-FINE_OUT = [GRID, (4, NL, ROWS, LANES), (7, 6, BY, BZ), (7, 4, BY, BZ)]
-FINE_SCRATCH = [(NL + 4, BY, BZ), (7, 6, ROWS, LANES), (42, ROWS, BZ)]
-WIDE = (ROWS, BZ)
+    for m in range(1, 6):
+        p = spread[3, m]
+        for c in range(3):
+            rows, lanes = sizes_of(c)
+            z = spread[c, m]
+            sides = (down(z, 0), up(z, 0), down(z, 1), up(z, 1))
+            for x in (2 * m - 2, 2 * m - 1):
+                if x > BX:
+                    continue
+                zs = (spread[c, (x + 1) // 2], spread[c, (x + 3) // 2]) + sides
+                push = weigh([last_sums[c, i, x, 0:rows, 0:lanes] for i in range(6)], [v[0:rows, 0:lanes] for v in zs])
+                if c > 0:
+                    push = push - 1.2 * (p - down(p, c - 1))[0:rows, 0:lanes]
+                elif x % 2 == 0:
+                    push = push - 1.2 * (p - spread[3, m - 1])[0:rows, 0:lanes]
+                u = base[c, x, 0:rows, 0:lanes] + 0.4 * z[0:rows, 0:lanes] + inv[c, x, 0:rows, 0:lanes] * push
+                un[c, x, 0:rows, 0:lanes] = u
+                if x < BX:
+                    out[c, x] = u[0:BY, 0:BZ]
+
+    for x in range(BX):
+        v, w = un[1, x, :, 0:BZ], un[2, x, 0:BY, :]
+        flow = un[0, x + 1, 0:BY, 0:BZ] - un[0, x, 0:BY, 0:BZ]
+        flow = flow + (up(v, 0) - v)[0:BY] + (up(w, 1) - w)[:, 0:BZ]
+        out[3, x] = pbase[x] + spread[3, (x + 2) // 2, 0:BY, 0:BZ] - cells[x] * flow
+
+
+WIDE, TILE, HUGE = (ROWS, BZ), (BY, BZ), (ROWS, LANES)
+HALF = (11, NL, BY, LANES)
+FINE_OUT = [(11, NL) + HUGE, (4, NL) + HUGE, (7, 6) + TILE, (7, 4) + TILE]
+FINE_SCRATCH = [(NL + 4,) + TILE, (7, 6) + HUGE, (42,) + WIDE]
+LAST_OUT = [(3, 6, 9) + HUGE, (3, 9) + HUGE, (3, 9) + HUGE, (BX,) + TILE, (BX,) + TILE]
 COARSE_SCRATCH = [
-    (7, ML) + WIDE, (4, ML) + WIDE, (3, ML) + WIDE, (4, 5) + WIDE, (3, 7) + WIDE, (4, 5) + WIDE,
-    (4, ML) + WIDE, (24,) + WIDE, (4, 6, ROWS, LANES), (4, 11, ROWS, LANES), (3, 9, ROWS, LANES),
+    (7, ML) + WIDE, (3, 5, ML) + WIDE, (4, ML) + WIDE, (3, ML) + WIDE, (3, ML) + WIDE, (4, 5) + WIDE, (3, 7) + WIDE,
+    (4, 5) + WIDE, (4, ML) + WIDE, (24,) + WIDE, (4, 6) + HUGE, (3, 9) + HUGE,
 ]
 
 
@@ -522,9 +579,9 @@
     )
     y_low = around(upward, "gy", ny, 1)
     y_high = around(downward, "gy", ny, -1)
-    (half,) = call(assemble_own, [(11, NL, BY, LANES)], [], place, own, first, second, x_low, x_high)
-
-    grid, fine, downward, upward = call(
+    (half,) = call(assemble_own, [HALF], [], place, own, first, second, x_low, x_high)
+
+    whole, fine, downward, upward = call(
         functools.partial(fine_level, sizes), FINE_OUT, FINE_SCRATCH, place, half, y_low, y_high
     )
     x_low = to_next(upward, "gx", nx)
@@ -534,9 +591,10 @@
     y_low = around(upward, "gy", ny, 1)
     y_high = around(downward, "gy", ny, -1)
 
+    terms = call(functools.partial(last_terms, sizes), LAST_OUT, [], place, whole, fine)
     (updated,) = call(
         functools.partial(coarse_levels, sizes), [(4, BX) + tile], COARSE_SCRATCH,
-        place, grid, fine, upward, y_low, y_high,
+        place, *terms, upward, y_low, y_high,
     )
     return updated
 

time: 82.6 us -> 79 us (0.956)
  Pallas kernels: 14.2 us -> 11.5 us
  waiting for transfers between devices: 38.3 us -> 37.4 us
    pallas_call x7 -> x8, Pallas kernels: 14.2 us -> 11.5 us  [call(): pl.pallas_call(kernel, out_shape=[jax.ShapeDtypeStruct(s, F32) for s in o...]
    ppermute x4, waiting for transfers between devices: 9.59 us -> 8.62 us  [around(): return lax.ppermute(a, axis, [(i, (i + by) % count) for i in range(count)])]
  transfers between devices with their start and end apart: 10 -> 10, of which waited for: 7 -> 7; matrix products, arithmetic and copies ran while one was open for 0% -> 0% of each run, Pallas kernels for 1% -> 2%
where the time goes in v3:
time: 79 us; the launch traced here: 78.1 us
  waiting for transfers between devices  37.4 us (47%)
  starting transfers between devices  29 us (37%)
  Pallas kernels  11.5 us (15%)
    ppermute x2, waiting for transfers between devices, swap(): return lax.ppermute(a, axis, pairs)  19.1 us
    ppermute x4, starting transfers between devices, around(): return lax.ppermute(a, axis, [(i, (i + by) % count) for i in range(count)])  11.8 us
    pallas_call x8, Pallas kernels, call(): pl.pallas_call(kernel, out_shape=[jax.ShapeDtypeStruct(s, F32) for s in o...  11.5 us
    ppermute x2, waiting for transfers between devices, to_next(): return lax.ppermute(a, axis, [(i, i + 1) for i in range(count - 1)])  9.7 us
    ppermute x4, waiting for transfers between devices, around(): return lax.ppermute(a, axis, [(i, (i + by) % count) for i in range(count)])  8.62 us
    ppermute x2, starting transfers between devices, swap(): return lax.ppermute(a, axis, pairs)  6.24 us
    ppermute x2, starting transfers between devices, to_previous(): return lax.ppermute(a, axis, [(i + 1, i) for i in range(count - 1)])  5.7 us
    ppermute x2, starting transfers between devices, to_next(): return lax.ppermute(a, axis, [(i, i + 1) for i in range(count - 1)])  5.28 us
  transfers between devices with their start and end apart: 10, of which 7 were waited for; matrix products, arithmetic and copies ran while one was open for 0% of the time, Pallas kernels for 2%

profile of v3, /device:TPU:641, one launch (start us, length us, event | category | flops | bytes accessed | tf_op | source)
XLA Modules:
  0.0 78.1 jit_solution(8589415082317260230)
XLA Ops:
  0.1 1.8 %shard_map.37 = (f32[11,8,8,128]{3,2,1,0:T(8,128)S(1)}, f32[11,8,128]{2,1,0:T(8,128)S(1)}, f32[11,8,128]{2,1,0:T(8,128)S(1)}) custom-call(s32[4]{0:T(128)S(1)} %pad_add_fusion.place, f32[4,8,8,128]{3,2,1,0:T(8,128)} %iterate.1, f32[4,8,8,128]{3,2,1,0:T(8,128)} %forcing.1, f32[3,8,8,128]{3,2,1,0:T(8,128)} %viscosity.1), custom_call_target="tpu_custom_call" | custom-call | tf_op jit(solution)/shard_map/pallas_call | solution.py:25
  1.9 1.9 %collective-permute-start = (f32[11,8,128]{2,1,0:T(8,128)S(1)}, f32[11,8,128]{2,1,0:T(8,128)S(1)}, u32[]{:S(2)}, u32[]{:S(2)}) collective-permute-start(f32[11,8,128]{2,1,0:T(8,128)S(1)} %get-tuple-element.24), channel_id=1, source_target_pairs={{1,2},{2,1},{3,4},{4,3},{5,6},{6,5},{9,10},{10,9},{11,12},{12,11},... | collective-permute-start | bytes 135176 | tf_op jit(solution)/shard_map/ppermute | solution.py:551
  3.9 4.3 %collective-permute-start.1 = (f32[11,8,128]{2,1,0:T(8,128)S(1)}, f32[11,8,128]{2,1,0:T(8,128)S(1)}, u32[]{:S(2)}, u32[]{:S(2)}) collective-permute-start(f32[11,8,128]{2,1,0:T(8,128)S(1)} %get-tuple-element.25), channel_id=1, source_target_pairs={{0,1},{1,0},{2,3},{3,2},{4,5},{5,4},{6,7},{7,6},{8,9},{9,8},{10,11... | collective-permute-start | bytes 135176 | tf_op jit(solution)/shard_map/ppermute | solution.py:551
  8.2 19.1 %collective-permute-done.first = f32[11,8,128]{2,1,0:T(8,128)S(1)} collective-permute-done((f32[11,8,128]{2,1,0:T(8,128)S(1)}, f32[11,8,128]{2,1,0:T(8,128)S(1)}, u32[]{:S(2)}, u32[]{:S(2)}) %collective-permute-start) | collective-permute-done | bytes 45088 | tf_op jit(solution)/shard_map/ppermute | solution.py:551
  27.2 0.6 shard_map.38
  27.9 3.8 %collective-permute-start.3 = (f32[11,5,8,128]{3,2,1,0:T(8,128)S(1)}, f32[11,5,8,128]{3,2,1,0:T(8,128)S(1)}, u32[]{:S(2)}, u32[]{:S(2)}) collective-permute-start(f32[11,5,8,128]{3,2,1,0:T(8,128)S(1)} %get-tuple-element.27), channel_id=1, source_target_pairs={{64,0},{128,64},{192,128},{256,192},{320,256},{384,320},{448,384},... | collective-permute-start | bytes 675848 | tf_op jit(solution)/shard_map/ppermute | solution.py:560
  31.7 1.9 %collective-permute-start.2 = (f32[11,3,8,128]{3,2,1,0:T(8,128)S(1)}, f32[11,3,8,128]{3,2,1,0:T(8,128)S(1)}, u32[]{:S(2)}, u32[]{:S(2)}) collective-permute-start(f32[11,3,8,128]{3,2,1,0:T(8,128)S(1)} %get-tuple-element.26), channel_id=1, source_target_pairs={{0,64},{64,128},{128,192},{192,256},{256,320},{320,384},{384,448},... | collective-permute-start | bytes 405512 | tf_op jit(solution)/shard_map/ppermute | solution.py:557
  33.6 5.0 %collective-permute-done.2.from_low = f32[11,3,8,128]{3,2,1,0:T(8,128)S(1)} collective-permute-done((f32[11,3,8,128]{3,2,1,0:T(8,128)S(1)}, f32[11,3,8,128]{3,2,1,0:T(8,128)S(1)}, u32[]{:S(2)}, u32[]{:S(2)}) %collective-permute-start.2) | collective-permute-done | bytes 135200 | tf_op jit(solution)/shard_map/ppermute | solution.py:557
  38.6 0.7 shard_map.40
  39.3 8.8 %collective-permute-start.5 = (f32[11,18,4,128]{3,2,1,0:T(4,128)S(1)}, f32[11,18,4,128]{3,2,1,0:T(4,128)S(1)}, u32[]{:S(2)}, u32[]{:S(2)}) collective-permute-start(f32[11,18,4,128]{3,2,1,0:T(4,128)S(1)} %get-tuple-element.29), channel_id=1, source_target_pairs={{0,56},{8,0},{16,8},{24,16},{32,24},{40,32},{48,40},{56,48},{1,57}... | collective-permute-start | bytes 1216520 | tf_op jit(solution)/shard_map/ppermute | solution.py:554
  48.1 1.2 %collective-permute-start.4 = (f32[11,18,2,128]{3,2,1,0:T(2,128)S(1)}, f32[11,18,2,128]{3,2,1,0:T(2,128)S(1)}, u32[]{:S(2)}, u32[]{:S(2)}) collective-permute-start(f32[11,18,2,128]{3,2,1,0:T(2,128)S(1)} %get-tuple-element.28), channel_id=1, source_target_pairs={{0,8},{8,16},{16,24},{24,32},{32,40},{40,48},{48,56},{56,0},{1,9},... | collective-permute-start | bytes 608264 | tf_op jit(solution)/shard_map/ppermute | solution.py:554
  49.3 0.9 %shard_map.39.half = f32[11,14,8,256]{3,2,1,0:T(8,128)S(1)} custom-call(s32[4]{0:T(128)S(1)} %pad_add_fusion.place, f32[11,8,8,128]{3,2,1,0:T(8,128)S(1)} %get-tuple-element.23.own, f32[11,8,128]{2,1,0:T(8,128)S(1)} %collective-permute-done.first, f32[11,8,128]{2,1,0:T(8,128)S(1)} %collective-permute-done.1.second, ...), custom_call_target="tpu_custom_call" | custom-call | tf_op jit(solution)/shard_map/pallas_call | solution.py:25
  50.2 1.8 %collective-permute-done.4.y_low = f32[11,18,2,128]{3,2,1,0:T(2,128)S(1)} collective-permute-done((f32[11,18,2,128]{3,2,1,0:T(2,128)S(1)}, f32[11,18,2,128]{3,2,1,0:T(2,128)S(1)}, u32[]{:S(2)}, u32[]{:S(2)}) %collective-permute-start.4) | collective-permute-done | bytes 202784 | tf_op jit(solution)/shard_map/ppermute | solution.py:554
  52.0 2.9 %collective-permute-done.5.y_high = f32[11,18,4,128]{3,2,1,0:T(4,128)S(1)} collective-permute-done((f32[11,18,4,128]{3,2,1,0:T(4,128)S(1)}, f32[11,18,4,128]{3,2,1,0:T(4,128)S(1)}, u32[]{:S(2)}, u32[]{:S(2)}) %collective-permute-start.5) | collective-permute-done | bytes 405536 | tf_op jit(solution)/shard_map/ppermute | solution.py:554
  54.9 3.7 %shard_map.41 = (f32[11,14,16,256]{3,2,1,0:T(8,128)S(1)}, f32[4,14,16,256]{3,2,1,0:T(8,128)S(1)}, f32[7,6,8,128]{3,2,1,0:T(8,128)S(1)}, f32[7,4,8,128]{3,2,1,0:T(8,128)S(1)}) custom-call(s32[4]{0:T(128)S(1)} %pad_add_fusion.place, f32[11,14,8,256]{3,2,1,0:T(8,128)S(1)} %shard_map.39.half, f32[11,18,2,128]{3,2,1,0:T(2,128)S(1)} %collective-permute-done.4.y_low, ...), custom_call_target="tpu_custom_call" | custom-call | tf_op jit(solution)/shard_map/pallas_call | solution.py:25
  58.6 1.9 %collective-permute-start.7 = (f32[7,6,8,128]{3,2,1,0:T(8,128)S(1)}, f32[7,6,8,128]{3,2,1,0:T(8,128)S(1)}, u32[]{:S(2)}, u32[]{:S(2)}) collective-permute-start(f32[7,6,8,128]{3,2,1,0:T(8,128)S(1)} %get-tuple-element.37.own), channel_id=1, source_target_pairs={{64,0},{128,64},{192,128},{256,192},{320,256},{384,320},{448,384},... | collective-permute-start | bytes 516104 | tf_op jit(solution)/shard_map/ppermute | solution.py:560
  60.6 3.4 %collective-permute-start.6 = (f32[7,4,8,128]{3,2,1,0:T(8,128)S(1)}, f32[7,4,8,128]{3,2,1,0:T(8,128)S(1)}, u32[]{:S(2)}, u32[]{:S(2)}) collective-permute-start(f32[7,4,8,128]{3,2,1,0:T(8,128)S(1)} %get-tuple-element.38), channel_id=1, source_target_pairs={{0,64},{64,128},{128,192},{192,256},{256,320},{320,384},{384,448},... | collective-permute-start | bytes 344072 | tf_op jit(solution)/shard_map/ppermute | solution.py:557
  63.9 4.7 %collective-permute-done.6.from_low = f32[7,4,8,128]{3,2,1,0:T(8,128)S(1)} collective-permute-done((f32[7,4,8,128]{3,2,1,0:T(8,128)S(1)}, f32[7,4,8,128]{3,2,1,0:T(8,128)S(1)}, u32[]{:S(2)}, u32[]{:S(2)}) %collective-permute-start.6) | collective-permute-done | bytes 114720 | tf_op jit(solution)/shard_map/ppermute | solution.py:557
  68.7 0.6 collective-permute-start.9
  69.3 1.1 %collective-permute-start.8 = (f32[7,14,4,128]{3,2,1,0:T(4,128)S(1)}, f32[7,14,4,128]{3,2,1,0:T(4,128)S(1)}, u32[]{:S(2)}, u32[]{:S(2)}) collective-permute-start(f32[7,14,4,128]{3,2,1,0:T(4,128)S(1)} %get-tuple-element.39.own), channel_id=1, source_target_pairs={{0,8},{8,16},{16,24},{24,32},{32,40},{40,48},{48,56},{56,0},{1,9},... | collective-permute-start | bytes 602120 | tf_op jit(solution)/shard_map/ppermute | solution.py:554
  70.4 1.0 %shard_map.42 = (f32[3,6,9,16,256]{4,3,2,1,0:T(8,128)S(1)}, f32[3,9,16,256]{3,2,1,0:T(8,128)S(1)}, f32[3,9,16,256]{3,2,1,0:T(8,128)S(1)}, f32[8,8,128]{2,1,0:T(8,128)S(1)}, f32[8,8,128]{2,1,0:T(8,128)S(1)}) custom-call(s32[4]{0:T(128)S(1)} %pad_add_fusion.place, f32[11,14,16,256]{3,2,1,0:T(8,128)S(1)} %get-tuple-element.30.whole, ...), custom_call_target="tpu_custom_call" | custom-call | tf_op jit(solution)/shard_map/pallas_call | solution.py:25
  71.4 1.7 %collective-permute-done.8.y_low = f32[7,14,4,128]{3,2,1,0:T(4,128)S(1)} collective-permute-done((f32[7,14,4,128]{3,2,1,0:T(4,128)S(1)}, f32[7,14,4,128]{3,2,1,0:T(4,128)S(1)}, u32[]{:S(2)}, u32[]{:S(2)}) %collective-permute-start.8) | collective-permute-done | bytes 200736 | tf_op jit(solution)/shard_map/ppermute | solution.py:554
  73.1 2.3 %collective-permute-done.9.y_high = f32[7,88,128]{2,1,0:T(8,128)S(1)} collective-permute-done((f32[7,88,128]{2,1,0:T(8,128)S(1)}, f32[7,88,128]{2,1,0:T(8,128)S(1)}, u32[]{:S(2)}, u32[]{:S(2)}) %collective-permute-start.9) | collective-permute-done | bytes 315424 | tf_op jit(solution)/shard_map/ppermute | solution.py:554
  75.3 2.7 %shard_map.44 = f32[4,8,8,128]{3,2,1,0:T(8,128)} custom-call(s32[4]{0:T(128)S(1)} %pad_add_fusion.place, f32[3,6,9,16,256]{4,3,2,1,0:T(8,128)S(1)} %get-tuple-element.32.last_sums, f32[3,9,16,256]{3,2,1,0:T(8,128)S(1)} %get-tuple-element.33.base, f32[3,9,16,256]{3,2,1,0:T(8,128)S(1)} %get-tuple-element.34.inv, f32[8,8,128]{2,1,0:T(8,128)S(1)} %get-tuple-element.35.cells, ...), custom_call_target="tpu_custom_call" | custom-call | tf_op jit(solution)/shard_map/pallas_call | solution.py:25
  (5 shorter events, 0.1 us)
Async XLA Ops:
  1.9 25.3 %collective-permute-start = (f32[11,8,128]{2,1,0:T(8,128)S(1)}, f32[11,8,128]{2,1,0:T(8,128)S(1)}, u32[]{:S(2)}, u32[]{:S(2)}) collective-permute-start(f32[11,8,128]{2,1,0:T(8,128)S(1)} %get-tuple-element.24), channel_id=1, source_target_pairs={{1,2},{2,1},{3,4},{4,3},{5,6},{6,5},{9,10},{10,9},{11,12},{12,11},... | collective-permute-start | bytes 135176 | tf_op jit(solution)/shard_map/ppermute | solution.py:551
  3.9 23.4 %collective-permute-start.1 = (f32[11,8,128]{2,1,0:T(8,128)S(1)}, f32[11,8,128]{2,1,0:T(8,128)S(1)}, u32[]{:S(2)}, u32[]{:S(2)}) collective-permute-start(f32[11,8,128]{2,1,0:T(8,128)S(1)} %get-tuple-element.25), channel_id=1, source_target_pairs={{0,1},{1,0},{2,3},{3,2},{4,5},{5,4},{6,7},{7,6},{8,9},{9,8},{10,11... | collective-permute-start | bytes 135176 | tf_op jit(solution)/shard_map/ppermute | solution.py:551
  27.9 10.8 %collective-permute-start.3 = (f32[11,5,8,128]{3,2,1,0:T(8,128)S(1)}, f32[11,5,8,128]{3,2,1,0:T(8,128)S(1)}, u32[]{:S(2)}, u32[]{:S(2)}) collective-permute-start(f32[11,5,8,128]{3,2,1,0:T(8,128)S(1)} %get-tuple-element.27), channel_id=1, source_target_pairs={{64,0},{128,64},{192,128},{256,192},{320,256},{384,320},{448,384},... | collective-permute-start | bytes 675848 | tf_op jit(solution)/shard_map/ppermute | solution.py:560
  31.7 7.0 %collective-permute-start.2 = (f32[11,3,8,128]{3,2,1,0:T(8,128)S(1)}, f32[11,3,8,128]{3,2,1,0:T(8,128)S(1)}, u32[]{:S(2)}, u32[]{:S(2)}) collective-permute-start(f32[11,3,8,128]{3,2,1,0:T(8,128)S(1)} %get-tuple-element.26), channel_id=1, source_target_pairs={{0,64},{64,128},{128,192},{192,256},{256,320},{320,384},{384,448},... | collective-permute-start | bytes 405512 | tf_op jit(solution)/shard_map/ppermute | solution.py:557
  39.3 15.6 %collective-permute-start.5 = (f32[11,18,4,128]{3,2,1,0:T(4,128)S(1)}, f32[11,18,4,128]{3,2,1,0:T(4,128)S(1)}, u32[]{:S(2)}, u32[]{:S(2)}) collective-permute-start(f32[11,18,4,128]{3,2,1,0:T(4,128)S(1)} %get-tuple-element.29), channel_id=1, source_target_pairs={{0,56},{8,0},{16,8},{24,16},{32,24},{40,32},{48,40},{56,48},{1,57}... | collective-permute-start | bytes 1216520 | tf_op jit(solution)/shard_map/ppermute | solution.py:554
  48.1 3.9 %collective-permute-start.4 = (f32[11,18,2,128]{3,2,1,0:T(2,128)S(1)}, f32[11,18,2,128]{3,2,1,0:T(2,128)S(1)}, u32[]{:S(2)}, u32[]{:S(2)}) collective-permute-start(f32[11,18,2,128]{3,2,1,0:T(2,128)S(1)} %get-tuple-element.28), channel_id=1, source_target_pairs={{0,8},{8,16},{16,24},{24,32},{32,40},{40,48},{48,56},{56,0},{1,9},... | collective-permute-start | bytes 608264 | tf_op jit(solution)/shard_map/ppermute | solution.py:554
  58.6 10.0 %collective-permute-start.7 = (f32[7,6,8,128]{3,2,1,0:T(8,128)S(1)}, f32[7,6,8,128]{3,2,1,0:T(8,128)S(1)}, u32[]{:S(2)}, u32[]{:S(2)}) collective-permute-start(f32[7,6,8,128]{3,2,1,0:T(8,128)S(1)} %get-tuple-element.37.own), channel_id=1, source_target_pairs={{64,0},{128,64},{192,128},{256,192},{320,256},{384,320},{448,384},... | collective-permute-start | bytes 516104 | tf_op jit(solution)/shard_map/ppermute | solution.py:560
  60.6 8.0 %collective-permute-start.6 = (f32[7,4,8,128]{3,2,1,0:T(8,128)S(1)}, f32[7,4,8,128]{3,2,1,0:T(8,128)S(1)}, u32[]{:S(2)}, u32[]{:S(2)}) collective-permute-start(f32[7,4,8,128]{3,2,1,0:T(8,128)S(1)} %get-tuple-element.38), channel_id=1, source_target_pairs={{0,64},{64,128},{128,192},{192,256},{256,320},{320,384},{384,448},... | collective-permute-start | bytes 344072 | tf_op jit(solution)/shard_map/ppermute | solution.py:557
  68.7 6.7 %collective-permute-start.9 = (f32[7,88,128]{2,1,0:T(8,128)S(1)}, f32[7,88,128]{2,1,0:T(8,128)S(1)}, u32[]{:S(2)}, u32[]{:S(2)}) collective-permute-start(f32[7,88,128]{2,1,0:T(8,128)S(1)} %get-tuple-element.40), channel_id=1, source_target_pairs={{0,56},{8,0},{16,8},{24,16},{32,24},{40,32},{48,40},{56,48},{1,57}... | collective-permute-start | bytes 946184 | tf_op jit(solution)/shard_map/ppermute | solution.py:554
  69.3 3.8 %collective-permute-start.8 = (f32[7,14,4,128]{3,2,1,0:T(4,128)S(1)}, f32[7,14,4,128]{3,2,1,0:T(4,128)S(1)}, u32[]{:S(2)}, u32[]{:S(2)}) collective-permute-start(f32[7,14,4,128]{3,2,1,0:T(4,128)S(1)} %get-tuple-element.39.own), channel_id=1, source_target_pairs={{0,8},{8,16},{16,24},{24,32},{32,40},{40,48},{48,56},{56,0},{1,9},... | collective-permute-start | bytes 602120 | tf_op jit(solution)/shard_map/ppermute | solution.py:554

commit v4 on v3

--- a/solution.py
+++ b/solution.py
@@ -51,6 +51,50 @@
 def lane_roll(a, by):
     by = by % a.shape[1]
     return pltpu.roll(a, by, 1) if by else a
+
+
+def fine_above(f, dim):
+    own = f % 4 == dim and f != 3
+    return (3, 2, 3)[f // 4] + own if f % 4 < 3 else (3, 2)[f // 4]
+
+
+def fine_below(f):
+    return 1 if 4 <= f < 8 else 2
+
+
+def mid_above(f, dim):
+    return (4, 5)[f // 4] + (f % 4 == dim and f != 3)
+
+
+def mid_below(f):
+    return (3, 4)[f // 4]
+
+
+def offsets(entries):
+    table, at = {}, 0
+    for key, rows in entries:
+        table[key] = at
+        at += rows
+    return table, -(-at // 8) * 8
+
+
+FINE, MID = range(11), range(7)
+X_UP, X_UP_TILES = offsets(
+    [((f, x), 1) for f in FINE for x in range(BX - fine_below(f), BX)] + [((f, "z"), 1) for f in FINE]
+)
+X_DOWN, X_DOWN_TILES = offsets(
+    [((f, x), 1) for f in FINE for x in range(fine_above(f, 0))] + [((f, "z"), 1) for f in FINE]
+)
+FINE_LAYERS = {
+    f: [x + XL for x in range(-fine_below(f), BX + fine_above(f, 0))] + list(range(NL, NL + 4)) for f in FINE
+}
+Y_UP, Y_UP_ROWS = offsets([((f, l), fine_below(f)) for f in FINE for l in FINE_LAYERS[f]])
+Y_DOWN, Y_DOWN_ROWS = offsets([((f, l), fine_above(f, 1)) for f in FINE for l in FINE_LAYERS[f]])
+MX_UP, MX_UP_ROWS = offsets([((f, m), mid_above(f, 1)) for f in MID for m in range(4 - mid_below(f), 4)])
+MX_DOWN, MX_DOWN_ROWS = offsets([((f, m), mid_above(f, 1)) for f in MID for m in range(mid_above(f, 0))])
+MID_LAYERS = {f: [m + 4 for m in range(-mid_below(f), 4 + mid_above(f, 0))] for f in MID}
+MY_UP, MY_UP_ROWS = offsets([((f, l), mid_below(f)) for f in MID for l in MID_LAYERS[f]])
+MY_DOWN, MY_DOWN_ROWS = offsets([((f, l), mid_above(f, 1)) for f in MID for l in MID_LAYERS[f]])
 
 
 def pack_z(place, iterate, forcing, viscosity, own, first, second, sems):
@@ -85,29 +129,40 @@
 
 def pack_x(place, own, first, second, to_up, to_down):
     lane = iota((BY, BZ), 1)
-    for f in range(11):
+    for f in FINE:
         low, high = strips(place, first, second, f)
-        for i in range(XL):
-            to_up[f, i] = own[f, BX - XL + i]
-        to_up[f, XL] = jnp.where(lane >= 96, low, lane_roll(high, -32))
-        for i in range(XH):
-            to_down[f, i] = own[f, i]
-        to_down[f, XH] = jnp.where(lane < 64, low, lane_roll(high, 64))
+        to_up[X_UP[f, "z"]] = jnp.where(lane >= 96, low, lane_roll(high, -32))
+        to_down[X_DOWN[f, "z"]] = jnp.where(lane < 64, low, lane_roll(high, 64))
+        for x in range(BX - fine_below(f), BX):
+            to_up[X_UP[f, x]] = own[f, x]
+        for x in range(fine_above(f, 0)):
+            to_down[X_DOWN[f, x]] = own[f, x]
+
+
+def fine_tile(own, from_low, from_high, f, l):
+    x = l - XL
+    if 0 <= x < BX:
+        return own[f, x]
+    if x < 0:
+        return from_low[X_UP[f, BX + x]] if -x <= fine_below(f) else None
+    return from_high[X_DOWN[f, x - BX]] if x - BX < fine_above(f, 0) else None
+
+
+def strip_tiles(place, first, second, from_low, from_high, f):
+    low, high = strips(place, first, second, f)
+    return [low, high, from_low[X_UP[f, "z"]], from_high[X_DOWN[f, "z"]]]
 
 
 def pack_y(place, own, first, second, from_low, from_high, to_up, to_down):
-    def field(f, carry):
-        low, high = strips(place, first, second, f)
-        tiles = [from_low[f, i] for i in range(XL)]
-        tiles += [own[f, i] for i in range(BX)]
-        tiles += [from_high[f, i] for i in range(XH)]
-        tiles += [low, high, from_low[f, XL], from_high[f, XH]]
-        for i, tile in enumerate(tiles):
-            to_up[f, i] = tile[BY - XL :, :]
-            to_down[f, i] = tile[:XH, :]
-        return carry
-
-    loop(0, 11, field, 0)
+    for f in FINE:
+        sides = strip_tiles(place, first, second, from_low, from_high, f)
+        below, above = fine_below(f), fine_above(f, 1)
+        for l in FINE_LAYERS[f]:
+            tile = sides[l - NL] if l >= NL else fine_tile(own, from_low, from_high, f, l)
+            at = Y_UP[f, l]
+            to_up[at : at + below] = tile[BY - below :, :]
+            at = Y_DOWN[f, l]
+            to_down[at : at + above] = tile[:above, :]
 
 
 def inside_yz(place, rows, lanes, ny, nz, end_y, low_y, end_z, low_z, by, bz):
@@ -182,19 +237,12 @@
 
 
 def assemble_own(place, own, first, second, from_low, from_high, half):
-    for f in range(11):
-        low, high = strips(place, first, second, f)
-        tiles = [low, high, from_low[f, XL], from_high[f, XH]]
+    for f in FINE:
+        sides = strip_tiles(place, first, second, from_low, from_high, f)
         for l in range(NL):
-            x = l - XL
-            if x < 0:
-                body = from_low[f, l]
-            elif x < BX:
-                body = own[f, x]
-            else:
-                body = from_high[f, x - BX]
-            half[f, l, :, 0:BZ] = body
-            half[f, l, :, BZ:] = side_lanes(l, tiles)
+            body = fine_tile(own, from_low, from_high, f, l)
+            half[f, l, :, 0:BZ] = jnp.zeros((BY, BZ), F32) if body is None else body
+            half[f, l, :, BZ:] = side_lanes(l, sides)
 
 
 def pair_sums(e, high):
@@ -205,22 +253,22 @@
     return total([a * b for a, b in zip(weights, values)])
 
 
-def fine_level(sizes, place, half, y_low, y_high, whole, full, to_down, to_up, rows, rsum, tsum):
+def fine_level(sizes, place, half, y_low, y_high, whole, full, middle, to_down, to_up, rows, rsum, tsum):
     keep_low, keep_high = kept(place, sizes)
 
-    def halo_rows(f, carry):
-        for i in range(NL + 4):
-            rows[i, 0:XH] = y_high[f, i] * keep_high
-            rows[i, XH:6] = jnp.zeros((2, BZ), F32)
-            rows[i, 6:8] = y_low[f, i] * keep_low
-        tiles = [rows[NL + i] for i in range(4)]
+    for f in FINE:
+        below, above = fine_below(f), fine_above(f, 1)
+        for l in FINE_LAYERS[f]:
+            rows[f, l] = jnp.zeros((BY, BZ), F32)
+            at = Y_DOWN[f, l]
+            rows[f, l, 0:above] = y_high[at : at + above] * keep_high
+            at = Y_UP[f, l]
+            rows[f, l, BY - below :] = y_low[at : at + below] * keep_low
+        sides = [rows[f, NL + i] for i in range(4)]
         for l in range(NL):
             whole[f, l, 0:BY] = half[f, l]
-            whole[f, l, BY:, 0:BZ] = rows[l]
-            whole[f, l, BY:, BZ:] = side_lanes(l, tiles)
-        return carry
-
-    loop(0, 11, halo_rows, 0)
+            whole[f, l, BY:, 0:BZ] = rows[f, l] if l in FINE_LAYERS[f] else jnp.zeros((BY, BZ), F32)
+            whole[f, l, BY:, BZ:] = side_lanes(l, sides)
 
     def grid(f, l):
         return whole[f, l]
@@ -287,13 +335,18 @@
     matrix = compact_matrix()
     for f in range(7):
         tsum[6 * f : 6 * f + 6] = exact_dot(rsum[f].reshape(6 * ROWS, LANES), matrix).reshape(6, ROWS, BZ)
-    for f in range(7):
-        for m in range(6):
+    for f in MID:
+        rows_sent = mid_above(f, 1)
+        for m in range(mid_above(f, 0)):
             i = 6 * f + m
             a = tsum[i, pl.ds(0, 8, stride=2), :] + tsum[i, pl.ds(1, 8, stride=2), :]
-            to_down[f, m] = a
+            at = MX_DOWN[f, m]
+            to_down[at : at + rows_sent] = a[:rows_sent]
             if m < 4:
-                to_up[f, m] = a
+                middle[f, m] = a
+            if (f, m) in MX_UP:
+                at = MX_UP[f, m]
+                to_up[at : at + rows_sent] = a[:rows_sent]
 
 
 def sizes_of(c):
@@ -333,33 +386,44 @@
             pbase[x] = (p - cell * grid(7, l))[0:BY, 0:BZ]
 
 
-def pack_y_mid(own, from_low, from_high, to_down, to_up):
-    for f in range(7):
-        tiles = [from_low[f, i] for i in range(4)]
-        tiles += [own[f, i] for i in range(4)]
-        tiles += [from_high[f, i] for i in range(6)]
-        for i, tile in enumerate(tiles):
-            to_down[f, 6 * i : 6 * i + 6] = tile[:6, :]
-            to_up[f, i] = tile[:4, :]
-        to_down[f, 6 * ML :] = jnp.zeros((4, BZ), F32)
+def pack_y_mid(own, from_low, from_high, to_down, to_up, rows):
+    for f in MID:
+        below, above = mid_below(f), mid_above(f, 1)
+        for l in range(ML):
+            if l not in MID_LAYERS[f]:
+                rows[f, l] = jnp.zeros((4, BZ), F32)
+                continue
+            m = l - 4
+            if m < 0:
+                at = MX_UP[f, 4 + m]
+                tile = from_low[at : at + above]
+            elif m < 4:
+                tile = own[f, m, 0:above]
+            else:
+                at = MX_DOWN[f, m - 4]
+                tile = from_high[at : at + above]
+            at = MY_DOWN[f, l]
+            to_down[at : at + above] = tile
+            at = MY_UP[f, l]
+            to_up[at : at + below] = tile[4 - below : 4]
+            rows[f, l] = tile[0:4]
 
 
 def coarse_levels(
     sizes, place, last_sums, base, inv, cells, pbase, own, y_low, y_high, out,
     mid, sums, um, over, dm, f2, e2, low, sm, twice, spread, un,
 ):
-    blank = jnp.zeros((2, BZ), F32)
     keep_low, keep_high = kept(place, sizes)
-
-    def assemble(f, carry):
+    for f in MID:
+        below, above = mid_below(f), mid_above(f, 1)
         for l in range(ML):
+            mid[f, l] = jnp.zeros((ROWS, BZ), F32)
             mid[f, l, 0:4] = own[f, l]
-            mid[f, l, 4:10] = y_high[f, 6 * l : 6 * l + 6] * keep_high
-            mid[f, l, 10:12] = blank
-            mid[f, l, 12:16] = y_low[f, l] * keep_low
-        return carry
-
-    loop(0, 7, assemble, 0)
+            if l in MID_LAYERS[f]:
+                at = MY_DOWN[f, l]
+                mid[f, l, 4 : 4 + above] = y_high[at : at + above] * keep_high
+                at = MY_UP[f, l]
+                mid[f, l, ROWS - below :] = y_low[at : at + below] * keep_low
 
     shape = (ROWS, BZ)
     yz = inside_yz(place, ROWS, BZ, sizes[1] // 2, sizes[2] // 2, 10, 4, BZ // 2 + 8, 8, BY // 2, BZ // 2)
@@ -530,8 +594,8 @@
 
 WIDE, TILE, HUGE = (ROWS, BZ), (BY, BZ), (ROWS, LANES)
 HALF = (11, NL, BY, LANES)
-FINE_OUT = [(11, NL) + HUGE, (4, NL) + HUGE, (7, 6) + TILE, (7, 4) + TILE]
-FINE_SCRATCH = [(NL + 4,) + TILE, (7, 6) + HUGE, (42,) + WIDE]
+FINE_OUT = [(11, NL) + HUGE, (4, NL) + HUGE, (7, 4) + TILE, (MX_DOWN_ROWS, BZ), (MX_UP_ROWS, BZ)]
+FINE_SCRATCH = [(11, NL + 4) + TILE, (7, 6) + HUGE, (42,) + WIDE]
 LAST_OUT = [(3, 6, 9) + HUGE, (3, 9) + HUGE, (3, 9) + HUGE, (BX,) + TILE, (BX,) + TILE]
 COARSE_SCRATCH = [
     (7, ML) + WIDE, (3, 5, ML) + WIDE, (4, ML) + WIDE, (3, ML) + WIDE, (3, ML) + WIDE, (4, 5) + WIDE, (3, 7) + WIDE,
@@ -570,31 +634,33 @@
     first = swap(first, "gz", nz, 1)
     second = swap(second, "gz", nz, 0)
 
-    upward, downward = call(pack_x, [(11, XL + 1) + tile, (11, XH + 1) + tile], [], place, own, first, second)
+    upward, downward = call(pack_x, [(X_UP_TILES,) + tile, (X_DOWN_TILES,) + tile], [], place, own, first, second)
     x_low = to_next(upward, "gx", nx)
     x_high = to_previous(downward, "gx", nx)
 
     upward, downward = call(
-        pack_y, [(11, NL + 4, XL, BZ), (11, NL + 4, XH, BZ)], [], place, own, first, second, x_low, x_high
+        pack_y, [(Y_UP_ROWS, BZ), (Y_DOWN_ROWS, BZ)], [], place, own, first, second, x_low, x_high
     )
     y_low = around(upward, "gy", ny, 1)
     y_high = around(downward, "gy", ny, -1)
     (half,) = call(assemble_own, [HALF], [], place, own, first, second, x_low, x_high)
 
-    whole, fine, downward, upward = call(
+    whole, fine, middle, downward, upward = call(
         functools.partial(fine_level, sizes), FINE_OUT, FINE_SCRATCH, place, half, y_low, y_high
     )
     x_low = to_next(upward, "gx", nx)
     x_high = to_previous(downward, "gx", nx)
 
-    downward, upward = call(pack_y_mid, [(7, 6 * ML + 4, BZ), (7, ML, 4, BZ)], [], downward, x_low, x_high)
+    downward, upward, middle = call(
+        pack_y_mid, [(MY_DOWN_ROWS, BZ), (MY_UP_ROWS, BZ), (7, ML, 4, BZ)], [], middle, x_low, x_high
+    )
     y_low = around(upward, "gy", ny, 1)
     y_high = around(downward, "gy", ny, -1)
 
     terms = call(functools.partial(last_terms, sizes), LAST_OUT, [], place, whole, fine)
     (updated,) = call(
         functools.partial(coarse_levels, sizes), [(4, BX) + tile], COARSE_SCRATCH,
-        place, *terms, upward, y_low, y_high,
+        place, *terms, middle, y_low, y_high,
     )
     return updated
 

time: 79 us -> 75.3 us (0.953)
  waiting for transfers between devices: 37.4 us -> 33.2 us
    ppermute x4, waiting for transfers between devices: 8.62 us -> 6.33 us  [around(): return lax.ppermute(a, axis, [(i, (i + by) % count) for i in range(count)])]
    ppermute x2, waiting for transfers between devices: 9.7 us -> 7.8 us  [to_next(): return lax.ppermute(a, axis, [(i, i + 1) for i in range(count - 1)])]
  transfers between devices with their start and end apart: 10 -> 10, of which waited for: 7 -> 7; matrix products, arithmetic and copies ran while one was open for 0% -> 0% of each run, Pallas kernels for 2% -> 3%
where the time goes in v4:
time: 75.3 us; the launch traced here: 73.9 us
  waiting for transfers between devices  33.2 us (44%)
  starting transfers between devices  29.1 us (39%)
  Pallas kernels  11.5 us (15%)
    ppermute x2, waiting for transfers between devices, swap(): return lax.ppermute(a, axis, pairs)  19.1 us
    ppermute x4, starting transfers between devices, around(): return lax.ppermute(a, axis, [(i, (i + by) % count) for i in range(count)])  11.9 us
    pallas_call x8, Pallas kernels, call(): pl.pallas_call(kernel, out_shape=[jax.ShapeDtypeStruct(s, F32) for s in o...  11.5 us
    ppermute x2, waiting for transfers between devices, to_next(): return lax.ppermute(a, axis, [(i, i + 1) for i in range(count - 1)])  7.8 us
    ppermute x4, waiting for transfers between devices, around(): return lax.ppermute(a, axis, [(i, (i + by) % count) for i in range(count)])  6.33 us
    ppermute x2, starting transfers between devices, swap(): return lax.ppermute(a, axis, pairs)  6.24 us
    ppermute x2, starting transfers between devices, to_previous(): return lax.ppermute(a, axis, [(i + 1, i) for i in range(count - 1)])  5.7 us
    ppermute x2, starting transfers between devices, to_next(): return lax.ppermute(a, axis, [(i, i + 1) for i in range(count - 1)])  5.28 us
  transfers between devices with their start and end apart: 10, of which 7 were waited for; matrix products, arithmetic and copies ran while one was open for 0% of the time, Pallas kernels for 3%

profile of v4, /device:TPU:641, one launch (start us, length us, event | category | flops | bytes accessed | tf_op | source)
XLA Modules:
  0.0 73.9 jit_solution(8017562517757166113)
XLA Ops:
  0.1 1.8 %shard_map.37 = (f32[11,8,8,128]{3,2,1,0:T(8,128)S(1)}, f32[11,8,128]{2,1,0:T(8,128)S(1)}, f32[11,8,128]{2,1,0:T(8,128)S(1)}) custom-call(s32[4]{0:T(128)S(1)} %pad_add_fusion.place, f32[4,8,8,128]{3,2,1,0:T(8,128)} %iterate.1, f32[4,8,8,128]{3,2,1,0:T(8,128)} %forcing.1, f32[3,8,8,128]{3,2,1,0:T(8,128)} %viscosity.1), custom_call_target="tpu_custom_call" | custom-call | tf_op jit(solution)/shard_map/pallas_call | solution.py:25
  1.9 1.9 %collective-permute-start = (f32[11,8,128]{2,1,0:T(8,128)S(1)}, f32[11,8,128]{2,1,0:T(8,128)S(1)}, u32[]{:S(2)}, u32[]{:S(2)}) collective-permute-start(f32[11,8,128]{2,1,0:T(8,128)S(1)} %get-tuple-element.26), channel_id=1, source_target_pairs={{1,2},{2,1},{3,4},{4,3},{5,6},{6,5},{9,10},{10,9},{11,12},{12,11},... | collective-permute-start | bytes 135176 | tf_op jit(solution)/shard_map/ppermute | solution.py:615
  3.9 4.3 %collective-permute-start.1 = (f32[11,8,128]{2,1,0:T(8,128)S(1)}, f32[11,8,128]{2,1,0:T(8,128)S(1)}, u32[]{:S(2)}, u32[]{:S(2)}) collective-permute-start(f32[11,8,128]{2,1,0:T(8,128)S(1)} %get-tuple-element.27), channel_id=1, source_target_pairs={{0,1},{1,0},{2,3},{3,2},{4,5},{5,4},{6,7},{7,6},{8,9},{9,8},{10,11... | collective-permute-start | bytes 135176 | tf_op jit(solution)/shard_map/ppermute | solution.py:615
  8.2 19.1 %collective-permute-done.first = f32[11,8,128]{2,1,0:T(8,128)S(1)} collective-permute-done((f32[11,8,128]{2,1,0:T(8,128)S(1)}, f32[11,8,128]{2,1,0:T(8,128)S(1)}, u32[]{:S(2)}, u32[]{:S(2)}) %collective-permute-start) | collective-permute-done | bytes 45088 | tf_op jit(solution)/shard_map/ppermute | solution.py:615
  27.2 0.6 shard_map.38
  27.9 3.8 %collective-permute-start.3 = (f32[48,8,128]{2,1,0:T(8,128)S(1)}, f32[48,8,128]{2,1,0:T(8,128)S(1)}, u32[]{:S(2)}, u32[]{:S(2)}) collective-permute-start(f32[48,8,128]{2,1,0:T(8,128)S(1)} %get-tuple-element.29), channel_id=1, source_target_pairs={{64,0},{128,64},{192,128},{256,192},{320,256},{384,320},{448,384},... | collective-permute-start | bytes 589832 | tf_op jit(solution)/shard_map/ppermute | solution.py:624
  31.7 1.9 %collective-permute-start.2 = (f32[32,8,128]{2,1,0:T(8,128)S(1)}, f32[32,8,128]{2,1,0:T(8,128)S(1)}, u32[]{:S(2)}, u32[]{:S(2)}) collective-permute-start(f32[32,8,128]{2,1,0:T(8,128)S(1)} %get-tuple-element.28), channel_id=1, source_target_pairs={{0,64},{64,128},{128,192},{192,256},{256,320},{320,384},{384,448},... | collective-permute-start | bytes 393224 | tf_op jit(solution)/shard_map/ppermute | solution.py:621
  33.6 5.0 %collective-permute-done.2.from_low = f32[32,8,128]{2,1,0:T(8,128)S(1)} collective-permute-done((f32[32,8,128]{2,1,0:T(8,128)S(1)}, f32[32,8,128]{2,1,0:T(8,128)S(1)}, u32[]{:S(2)}, u32[]{:S(2)}) %collective-permute-start.2) | collective-permute-done | bytes 131104 | tf_op jit(solution)/shard_map/ppermute | solution.py:621
  38.6 0.6 shard_map.40
  39.2 8.8 %collective-permute-start.5 = (f32[536,128]{1,0:T(8,128)S(1)}, f32[536,128]{1,0:T(8,128)S(1)}, u32[]{:S(2)}, u32[]{:S(2)}) collective-permute-start(f32[536,128]{1,0:T(8,128)S(1)} %get-tuple-element.31), channel_id=1, source_target_pairs={{0,56},{8,0},{16,8},{24,16},{32,24},{40,32},{48,40},{56,48},{1,57}... | collective-permute-start | bytes 823304 | tf_op jit(solution)/shard_map/ppermute | solution.py:618
  48.1 1.2 %collective-permute-start.4 = (f32[304,128]{1,0:T(8,128)S(1)}, f32[304,128]{1,0:T(8,128)S(1)}, u32[]{:S(2)}, u32[]{:S(2)}) collective-permute-start(f32[304,128]{1,0:T(8,128)S(1)} %get-tuple-element.30), channel_id=1, source_target_pairs={{0,8},{8,16},{16,24},{24,32},{32,40},{40,48},{48,56},{56,0},{1,9},... | collective-permute-start | bytes 466952 | tf_op jit(solution)/shard_map/ppermute | solution.py:618
  49.3 0.9 %shard_map.39.half = f32[11,14,8,256]{3,2,1,0:T(8,128)S(1)} custom-call(s32[4]{0:T(128)S(1)} %pad_add_fusion.place, f32[11,8,8,128]{3,2,1,0:T(8,128)S(1)} %get-tuple-element.25.own, f32[11,8,128]{2,1,0:T(8,128)S(1)} %collective-permute-done.first, f32[11,8,128]{2,1,0:T(8,128)S(1)} %collective-permute-done.1.second, ...), custom_call_target="tpu_custom_call" | custom-call | tf_op jit(solution)/shard_map/pallas_call | solution.py:25
  50.2 1.3 %collective-permute-done.4.y_low = f32[304,128]{1,0:T(8,128)S(1)} collective-permute-done((f32[304,128]{1,0:T(8,128)S(1)}, f32[304,128]{1,0:T(8,128)S(1)}, u32[]{:S(2)}, u32[]{:S(2)}) %collective-permute-start.4) | collective-permute-done | bytes 155680 | tf_op jit(solution)/shard_map/ppermute | solution.py:618
  51.4 2.3 %collective-permute-done.5.y_high = f32[536,128]{1,0:T(8,128)S(1)} collective-permute-done((f32[536,128]{1,0:T(8,128)S(1)}, f32[536,128]{1,0:T(8,128)S(1)}, u32[]{:S(2)}, u32[]{:S(2)}) %collective-permute-start.5) | collective-permute-done | bytes 274464 | tf_op jit(solution)/shard_map/ppermute | solution.py:618
  53.7 3.6 %shard_map.41 = (f32[11,14,16,256]{3,2,1,0:T(8,128)S(1)}, f32[4,14,16,256]{3,2,1,0:T(8,128)S(1)}, f32[7,4,8,128]{3,2,1,0:T(8,128)S(1)}, f32[160,128]{1,0:T(8,128)S(1)}, f32[120,128]{1,0:T(8,128)S(1)}) custom-call(s32[4]{0:T(128)S(1)} %pad_add_fusion.place, f32[11,14,8,256]{3,2,1,0:T(8,128)S(1)} %shard_map.39.half, ...), custom_call_target="tpu_custom_call" | custom-call | tf_op jit(solution)/shard_map/pallas_call | solution.py:25
  57.3 1.9 %collective-permute-start.7 = (f32[160,128]{1,0:T(8,128)S(1)}, f32[160,128]{1,0:T(8,128)S(1)}, u32[]{:S(2)}, u32[]{:S(2)}) collective-permute-start(f32[160,128]{1,0:T(8,128)S(1)} %get-tuple-element.41), channel_id=1, source_target_pairs={{64,0},{128,64},{192,128},{256,192},{320,256},{384,320},{448,384},... | collective-permute-start | bytes 245768 | tf_op jit(solution)/shard_map/ppermute | solution.py:624
  59.3 3.4 %collective-permute-start.6 = (f32[120,128]{1,0:T(8,128)S(1)}, f32[120,128]{1,0:T(8,128)S(1)}, u32[]{:S(2)}, u32[]{:S(2)}) collective-permute-start(f32[120,128]{1,0:T(8,128)S(1)} %get-tuple-element.40), channel_id=1, source_target_pairs={{0,64},{64,128},{128,192},{192,256},{256,320},{320,384},{384,448},... | collective-permute-start | bytes 184328 | tf_op jit(solution)/shard_map/ppermute | solution.py:621
  62.6 2.8 %collective-permute-done.6.from_low = f32[120,128]{1,0:T(8,128)S(1)} collective-permute-done((f32[120,128]{1,0:T(8,128)S(1)}, f32[120,128]{1,0:T(8,128)S(1)}, u32[]{:S(2)}, u32[]{:S(2)}) %collective-permute-start.6) | collective-permute-done | bytes 61472 | tf_op jit(solution)/shard_map/ppermute | solution.py:621
  65.5 1.6 %collective-permute-start.9 = (f32[408,128]{1,0:T(8,128)S(1)}, f32[408,128]{1,0:T(8,128)S(1)}, u32[]{:S(2)}, u32[]{:S(2)}) collective-permute-start(f32[408,128]{1,0:T(8,128)S(1)} %get-tuple-element.44), channel_id=1, source_target_pairs={{0,56},{8,0},{16,8},{24,16},{32,24},{40,32},{48,40},{56,48},{1,57}... | collective-permute-start | bytes 626696 | tf_op jit(solution)/shard_map/ppermute | solution.py:618
  67.1 0.3 collective-permute-start.8
  67.4 1.0 %shard_map.42 = (f32[3,6,9,16,256]{4,3,2,1,0:T(8,128)S(1)}, f32[3,9,16,256]{3,2,1,0:T(8,128)S(1)}, f32[3,9,16,256]{3,2,1,0:T(8,128)S(1)}, f32[8,8,128]{2,1,0:T(8,128)S(1)}, f32[8,8,128]{2,1,0:T(8,128)S(1)}) custom-call(s32[4]{0:T(128)S(1)} %pad_add_fusion.place, f32[11,14,16,256]{3,2,1,0:T(8,128)S(1)} %get-tuple-element.32.whole, ...), custom_call_target="tpu_custom_call" | custom-call | tf_op jit(solution)/shard_map/pallas_call | solution.py:25
  68.3 1.2 %collective-permute-done.8.y_low = f32[296,128]{1,0:T(8,128)S(1)} collective-permute-done((f32[296,128]{1,0:T(8,128)S(1)}, f32[296,128]{1,0:T(8,128)S(1)}, u32[]{:S(2)}, u32[]{:S(2)}) %collective-permute-start.8) | collective-permute-done | bytes 151584 | tf_op jit(solution)/shard_map/ppermute | solution.py:618
  69.5 1.6 %collective-permute-done.9.y_high = f32[408,128]{1,0:T(8,128)S(1)} collective-permute-done((f32[408,128]{1,0:T(8,128)S(1)}, f32[408,128]{1,0:T(8,128)S(1)}, u32[]{:S(2)}, u32[]{:S(2)}) %collective-permute-start.9) | collective-permute-done | bytes 208928 | tf_op jit(solution)/shard_map/ppermute | solution.py:618
  71.1 2.8 %shard_map.44 = f32[4,8,8,128]{3,2,1,0:T(8,128)} custom-call(s32[4]{0:T(128)S(1)} %pad_add_fusion.place, f32[3,6,9,16,256]{4,3,2,1,0:T(8,128)S(1)} %get-tuple-element.34.last_sums, f32[3,9,16,256]{3,2,1,0:T(8,128)S(1)} %get-tuple-element.35.base, f32[3,9,16,256]{3,2,1,0:T(8,128)S(1)} %get-tuple-element.36.inv, f32[8,8,128]{2,1,0:T(8,128)S(1)} %get-tuple-element.37.cells, ...), custom_call_target="tpu_custom_call" | custom-call | tf_op jit(solution)/shard_map/pallas_call | solution.py:25
  (5 shorter events, 0.2 us)
Async XLA Ops:
  1.9 25.3 %collective-permute-start = (f32[11,8,128]{2,1,0:T(8,128)S(1)}, f32[11,8,128]{2,1,0:T(8,128)S(1)}, u32[]{:S(2)}, u32[]{:S(2)}) collective-permute-start(f32[11,8,128]{2,1,0:T(8,128)S(1)} %get-tuple-element.26), channel_id=1, source_target_pairs={{1,2},{2,1},{3,4},{4,3},{5,6},{6,5},{9,10},{10,9},{11,12},{12,11},... | collective-permute-start | bytes 135176 | tf_op jit(solution)/shard_map/ppermute | solution.py:615
  3.9 23.4 %collective-permute-start.1 = (f32[11,8,128]{2,1,0:T(8,128)S(1)}, f32[11,8,128]{2,1,0:T(8,128)S(1)}, u32[]{:S(2)}, u32[]{:S(2)}) collective-permute-start(f32[11,8,128]{2,1,0:T(8,128)S(1)} %get-tuple-element.27), channel_id=1, source_target_pairs={{0,1},{1,0},{2,3},{3,2},{4,5},{5,4},{6,7},{7,6},{8,9},{9,8},{10,11... | collective-permute-start | bytes 135176 | tf_op jit(solution)/shard_map/ppermute | solution.py:615
  27.9 10.7 %collective-permute-start.3 = (f32[48,8,128]{2,1,0:T(8,128)S(1)}, f32[48,8,128]{2,1,0:T(8,128)S(1)}, u32[]{:S(2)}, u32[]{:S(2)}) collective-permute-start(f32[48,8,128]{2,1,0:T(8,128)S(1)} %get-tuple-element.29), channel_id=1, source_target_pairs={{64,0},{128,64},{192,128},{256,192},{320,256},{384,320},{448,384},... | collective-permute-start | bytes 589832 | tf_op jit(solution)/shard_map/ppermute | solution.py:624
  31.7 6.9 %collective-permute-start.2 = (f32[32,8,128]{2,1,0:T(8,128)S(1)}, f32[32,8,128]{2,1,0:T(8,128)S(1)}, u32[]{:S(2)}, u32[]{:S(2)}) collective-permute-start(f32[32,8,128]{2,1,0:T(8,128)S(1)} %get-tuple-element.28), channel_id=1, source_target_pairs={{0,64},{64,128},{128,192},{192,256},{256,320},{320,384},{384,448},... | collective-permute-start | bytes 393224 | tf_op jit(solution)/shard_map/ppermute | solution.py:621
  39.2 14.5 %collective-permute-start.5 = (f32[536,128]{1,0:T(8,128)S(1)}, f32[536,128]{1,0:T(8,128)S(1)}, u32[]{:S(2)}, u32[]{:S(2)}) collective-permute-start(f32[536,128]{1,0:T(8,128)S(1)} %get-tuple-element.31), channel_id=1, source_target_pairs={{0,56},{8,0},{16,8},{24,16},{32,24},{40,32},{48,40},{56,48},{1,57}... | collective-permute-start | bytes 823304 | tf_op jit(solution)/shard_map/ppermute | solution.py:618
  48.1 3.4 %collective-permute-start.4 = (f32[304,128]{1,0:T(8,128)S(1)}, f32[304,128]{1,0:T(8,128)S(1)}, u32[]{:S(2)}, u32[]{:S(2)}) collective-permute-start(f32[304,128]{1,0:T(8,128)S(1)} %get-tuple-element.30), channel_id=1, source_target_pairs={{0,8},{8,16},{16,24},{24,32},{32,40},{40,48},{48,56},{56,0},{1,9},... | collective-permute-start | bytes 466952 | tf_op jit(solution)/shard_map/ppermute | solution.py:618
  57.3 8.1 %collective-permute-start.7 = (f32[160,128]{1,0:T(8,128)S(1)}, f32[160,128]{1,0:T(8,128)S(1)}, u32[]{:S(2)}, u32[]{:S(2)}) collective-permute-start(f32[160,128]{1,0:T(8,128)S(1)} %get-tuple-element.41), channel_id=1, source_target_pairs={{64,0},{128,64},{192,128},{256,192},{320,256},{384,320},{448,384},... | collective-permute-start | bytes 245768 | tf_op jit(solution)/shard_map/ppermute | solution.py:624
  59.3 6.2 %collective-permute-start.6 = (f32[120,128]{1,0:T(8,128)S(1)}, f32[120,128]{1,0:T(8,128)S(1)}, u32[]{:S(2)}, u32[]{:S(2)}) collective-permute-start(f32[120,128]{1,0:T(8,128)S(1)} %get-tuple-element.40), channel_id=1, source_target_pairs={{0,64},{64,128},{128,192},{192,256},{256,320},{320,384},{384,448},... | collective-permute-start | bytes 184328 | tf_op jit(solution)/shard_map/ppermute | solution.py:621
  65.5 5.6 %collective-permute-start.9 = (f32[408,128]{1,0:T(8,128)S(1)}, f32[408,128]{1,0:T(8,128)S(1)}, u32[]{:S(2)}, u32[]{:S(2)}) collective-permute-start(f32[408,128]{1,0:T(8,128)S(1)} %get-tuple-element.44), channel_id=1, source_target_pairs={{0,56},{8,0},{16,8},{24,16},{32,24},{40,32},{48,40},{56,48},{1,57}... | collective-permute-start | bytes 626696 | tf_op jit(solution)/shard_map/ppermute | solution.py:618
  67.1 2.4 %collective-permute-start.8 = (f32[296,128]{1,0:T(8,128)S(1)}, f32[296,128]{1,0:T(8,128)S(1)}, u32[]{:S(2)}, u32[]{:S(2)}) collective-permute-start(f32[296,128]{1,0:T(8,128)S(1)} %get-tuple-element.43), channel_id=1, source_target_pairs={{0,8},{8,16},{16,24},{24,32},{32,40},{40,48},{48,56},{56,0},{1,9},... | collective-permute-start | bytes 454664 | tf_op jit(solution)/shard_map/ppermute | solution.py:618

commit v5 on v4

--- a/solution.py
+++ b/solution.py
@@ -14,14 +14,13 @@
 ROWS, LANES = 16, 256
 ML = 14
 VMEM = pl.BlockSpec(memory_space=pltpu.VMEM)
-SMEM = pl.BlockSpec(memory_space=pltpu.SMEM)
 HBM = pl.BlockSpec(memory_space=pltpu.HBM)
 UNROLL = True
 PARAMS = pltpu.CompilerParams(vmem_limit_bytes=20 * 1024 * 1024)
 
 
 def call(kernel, outs, scratch, *args, space=VMEM):
-    specs = [SMEM if a.dtype == jnp.int32 else space for a in args]
+    specs = [VMEM if a.dtype == jnp.int32 else space for a in args]
     return pl.pallas_call(
         kernel,
         out_shape=[jax.ShapeDtypeStruct(s, F32) for s in outs],
@@ -106,7 +105,7 @@
     for copy in copies:
         copy.start()
     lane = iota((BY, BZ), 1) // 16
-    odd = jnp.full((BY, BZ), place[3], jnp.int32) == 1
+    odd = place[3] == 1
     for copy, (_, at, count) in zip(copies, parts):
         copy.wait()
         for f in range(at, at + count):
@@ -122,7 +121,7 @@
 
 
 def strips(place, first, second, f):
-    odd = jnp.full((BY, BZ), place[3], jnp.int32) == 1
+    odd = place[3] == 1
     a, b = first[f], second[f]
     return jnp.where(odd, b, a), jnp.where(odd, a, b)
 
@@ -165,19 +164,23 @@
             to_down[at : at + above] = tile[:above, :]
 
 
+def widen(tile, rows, lanes):
+    tile = jnp.concatenate([tile] * (rows // BY), axis=0) if rows > BY else tile
+    return jnp.concatenate([tile] * (lanes // BZ), axis=1) if lanes > BZ else tile
+
+
 def inside_yz(place, rows, lanes, ny, nz, end_y, low_y, end_z, low_z, by, bz):
     y = iota((rows, lanes), 0)
     z = iota((rows, lanes), 1)
     held = ((y < end_y) | (y >= rows - low_y)) & ((z < end_z) | (z >= lanes - low_z))
-    y = jnp.where(y < end_y, y, y - rows) + place[1] * by
-    z = jnp.where(z < end_z, z, z - lanes) + place[2] * bz
-    good = held & (y >= 0) & (y < ny) & (z >= 0) & (z < nz)
-    return jnp.where(good, 1, 0)
+    y = jnp.where(y < end_y, y, y - rows) + widen(place[1] * by, rows, lanes)
+    z = jnp.where(z < end_z, z, z - lanes) + widen(place[2] * bz, rows, lanes)
+    return jnp.where(held & (y >= 0) & (y < ny) & (z >= 0) & (z < nz), 1, 0)
 
 
 def inside(yz, x, nx):
     ok = jnp.where((x >= 0) & (x < nx), 1, 0)
-    return (yz * ok) != 0
+    return (yz * widen(ok, *yz.shape)) != 0
 
 
 def neighbours(low, mid, high, by=1):
@@ -219,8 +222,8 @@
 
 
 def kept(place, sizes):
-    low = jnp.where(place[1] > 0, 1.0, 0.0).astype(F32)
-    high = jnp.where(place[1] < sizes[1] // BY - 1, 1.0, 0.0).astype(F32)
+    low = jnp.where(place[1] > 0, 1.0, 0.0)
+    high = jnp.where(place[1] < sizes[1] // BY - 1, 1.0, 0.0)
     return low, high
 
 
@@ -261,9 +264,9 @@
         for l in FINE_LAYERS[f]:
             rows[f, l] = jnp.zeros((BY, BZ), F32)
             at = Y_DOWN[f, l]
-            rows[f, l, 0:above] = y_high[at : at + above] * keep_high
+            rows[f, l, 0:above] = y_high[at : at + above] * keep_high[:above]
             at = Y_UP[f, l]
-            rows[f, l, BY - below :] = y_low[at : at + below] * keep_low
+            rows[f, l, BY - below :] = y_low[at : at + below] * keep_low[:below]
         sides = [rows[f, NL + i] for i in range(4)]
         for l in range(NL):
             whole[f, l, 0:BY] = half[f, l]
@@ -421,9 +424,9 @@
             mid[f, l, 0:4] = own[f, l]
             if l in MID_LAYERS[f]:
                 at = MY_DOWN[f, l]
-                mid[f, l, 4 : 4 + above] = y_high[at : at + above] * keep_high
+                mid[f, l, 4 : 4 + above] = y_high[at : at + above] * keep_high[:above]
                 at = MY_UP[f, l]
-                mid[f, l, ROWS - below :] = y_low[at : at + below] * keep_low
+                mid[f, l, ROWS - below :] = y_low[at : at + below] * keep_low[:below]
 
     shape = (ROWS, BZ)
     yz = inside_yz(place, ROWS, BZ, sizes[1] // 2, sizes[2] // 2, 10, 4, BZ // 2 + 8, 8, BY // 2, BZ // 2)
@@ -606,7 +609,7 @@
 def per_device(sizes, iterate, forcing, viscosity):
     nx, ny, nz = (lax.axis_size(a) for a in ("gx", "gy", "gz"))
     at = [lax.axis_index(a) for a in ("gx", "gy", "gz")]
-    place = jnp.stack(at + [at[2] % 2]).astype(jnp.int32)
+    place = jnp.stack([jnp.full((BY, BZ), a, jnp.int32) for a in at + [at[2] % 2]])
 
     def swap(a, axis, count, start):
         pairs = []

time: 75.3 us -> 72.7 us (0.965)
  Pallas kernels: 11.5 us -> 7.66 us
  waiting for transfers between devices: 33.2 us -> 34.3 us
    pallas_call x8, Pallas kernels: 11.5 us -> 7.66 us  [call(): pl.pallas_call(kernel, out_shape=[jax.ShapeDtypeStruct(s, F32) for s in o...]
    ppermute x4, waiting for transfers between devices: 6.33 us -> 7.41 us  [around(): return lax.ppermute(a, axis, [(i, (i + by) % count) for i in range(count)])]
  transfers between devices with their start and end apart: 10 -> 10, of which waited for: 7 -> 7; matrix products, arithmetic and copies ran while one was open for 0% -> 0% of each run, Pallas kernels for 3% -> 1%
where the time goes in v5:
time: 72.7 us; the launch traced here: 71.3 us
  waiting for transfers between devices  34.3 us (47%)
  starting transfers between devices  29.1 us (40%)
  Pallas kernels  7.66 us (11%)
    ppermute x2, waiting for transfers between devices, swap(): return lax.ppermute(a, axis, pairs)  19.1 us
    ppermute x4, starting transfers between devices, around(): return lax.ppermute(a, axis, [(i, (i + by) % count) for i in range(count)])  11.9 us
    ppermute x2, waiting for transfers between devices, to_next(): return lax.ppermute(a, axis, [(i, i + 1) for i in range(count - 1)])  7.8 us
    pallas_call x8, Pallas kernels, call(): pl.pallas_call(kernel, out_shape=[jax.ShapeDtypeStruct(s, F32) for s in o...  7.66 us
    ppermute x4, waiting for transfers between devices, around(): return lax.ppermute(a, axis, [(i, (i + by) % count) for i in range(count)])  7.41 us
    ppermute x2, starting transfers between devices, swap(): return lax.ppermute(a, axis, pairs)  6.24 us
    ppermute x2, starting transfers between devices, to_previous(): return lax.ppermute(a, axis, [(i + 1, i) for i in range(count - 1)])  5.7 us
    ppermute x2, starting transfers between devices, to_next(): return lax.ppermute(a, axis, [(i, i + 1) for i in range(count - 1)])  5.28 us
  transfers between devices with their start and end apart: 10, of which 7 were waited for; matrix products, arithmetic and copies ran while one was open for 0% of the time, Pallas kernels for 1%

profile of v5, /device:TPU:641, one launch (start us, length us, event | category | flops | bytes accessed | tf_op | source)
XLA Modules:
  0.0 71.3 jit_solution(10230838456808044348)
XLA Ops:
  0.2 1.3 %shard_map.37 = (f32[11,8,8,128]{3,2,1,0:T(8,128)S(1)}, f32[11,8,128]{2,1,0:T(8,128)S(1)}, f32[11,8,128]{2,1,0:T(8,128)S(1)}) custom-call(s32[4,8,128]{2,1,0:T(8,128)S(1)} %broadcast.7.place, f32[4,8,8,128]{3,2,1,0:T(8,128)} %iterate.1, f32[4,8,8,128]{3,2,1,0:T(8,128)} %forcing.1, f32[3,8,8,128]{3,2,1,0:T(8,128)} %viscosity.1), custom_call_target="tpu_custom_call" | custom-call | tf_op jit(solution)/shard_map/pallas_call | solution.py:24
  1.5 1.9 %collective-permute-start = (f32[11,8,128]{2,1,0:T(8,128)S(1)}, f32[11,8,128]{2,1,0:T(8,128)S(1)}, u32[]{:S(2)}, u32[]{:S(2)}) collective-permute-start(f32[11,8,128]{2,1,0:T(8,128)S(1)} %get-tuple-element.26), channel_id=1, source_target_pairs={{1,2},{2,1},{3,4},{4,3},{5,6},{6,5},{9,10},{10,9},{11,12},{12,11},... | collective-permute-start | bytes 135176 | tf_op jit(solution)/shard_map/ppermute | solution.py:618
  3.4 4.3 %collective-permute-start.1 = (f32[11,8,128]{2,1,0:T(8,128)S(1)}, f32[11,8,128]{2,1,0:T(8,128)S(1)}, u32[]{:S(2)}, u32[]{:S(2)}) collective-permute-start(f32[11,8,128]{2,1,0:T(8,128)S(1)} %get-tuple-element.27), channel_id=1, source_target_pairs={{0,1},{1,0},{2,3},{3,2},{4,5},{5,4},{6,7},{7,6},{8,9},{9,8},{10,11... | collective-permute-start | bytes 135176 | tf_op jit(solution)/shard_map/ppermute | solution.py:618
  7.7 19.1 %collective-permute-done.first = f32[11,8,128]{2,1,0:T(8,128)S(1)} collective-permute-done((f32[11,8,128]{2,1,0:T(8,128)S(1)}, f32[11,8,128]{2,1,0:T(8,128)S(1)}, u32[]{:S(2)}, u32[]{:S(2)}) %collective-permute-start) | collective-permute-done | bytes 45088 | tf_op jit(solution)/shard_map/ppermute | solution.py:618
  26.8 0.1 shard_map.38
  26.9 3.8 %collective-permute-start.3 = (f32[48,8,128]{2,1,0:T(8,128)S(1)}, f32[48,8,128]{2,1,0:T(8,128)S(1)}, u32[]{:S(2)}, u32[]{:S(2)}) collective-permute-start(f32[48,8,128]{2,1,0:T(8,128)S(1)} %get-tuple-element.29), channel_id=1, source_target_pairs={{64,0},{128,64},{192,128},{256,192},{320,256},{384,320},{448,384},... | collective-permute-start | bytes 589832 | tf_op jit(solution)/shard_map/ppermute | solution.py:627
  30.7 1.9 %collective-permute-start.2 = (f32[32,8,128]{2,1,0:T(8,128)S(1)}, f32[32,8,128]{2,1,0:T(8,128)S(1)}, u32[]{:S(2)}, u32[]{:S(2)}) collective-permute-start(f32[32,8,128]{2,1,0:T(8,128)S(1)} %get-tuple-element.28), channel_id=1, source_target_pairs={{0,64},{64,128},{128,192},{192,256},{256,320},{320,384},{384,448},... | collective-permute-start | bytes 393224 | tf_op jit(solution)/shard_map/ppermute | solution.py:624
  32.6 5.0 %collective-permute-done.2.from_low = f32[32,8,128]{2,1,0:T(8,128)S(1)} collective-permute-done((f32[32,8,128]{2,1,0:T(8,128)S(1)}, f32[32,8,128]{2,1,0:T(8,128)S(1)}, u32[]{:S(2)}, u32[]{:S(2)}) %collective-permute-start.2) | collective-permute-done | bytes 131104 | tf_op jit(solution)/shard_map/ppermute | solution.py:624
  37.6 0.1 shard_map.40
  37.7 8.8 %collective-permute-start.5 = (f32[536,128]{1,0:T(8,128)S(1)}, f32[536,128]{1,0:T(8,128)S(1)}, u32[]{:S(2)}, u32[]{:S(2)}) collective-permute-start(f32[536,128]{1,0:T(8,128)S(1)} %get-tuple-element.31), channel_id=1, source_target_pairs={{0,56},{8,0},{16,8},{24,16},{32,24},{40,32},{48,40},{56,48},{1,57}... | collective-permute-start | bytes 823304 | tf_op jit(solution)/shard_map/ppermute | solution.py:621
  46.5 1.2 %collective-permute-start.4 = (f32[304,128]{1,0:T(8,128)S(1)}, f32[304,128]{1,0:T(8,128)S(1)}, u32[]{:S(2)}, u32[]{:S(2)}) collective-permute-start(f32[304,128]{1,0:T(8,128)S(1)} %get-tuple-element.30), channel_id=1, source_target_pairs={{0,8},{8,16},{16,24},{24,32},{32,40},{40,48},{48,56},{56,0},{1,9},... | collective-permute-start | bytes 466952 | tf_op jit(solution)/shard_map/ppermute | solution.py:621
  47.7 0.4 shard_map.39.half
  48.1 1.8 %collective-permute-done.4.y_low = f32[304,128]{1,0:T(8,128)S(1)} collective-permute-done((f32[304,128]{1,0:T(8,128)S(1)}, f32[304,128]{1,0:T(8,128)S(1)}, u32[]{:S(2)}, u32[]{:S(2)}) %collective-permute-start.4) | collective-permute-done | bytes 155680 | tf_op jit(solution)/shard_map/ppermute | solution.py:621
  49.9 2.3 %collective-permute-done.5.y_high = f32[536,128]{1,0:T(8,128)S(1)} collective-permute-done((f32[536,128]{1,0:T(8,128)S(1)}, f32[536,128]{1,0:T(8,128)S(1)}, u32[]{:S(2)}, u32[]{:S(2)}) %collective-permute-start.5) | collective-permute-done | bytes 274464 | tf_op jit(solution)/shard_map/ppermute | solution.py:621
  52.2 3.1 %shard_map.41 = (f32[11,14,16,256]{3,2,1,0:T(8,128)S(1)}, f32[4,14,16,256]{3,2,1,0:T(8,128)S(1)}, f32[7,4,8,128]{3,2,1,0:T(8,128)S(1)}, f32[160,128]{1,0:T(8,128)S(1)}, f32[120,128]{1,0:T(8,128)S(1)}) custom-call(s32[4,8,128]{2,1,0:T(8,128)S(1)} %broadcast.7.place, f32[11,14,8,256]{3,2,1,0:T(8,128)S(1)} %shard_map.39.half, ...), custom_call_target="tpu_custom_call" | custom-call | tf_op jit(solution)/shard_map/pallas_call | solution.py:24
  55.2 1.9 %collective-permute-start.7 = (f32[160,128]{1,0:T(8,128)S(1)}, f32[160,128]{1,0:T(8,128)S(1)}, u32[]{:S(2)}, u32[]{:S(2)}) collective-permute-start(f32[160,128]{1,0:T(8,128)S(1)} %get-tuple-element.41), channel_id=1, source_target_pairs={{64,0},{128,64},{192,128},{256,192},{320,256},{384,320},{448,384},... | collective-permute-start | bytes 245768 | tf_op jit(solution)/shard_map/ppermute | solution.py:627
  57.2 3.4 %collective-permute-start.6 = (f32[120,128]{1,0:T(8,128)S(1)}, f32[120,128]{1,0:T(8,128)S(1)}, u32[]{:S(2)}, u32[]{:S(2)}) collective-permute-start(f32[120,128]{1,0:T(8,128)S(1)} %get-tuple-element.40), channel_id=1, source_target_pairs={{0,64},{64,128},{128,192},{192,256},{256,320},{320,384},{384,448},... | collective-permute-start | bytes 184328 | tf_op jit(solution)/shard_map/ppermute | solution.py:624
  60.5 2.8 %collective-permute-done.6.from_low = f32[120,128]{1,0:T(8,128)S(1)} collective-permute-done((f32[120,128]{1,0:T(8,128)S(1)}, f32[120,128]{1,0:T(8,128)S(1)}, u32[]{:S(2)}, u32[]{:S(2)}) %collective-permute-start.6) | collective-permute-done | bytes 61472 | tf_op jit(solution)/shard_map/ppermute | solution.py:624
  63.4 1.6 %collective-permute-start.9 = (f32[408,128]{1,0:T(8,128)S(1)}, f32[408,128]{1,0:T(8,128)S(1)}, u32[]{:S(2)}, u32[]{:S(2)}) collective-permute-start(f32[408,128]{1,0:T(8,128)S(1)} %get-tuple-element.44), channel_id=1, source_target_pairs={{0,56},{8,0},{16,8},{24,16},{32,24},{40,32},{48,40},{56,48},{1,57}... | collective-permute-start | bytes 626696 | tf_op jit(solution)/shard_map/ppermute | solution.py:621
  65.0 0.3 collective-permute-start.8
  65.3 0.4 shard_map.42
  65.7 1.7 %collective-permute-done.8.y_low = f32[296,128]{1,0:T(8,128)S(1)} collective-permute-done((f32[296,128]{1,0:T(8,128)S(1)}, f32[296,128]{1,0:T(8,128)S(1)}, u32[]{:S(2)}, u32[]{:S(2)}) %collective-permute-start.8) | collective-permute-done | bytes 151584 | tf_op jit(solution)/shard_map/ppermute | solution.py:621
  67.4 1.6 %collective-permute-done.9.y_high = f32[408,128]{1,0:T(8,128)S(1)} collective-permute-done((f32[408,128]{1,0:T(8,128)S(1)}, f32[408,128]{1,0:T(8,128)S(1)}, u32[]{:S(2)}, u32[]{:S(2)}) %collective-permute-start.9) | collective-permute-done | bytes 208928 | tf_op jit(solution)/shard_map/ppermute | solution.py:621
  69.0 2.2 %shard_map.44 = f32[4,8,8,128]{3,2,1,0:T(8,128)} custom-call(s32[4,8,128]{2,1,0:T(8,128)S(1)} %broadcast.7.place, f32[3,6,9,16,256]{4,3,2,1,0:T(8,128)S(1)} %get-tuple-element.34.last_sums, f32[3,9,16,256]{3,2,1,0:T(8,128)S(1)} %get-tuple-element.35.base, f32[3,9,16,256]{3,2,1,0:T(8,128)S(1)} %get-tuple-element.36.inv, ...), custom_call_target="tpu_custom_call" | custom-call | tf_op jit(solution)/shard_map/pallas_call | solution.py:24
  (6 shorter events, 0.2 us)
Async XLA Ops:
  1.5 25.3 %collective-permute-start = (f32[11,8,128]{2,1,0:T(8,128)S(1)}, f32[11,8,128]{2,1,0:T(8,128)S(1)}, u32[]{:S(2)}, u32[]{:S(2)}) collective-permute-start(f32[11,8,128]{2,1,0:T(8,128)S(1)} %get-tuple-element.26), channel_id=1, source_target_pairs={{1,2},{2,1},{3,4},{4,3},{5,6},{6,5},{9,10},{10,9},{11,12},{12,11},... | collective-permute-start | bytes 135176 | tf_op jit(solution)/shard_map/ppermute | solution.py:618
  3.4 23.4 %collective-permute-start.1 = (f32[11,8,128]{2,1,0:T(8,128)S(1)}, f32[11,8,128]{2,1,0:T(8,128)S(1)}, u32[]{:S(2)}, u32[]{:S(2)}) collective-permute-start(f32[11,8,128]{2,1,0:T(8,128)S(1)} %get-tuple-element.27), channel_id=1, source_target_pairs={{0,1},{1,0},{2,3},{3,2},{4,5},{5,4},{6,7},{7,6},{8,9},{9,8},{10,11... | collective-permute-start | bytes 135176 | tf_op jit(solution)/shard_map/ppermute | solution.py:618
  26.9 10.7 %collective-permute-start.3 = (f32[48,8,128]{2,1,0:T(8,128)S(1)}, f32[48,8,128]{2,1,0:T(8,128)S(1)}, u32[]{:S(2)}, u32[]{:S(2)}) collective-permute-start(f32[48,8,128]{2,1,0:T(8,128)S(1)} %get-tuple-element.29), channel_id=1, source_target_pairs={{64,0},{128,64},{192,128},{256,192},{320,256},{384,320},{448,384},... | collective-permute-start | bytes 589832 | tf_op jit(solution)/shard_map/ppermute | solution.py:627
  30.7 6.9 %collective-permute-start.2 = (f32[32,8,128]{2,1,0:T(8,128)S(1)}, f32[32,8,128]{2,1,0:T(8,128)S(1)}, u32[]{:S(2)}, u32[]{:S(2)}) collective-permute-start(f32[32,8,128]{2,1,0:T(8,128)S(1)} %get-tuple-element.28), channel_id=1, source_target_pairs={{0,64},{64,128},{128,192},{192,256},{256,320},{320,384},{384,448},... | collective-permute-start | bytes 393224 | tf_op jit(solution)/shard_map/ppermute | solution.py:624
  37.7 14.5 %collective-permute-start.5 = (f32[536,128]{1,0:T(8,128)S(1)}, f32[536,128]{1,0:T(8,128)S(1)}, u32[]{:S(2)}, u32[]{:S(2)}) collective-permute-start(f32[536,128]{1,0:T(8,128)S(1)} %get-tuple-element.31), channel_id=1, source_target_pairs={{0,56},{8,0},{16,8},{24,16},{32,24},{40,32},{48,40},{56,48},{1,57}... | collective-permute-start | bytes 823304 | tf_op jit(solution)/shard_map/ppermute | solution.py:621
  46.5 3.4 %collective-permute-start.4 = (f32[304,128]{1,0:T(8,128)S(1)}, f32[304,128]{1,0:T(8,128)S(1)}, u32[]{:S(2)}, u32[]{:S(2)}) collective-permute-start(f32[304,128]{1,0:T(8,128)S(1)} %get-tuple-element.30), channel_id=1, source_target_pairs={{0,8},{8,16},{16,24},{24,32},{32,40},{40,48},{48,56},{56,0},{1,9},... | collective-permute-start | bytes 466952 | tf_op jit(solution)/shard_map/ppermute | solution.py:621
  55.2 8.1 %collective-permute-start.7 = (f32[160,128]{1,0:T(8,128)S(1)}, f32[160,128]{1,0:T(8,128)S(1)}, u32[]{:S(2)}, u32[]{:S(2)}) collective-permute-start(f32[160,128]{1,0:T(8,128)S(1)} %get-tuple-element.41), channel_id=1, source_target_pairs={{64,0},{128,64},{192,128},{256,192},{320,256},{384,320},{448,384},... | collective-permute-start | bytes 245768 | tf_op jit(solution)/shard_map/ppermute | solution.py:627
  57.2 6.2 %collective-permute-start.6 = (f32[120,128]{1,0:T(8,128)S(1)}, f32[120,128]{1,0:T(8,128)S(1)}, u32[]{:S(2)}, u32[]{:S(2)}) collective-permute-start(f32[120,128]{1,0:T(8,128)S(1)} %get-tuple-element.40), channel_id=1, source_target_pairs={{0,64},{64,128},{128,192},{192,256},{256,320},{320,384},{384,448},... | collective-permute-start | bytes 184328 | tf_op jit(solution)/shard_map/ppermute | solution.py:624
  63.4 5.6 %collective-permute-start.9 = (f32[408,128]{1,0:T(8,128)S(1)}, f32[408,128]{1,0:T(8,128)S(1)}, u32[]{:S(2)}, u32[]{:S(2)}) collective-permute-start(f32[408,128]{1,0:T(8,128)S(1)} %get-tuple-element.44), channel_id=1, source_target_pairs={{0,56},{8,0},{16,8},{24,16},{32,24},{40,32},{48,40},{56,48},{1,57}... | collective-permute-start | bytes 626696 | tf_op jit(solution)/shard_map/ppermute | solution.py:621
  65.0 2.4 %collective-permute-start.8 = (f32[296,128]{1,0:T(8,128)S(1)}, f32[296,128]{1,0:T(8,128)S(1)}, u32[]{:S(2)}, u32[]{:S(2)}) collective-permute-start(f32[296,128]{1,0:T(8,128)S(1)} %get-tuple-element.43), channel_id=1, source_target_pairs={{0,8},{8,16},{16,24},{24,32},{32,40},{40,48},{48,56},{56,0},{1,9},... | collective-permute-start | bytes 454664 | tf_op jit(solution)/shard_map/ppermute | solution.py:621

commit v6 on v5

--- a/solution.py
+++ b/solution.py
@@ -69,21 +69,22 @@
     return (3, 4)[f // 4]
 
 
-def offsets(entries):
+def offsets(entries, unit=8):
     table, at = {}, 0
     for key, rows in entries:
         table[key] = at
         at += rows
-    return table, -(-at // 8) * 8
+    return table, -(-at // unit) * unit
 
 
 FINE, MID = range(11), range(7)
-X_UP, X_UP_TILES = offsets(
-    [((f, x), 1) for f in FINE for x in range(BX - fine_below(f), BX)] + [((f, "z"), 1) for f in FINE]
-)
-X_DOWN, X_DOWN_TILES = offsets(
-    [((f, x), 1) for f in FINE for x in range(fine_above(f, 0))] + [((f, "z"), 1) for f in FINE]
-)
+X_UP = [(f, x) for f in FINE for x in range(BX - fine_below(f), BX)]
+X_DOWN = [(f, x) for f in FINE for x in range(fine_above(f, 0))]
+EARLY_UP, EARLY_DOWN = 18, 24
+X_UP_EARLY, X_UP_EARLY_TILES = offsets([(key, 1) for key in X_UP[:EARLY_UP]], 8)
+X_DOWN_EARLY, X_DOWN_EARLY_TILES = offsets([(key, 1) for key in X_DOWN[:EARLY_DOWN]], 1)
+X_UP_LATE, X_UP_LATE_TILES = offsets([((f, "z"), 1) for f in FINE] + [(key, 1) for key in X_UP[EARLY_UP:]], 1)
+X_DOWN_LATE, X_DOWN_LATE_TILES = offsets([((f, "z"), 1) for f in FINE] + [(key, 1) for key in X_DOWN[EARLY_DOWN:]], 1)
 FINE_LAYERS = {
     f: [x + XL for x in range(-fine_below(f), BX + fine_above(f, 0))] + list(range(NL, NL + 4)) for f in FINE
 }
@@ -126,38 +127,54 @@
     return jnp.where(odd, b, a), jnp.where(odd, a, b)
 
 
-def pack_x(place, own, first, second, to_up, to_down):
+def fill(message, table, own):
+    for key, at in table.items():
+        if key[1] != "z":
+            message[at] = own[key]
+    for at in range(len(table), message.shape[0]):
+        message[at] = jnp.zeros((BY, BZ), F32)
+
+
+def pack_x_early(own, to_up, to_down):
+    fill(to_up, X_UP_EARLY, own)
+    fill(to_down, X_DOWN_EARLY, own)
+
+
+def pack_x_late(place, own, first, second, to_up, to_down):
     lane = iota((BY, BZ), 1)
     for f in FINE:
         low, high = strips(place, first, second, f)
-        to_up[X_UP[f, "z"]] = jnp.where(lane >= 96, low, lane_roll(high, -32))
-        to_down[X_DOWN[f, "z"]] = jnp.where(lane < 64, low, lane_roll(high, 64))
-        for x in range(BX - fine_below(f), BX):
-            to_up[X_UP[f, x]] = own[f, x]
-        for x in range(fine_above(f, 0)):
-            to_down[X_DOWN[f, x]] = own[f, x]
-
-
-def fine_tile(own, from_low, from_high, f, l):
+        to_up[X_UP_LATE[f, "z"]] = jnp.where(lane >= 96, low, lane_roll(high, -32))
+        to_down[X_DOWN_LATE[f, "z"]] = jnp.where(lane < 64, low, lane_roll(high, 64))
+    fill(to_up, X_UP_LATE, own)
+    fill(to_down, X_DOWN_LATE, own)
+
+
+def fine_tile(own, halos, f, l):
     x = l - XL
     if 0 <= x < BX:
         return own[f, x]
-    if x < 0:
-        return from_low[X_UP[f, BX + x]] if -x <= fine_below(f) else None
-    return from_high[X_DOWN[f, x - BX]] if x - BX < fine_above(f, 0) else None
-
-
-def strip_tiles(place, first, second, from_low, from_high, f):
+    low_early, high_early, low_late, high_late = halos
+    key = (f, BX + x) if x < 0 else (f, x - BX)
+    early, late = (low_early, low_late) if x < 0 else (high_early, high_late)
+    table, rest = (X_UP_EARLY, X_UP_LATE) if x < 0 else (X_DOWN_EARLY, X_DOWN_LATE)
+    if key in table:
+        return early[table[key]]
+    return late[rest[key]] if key in rest else None
+
+
+def strip_tiles(place, first, second, halos, f):
     low, high = strips(place, first, second, f)
-    return [low, high, from_low[X_UP[f, "z"]], from_high[X_DOWN[f, "z"]]]
-
-
-def pack_y(place, own, first, second, from_low, from_high, to_up, to_down):
+    return [low, high, halos[2][X_UP_LATE[f, "z"]], halos[3][X_DOWN_LATE[f, "z"]]]
+
+
+def pack_y(place, own, first, second, low_early, high_early, low_late, high_late, to_up, to_down):
+    halos = (low_early, high_early, low_late, high_late)
     for f in FINE:
-        sides = strip_tiles(place, first, second, from_low, from_high, f)
+        sides = strip_tiles(place, first, second, halos, f)
         below, above = fine_below(f), fine_above(f, 1)
         for l in FINE_LAYERS[f]:
-            tile = sides[l - NL] if l >= NL else fine_tile(own, from_low, from_high, f, l)
+            tile = sides[l - NL] if l >= NL else fine_tile(own, halos, f, l)
             at = Y_UP[f, l]
             to_up[at : at + below] = tile[BY - below :, :]
             at = Y_DOWN[f, l]
@@ -239,11 +256,12 @@
     return jnp.where(lane >= 112, a, jnp.where(lane < 16, b, 0.0))
 
 
-def assemble_own(place, own, first, second, from_low, from_high, half):
+def assemble_own(place, own, first, second, low_early, high_early, low_late, high_late, half):
+    halos = (low_early, high_early, low_late, high_late)
     for f in FINE:
-        sides = strip_tiles(place, first, second, from_low, from_high, f)
+        sides = strip_tiles(place, first, second, halos, f)
         for l in range(NL):
-            body = fine_tile(own, from_low, from_high, f, l)
+            body = fine_tile(own, halos, f, l)
             half[f, l, :, 0:BZ] = jnp.zeros((BY, BZ), F32) if body is None else body
             half[f, l, :, BZ:] = side_lanes(l, sides)
 
@@ -637,16 +655,21 @@
     first = swap(first, "gz", nz, 1)
     second = swap(second, "gz", nz, 0)
 
-    upward, downward = call(pack_x, [(X_UP_TILES,) + tile, (X_DOWN_TILES,) + tile], [], place, own, first, second)
-    x_low = to_next(upward, "gx", nx)
-    x_high = to_previous(downward, "gx", nx)
-
     upward, downward = call(
-        pack_y, [(Y_UP_ROWS, BZ), (Y_DOWN_ROWS, BZ)], [], place, own, first, second, x_low, x_high
+        pack_x_early, [(X_UP_EARLY_TILES,) + tile, (X_DOWN_EARLY_TILES,) + tile], [], own
+    )
+    early = (to_next(upward, "gx", nx), to_previous(downward, "gx", nx))
+    upward, downward = call(
+        pack_x_late, [(X_UP_LATE_TILES,) + tile, (X_DOWN_LATE_TILES,) + tile], [], place, own, first, second
+    )
+    halos = (*early, to_next(upward, "gx", nx), to_previous(downward, "gx", nx))
+
+    upward, downward = call(
+        pack_y, [(Y_UP_ROWS, BZ), (Y_DOWN_ROWS, BZ)], [], place, own, first, second, *halos
     )
     y_low = around(upward, "gy", ny, 1)
     y_high = around(downward, "gy", ny, -1)
-    (half,) = call(assemble_own, [HALF], [], place, own, first, second, x_low, x_high)
+    (half,) = call(assemble_own, [HALF], [], place, own, first, second, *halos)
 
     whole, fine, middle, downward, upward = call(
         functools.partial(fine_level, sizes), FINE_OUT, FINE_SCRATCH, place, half, y_low, y_high

time: 72.7 us -> 73 us (level)
  the two profiles are of different devices: /device:TPU:641 before, /device:TPU:132 now
where the time goes in v6:
time: 73 us; the launch traced here: 72.6 us
  starting transfers between devices  47 us (64%)
  waiting for transfers between devices  17.7 us (24%)
  Pallas kernels  7.66 us (10%)
    ppermute x2, starting transfers between devices, swap(): return lax.ppermute(a, axis, pairs)  27.2 us
    ppermute x4, waiting for transfers between devices, around(): return lax.ppermute(a, axis, [(i, (i + by) % count) for i in range(count)])  10.1 us
    ppermute x3, starting transfers between devices, to_next(): return lax.ppermute(a, axis, [(i, i + 1) for i in range(count - 1)])  9.78 us
    ppermute x3, starting transfers between devices, to_previous(): return lax.ppermute(a, axis, [(i + 1, i) for i in range(count - 1)])  8.96 us
    pallas_call x9, Pallas kernels, call(): pl.pallas_call(kernel, out_shape=[jax.ShapeDtypeStruct(s, F32) for s in o...  7.66 us
    ppermute x3, waiting for transfers between devices, to_next(): return lax.ppermute(a, axis, [(i, i + 1) for i in range(count - 1)])  7.61 us
  transfers between devices with their start and end apart: 12, of which 4 were waited for; matrix products, arithmetic and copies ran while one was open for 0% of the time, Pallas kernels for 1%

profile of v6, /device:TPU:132, one launch (start us, length us, event | category | flops | bytes accessed | tf_op | source)
XLA Modules:
  0.0 72.6 jit_solution(2326699342040218285)
XLA Ops:
  0.0 0.1 add_add_fusion
  0.1 0.1 broadcast.7.place
  0.2 1.3 %shard_map.37 = (f32[11,8,8,128]{3,2,1,0:T(8,128)S(1)}, f32[11,8,128]{2,1,0:T(8,128)S(1)}, f32[11,8,128]{2,1,0:T(8,128)S(1)}) custom-call(s32[4,8,128]{2,1,0:T(8,128)S(1)} %broadcast.7.place, f32[4,8,8,128]{3,2,1,0:T(8,128)} %iterate.1, f32[4,8,8,128]{3,2,1,0:T(8,128)} %forcing.1, f32[3,8,8,128]{3,2,1,0:T(8,128)} %viscosity.1), custom_call_target="tpu_custom_call" | custom-call | tf_op jit(solution)/shard_map/pallas_call | solution.py:24
  1.5 2.4 %collective-permute-start = (f32[11,8,128]{2,1,0:T(8,128)S(1)}, f32[11,8,128]{2,1,0:T(8,128)S(1)}, u32[]{:S(2)}, u32[]{:S(2)}) collective-permute-start(f32[11,8,128]{2,1,0:T(8,128)S(1)} %get-tuple-element.28), channel_id=1, source_target_pairs={{1,2},{2,1},{3,4},{4,3},{5,6},{6,5},{9,10},{10,9},{11,12},{12,11},... | collective-permute-start | bytes 135176 | tf_op jit(solution)/shard_map/ppermute | solution.py:636
  3.9 24.7 %collective-permute-start.1 = (f32[11,8,128]{2,1,0:T(8,128)S(1)}, f32[11,8,128]{2,1,0:T(8,128)S(1)}, u32[]{:S(2)}, u32[]{:S(2)}) collective-permute-start(f32[11,8,128]{2,1,0:T(8,128)S(1)} %get-tuple-element.29), channel_id=1, source_target_pairs={{0,1},{1,0},{2,3},{3,2},{4,5},{5,4},{6,7},{7,6},{8,9},{9,8},{10,11... | collective-permute-start | bytes 135176 | tf_op jit(solution)/shard_map/ppermute | solution.py:636
  28.7 2.9 %collective-permute-start.2 = (f32[24,8,128]{2,1,0:T(8,128)S(1)}, f32[24,8,128]{2,1,0:T(8,128)S(1)}, u32[]{:S(2)}, u32[]{:S(2)}) collective-permute-start(f32[24,8,128]{2,1,0:T(8,128)S(1)} %get-tuple-element.30), channel_id=1, source_target_pairs={{0,64},{64,128},{128,192},{192,256},{256,320},{320,384},{384,448},... | collective-permute-start | bytes 294920 | tf_op jit(solution)/shard_map/ppermute | solution.py:642
  31.6 4.1 %collective-permute-start.3 = (f32[24,8,128]{2,1,0:T(8,128)S(1)}, f32[24,8,128]{2,1,0:T(8,128)S(1)}, u32[]{:S(2)}, u32[]{:S(2)}) collective-permute-start(f32[24,8,128]{2,1,0:T(8,128)S(1)} %get-tuple-element.31), channel_id=1, source_target_pairs={{64,0},{128,64},{192,128},{256,192},{320,256},{384,320},{448,384},... | collective-permute-start | bytes 294920 | tf_op jit(solution)/shard_map/ppermute | solution.py:645
  35.8 0.1 shard_map.39
  35.9 2.9 %collective-permute-start.5 = (f32[19,8,128]{2,1,0:T(8,128)S(1)}, f32[19,8,128]{2,1,0:T(8,128)S(1)}, u32[]{:S(2)}, u32[]{:S(2)}) collective-permute-start(f32[19,8,128]{2,1,0:T(8,128)S(1)} %get-tuple-element.33), channel_id=1, source_target_pairs={{64,0},{128,64},{192,128},{256,192},{320,256},{384,320},{448,384},... | collective-permute-start | bytes 233480 | tf_op jit(solution)/shard_map/ppermute | solution.py:645
  38.8 2.9 %collective-permute-start.4 = (f32[11,8,128]{2,1,0:T(8,128)S(1)}, f32[11,8,128]{2,1,0:T(8,128)S(1)}, u32[]{:S(2)}, u32[]{:S(2)}) collective-permute-start(f32[11,8,128]{2,1,0:T(8,128)S(1)} %get-tuple-element.32), channel_id=1, source_target_pairs={{0,64},{64,128},{128,192},{192,256},{256,320},{320,384},{384,448},... | collective-permute-start | bytes 135176 | tf_op jit(solution)/shard_map/ppermute | solution.py:642
  41.7 4.2 %collective-permute-done.4.low_late = f32[11,8,128]{2,1,0:T(8,128)S(1)} collective-permute-done((f32[11,8,128]{2,1,0:T(8,128)S(1)}, f32[11,8,128]{2,1,0:T(8,128)S(1)}, u32[]{:S(2)}, u32[]{:S(2)}) %collective-permute-start.4) | collective-permute-done | bytes 45088 | tf_op jit(solution)/shard_map/ppermute | solution.py:642
  46.0 0.1 shard_map.41
  46.1 0.5 collective-permute-start.6
  46.6 0.3 shard_map.40.half
  46.9 5.2 %collective-permute-done.6.y_low = f32[304,128]{1,0:T(8,128)S(1)} collective-permute-done((f32[304,128]{1,0:T(8,128)S(1)}, f32[304,128]{1,0:T(8,128)S(1)}, u32[]{:S(2)}, u32[]{:S(2)}) %collective-permute-start.6) | collective-permute-done | bytes 155680 | tf_op jit(solution)/shard_map/ppermute | solution.py:639
  52.1 3.1 %shard_map.42 = (f32[11,14,16,256]{3,2,1,0:T(8,128)S(1)}, f32[4,14,16,256]{3,2,1,0:T(8,128)S(1)}, f32[7,4,8,128]{3,2,1,0:T(8,128)S(1)}, f32[160,128]{1,0:T(8,128)S(1)}, f32[120,128]{1,0:T(8,128)S(1)}) custom-call(s32[4,8,128]{2,1,0:T(8,128)S(1)} %broadcast.7.place, f32[11,14,8,256]{3,2,1,0:T(8,128)S(1)} %shard_map.40.half, ...), custom_call_target="tpu_custom_call" | custom-call | tf_op jit(solution)/shard_map/pallas_call | solution.py:24
  55.2 1.9 %collective-permute-start.9 = (f32[160,128]{1,0:T(8,128)S(1)}, f32[160,128]{1,0:T(8,128)S(1)}, u32[]{:S(2)}, u32[]{:S(2)}) collective-permute-start(f32[160,128]{1,0:T(8,128)S(1)} %get-tuple-element.45), channel_id=1, source_target_pairs={{64,0},{128,64},{192,128},{256,192},{320,256},{384,320},{448,384},... | collective-permute-start | bytes 245768 | tf_op jit(solution)/shard_map/ppermute | solution.py:645
  57.1 3.9 %collective-permute-start.8 = (f32[120,128]{1,0:T(8,128)S(1)}, f32[120,128]{1,0:T(8,128)S(1)}, u32[]{:S(2)}, u32[]{:S(2)}) collective-permute-start(f32[120,128]{1,0:T(8,128)S(1)} %get-tuple-element.44), channel_id=1, source_target_pairs={{0,64},{64,128},{128,192},{192,256},{256,320},{320,384},{384,448},... | collective-permute-start | bytes 184328 | tf_op jit(solution)/shard_map/ppermute | solution.py:642
  61.0 3.4 %collective-permute-done.8.from_low = f32[120,128]{1,0:T(8,128)S(1)} collective-permute-done((f32[120,128]{1,0:T(8,128)S(1)}, f32[120,128]{1,0:T(8,128)S(1)}, u32[]{:S(2)}, u32[]{:S(2)}) %collective-permute-start.8) | collective-permute-done | bytes 61472 | tf_op jit(solution)/shard_map/ppermute | solution.py:642
  64.4 0.1 shard_map.44
  64.5 0.5 collective-permute-start.10
  65.0 0.4 shard_map.43
  65.5 4.9 %collective-permute-done.10.y_low = f32[296,128]{1,0:T(8,128)S(1)} collective-permute-done((f32[296,128]{1,0:T(8,128)S(1)}, f32[296,128]{1,0:T(8,128)S(1)}, u32[]{:S(2)}, u32[]{:S(2)}) %collective-permute-start.10) | collective-permute-done | bytes 151584 | tf_op jit(solution)/shard_map/ppermute | solution.py:639
  70.4 2.3 %shard_map.45 = f32[4,8,8,128]{3,2,1,0:T(8,128)} custom-call(s32[4,8,128]{2,1,0:T(8,128)S(1)} %broadcast.7.place, f32[3,6,9,16,256]{4,3,2,1,0:T(8,128)S(1)} %get-tuple-element.38.last_sums, f32[3,9,16,256]{3,2,1,0:T(8,128)S(1)} %get-tuple-element.39.base, f32[3,9,16,256]{3,2,1,0:T(8,128)S(1)} %get-tuple-element.40.inv, ...), custom_call_target="tpu_custom_call" | custom-call | tf_op jit(solution)/shard_map/pallas_call | solution.py:24
  (11 shorter events, 0.1 us)
Async XLA Ops:
  1.5 34.3 %collective-permute-start = (f32[11,8,128]{2,1,0:T(8,128)S(1)}, f32[11,8,128]{2,1,0:T(8,128)S(1)}, u32[]{:S(2)}, u32[]{:S(2)}) collective-permute-start(f32[11,8,128]{2,1,0:T(8,128)S(1)} %get-tuple-element.28), channel_id=1, source_target_pairs={{1,2},{2,1},{3,4},{4,3},{5,6},{6,5},{9,10},{10,9},{11,12},{12,11},... | collective-permute-start | bytes 135176 | tf_op jit(solution)/shard_map/ppermute | solution.py:636
  3.9 31.9 %collective-permute-start.1 = (f32[11,8,128]{2,1,0:T(8,128)S(1)}, f32[11,8,128]{2,1,0:T(8,128)S(1)}, u32[]{:S(2)}, u32[]{:S(2)}) collective-permute-start(f32[11,8,128]{2,1,0:T(8,128)S(1)} %get-tuple-element.29), channel_id=1, source_target_pairs={{0,1},{1,0},{2,3},{3,2},{4,5},{5,4},{6,7},{7,6},{8,9},{9,8},{10,11... | collective-permute-start | bytes 135176 | tf_op jit(solution)/shard_map/ppermute | solution.py:636
  28.7 17.3 %collective-permute-start.2 = (f32[24,8,128]{2,1,0:T(8,128)S(1)}, f32[24,8,128]{2,1,0:T(8,128)S(1)}, u32[]{:S(2)}, u32[]{:S(2)}) collective-permute-start(f32[24,8,128]{2,1,0:T(8,128)S(1)} %get-tuple-element.30), channel_id=1, source_target_pairs={{0,64},{64,128},{128,192},{192,256},{256,320},{320,384},{384,448},... | collective-permute-start | bytes 294920 | tf_op jit(solution)/shard_map/ppermute | solution.py:642
  31.6 14.3 %collective-permute-start.3 = (f32[24,8,128]{2,1,0:T(8,128)S(1)}, f32[24,8,128]{2,1,0:T(8,128)S(1)}, u32[]{:S(2)}, u32[]{:S(2)}) collective-permute-start(f32[24,8,128]{2,1,0:T(8,128)S(1)} %get-tuple-element.31), channel_id=1, source_target_pairs={{64,0},{128,64},{192,128},{256,192},{320,256},{384,320},{448,384},... | collective-permute-start | bytes 294920 | tf_op jit(solution)/shard_map/ppermute | solution.py:645
  35.9 10.1 %collective-permute-start.5 = (f32[19,8,128]{2,1,0:T(8,128)S(1)}, f32[19,8,128]{2,1,0:T(8,128)S(1)}, u32[]{:S(2)}, u32[]{:S(2)}) collective-permute-start(f32[19,8,128]{2,1,0:T(8,128)S(1)} %get-tuple-element.33), channel_id=1, source_target_pairs={{64,0},{128,64},{192,128},{256,192},{320,256},{384,320},{448,384},... | collective-permute-start | bytes 233480 | tf_op jit(solution)/shard_map/ppermute | solution.py:645
  38.8 7.2 %collective-permute-start.4 = (f32[11,8,128]{2,1,0:T(8,128)S(1)}, f32[11,8,128]{2,1,0:T(8,128)S(1)}, u32[]{:S(2)}, u32[]{:S(2)}) collective-permute-start(f32[11,8,128]{2,1,0:T(8,128)S(1)} %get-tuple-element.32), channel_id=1, source_target_pairs={{0,64},{64,128},{128,192},{192,256},{256,320},{320,384},{384,448},... | collective-permute-start | bytes 135176 | tf_op jit(solution)/shard_map/ppermute | solution.py:642
  46.1 6.1 %collective-permute-start.7 = (f32[536,128]{1,0:T(8,128)S(1)}, f32[536,128]{1,0:T(8,128)S(1)}, u32[]{:S(2)}, u32[]{:S(2)}) collective-permute-start(f32[536,128]{1,0:T(8,128)S(1)} %get-tuple-element.35), channel_id=1, source_target_pairs={{0,56},{8,0},{16,8},{24,16},{32,24},{40,32},{48,40},{56,48},{1,57}... | collective-permute-start | bytes 823304 | tf_op jit(solution)/shard_map/ppermute | solution.py:639
  46.1 6.0 %collective-permute-start.6 = (f32[304,128]{1,0:T(8,128)S(1)}, f32[304,128]{1,0:T(8,128)S(1)}, u32[]{:S(2)}, u32[]{:S(2)}) collective-permute-start(f32[304,128]{1,0:T(8,128)S(1)} %get-tuple-element.34), channel_id=1, source_target_pairs={{0,8},{8,16},{16,24},{24,32},{32,40},{40,48},{48,56},{56,0},{1,9},... | collective-permute-start | bytes 466952 | tf_op jit(solution)/shard_map/ppermute | solution.py:639
  55.2 9.3 %collective-permute-start.9 = (f32[160,128]{1,0:T(8,128)S(1)}, f32[160,128]{1,0:T(8,128)S(1)}, u32[]{:S(2)}, u32[]{:S(2)}) collective-permute-start(f32[160,128]{1,0:T(8,128)S(1)} %get-tuple-element.45), channel_id=1, source_target_pairs={{64,0},{128,64},{192,128},{256,192},{320,256},{384,320},{448,384},... | collective-permute-start | bytes 245768 | tf_op jit(solution)/shard_map/ppermute | solution.py:645
  57.1 7.3 %collective-permute-start.8 = (f32[120,128]{1,0:T(8,128)S(1)}, f32[120,128]{1,0:T(8,128)S(1)}, u32[]{:S(2)}, u32[]{:S(2)}) collective-permute-start(f32[120,128]{1,0:T(8,128)S(1)} %get-tuple-element.44), channel_id=1, source_target_pairs={{0,64},{64,128},{128,192},{192,256},{256,320},{320,384},{384,448},... | collective-permute-start | bytes 184328 | tf_op jit(solution)/shard_map/ppermute | solution.py:642
  64.5 5.9 %collective-permute-start.11 = (f32[408,128]{1,0:T(8,128)S(1)}, f32[408,128]{1,0:T(8,128)S(1)}, u32[]{:S(2)}, u32[]{:S(2)}) collective-permute-start(f32[408,128]{1,0:T(8,128)S(1)} %get-tuple-element.48), channel_id=1, source_target_pairs={{0,56},{8,0},{16,8},{24,16},{32,24},{40,32},{48,40},{56,48},{1,57}... | collective-permute-start | bytes 626696 | tf_op jit(solution)/shard_map/ppermute | solution.py:639
  64.5 5.8 %collective-permute-start.10 = (f32[296,128]{1,0:T(8,128)S(1)}, f32[296,128]{1,0:T(8,128)S(1)}, u32[]{:S(2)}, u32[]{:S(2)}) collective-permute-start(f32[296,128]{1,0:T(8,128)S(1)} %get-tuple-element.47), channel_id=1, source_target_pairs={{0,8},{8,16},{16,24},{24,32},{32,40},{40,48},{48,56},{56,0},{1,9},... | collective-permute-start | bytes 454664 | tf_op jit(solution)/shard_map/ppermute | solution.py:639

commit v7 on v6

--- a/solution.py
+++ b/solution.py
@@ -81,8 +81,9 @@
 X_UP = [(f, x) for f in FINE for x in range(BX - fine_below(f), BX)]
 X_DOWN = [(f, x) for f in FINE for x in range(fine_above(f, 0))]
 EARLY_UP, EARLY_DOWN = 18, 24
-X_UP_EARLY, X_UP_EARLY_TILES = offsets([(key, 1) for key in X_UP[:EARLY_UP]], 8)
-X_DOWN_EARLY, X_DOWN_EARLY_TILES = offsets([(key, 1) for key in X_DOWN[:EARLY_DOWN]], 1)
+FIRST_TILES = 16
+X_UP_EARLY, X_UP_EARLY_TILES = offsets([(key, 1) for key in X_UP[:EARLY_UP]], 32)
+X_DOWN_EARLY, X_DOWN_EARLY_TILES = offsets([(key, 1) for key in X_DOWN[:EARLY_DOWN]], 32)
 X_UP_LATE, X_UP_LATE_TILES = offsets([((f, "z"), 1) for f in FINE] + [(key, 1) for key in X_UP[EARLY_UP:]], 1)
 X_DOWN_LATE, X_DOWN_LATE_TILES = offsets([((f, "z"), 1) for f in FINE] + [(key, 1) for key in X_DOWN[EARLY_DOWN:]], 1)
 FINE_LAYERS = {
@@ -105,6 +106,8 @@
     ]
     for copy in copies:
         copy.start()
+    for f in range(11, FIRST_TILES):
+        first[f] = jnp.zeros((BY, BZ), F32)
     lane = iota((BY, BZ), 1) // 16
     odd = place[3] == 1
     for copy, (_, at, count) in zip(copies, parts):
@@ -649,7 +652,7 @@
     )
     tile = (BY, BZ)
     own, first, second = call(
-        pack_z, [(11, BX) + tile, (11,) + tile, (11,) + tile], [pltpu.SemaphoreType.DMA((3,))],
+        pack_z, [(11, BX) + tile, (FIRST_TILES,) + tile, (11,) + tile], [pltpu.SemaphoreType.DMA((3,))],
         place, iterate, forcing, viscosity, space=HBM,
     )
     first = swap(first, "gz", nz, 1)

time: 73 us -> 75.8 us (1.038)
  the two profiles are of different devices: /device:TPU:132 before, /device:TPU:134 now
where the time goes in v7:
time: 75.8 us; the launch traced here: 75.5 us
  starting transfers between devices  45.8 us (60%)
  waiting for transfers between devices  21.7 us (29%)
  Pallas kernels  7.68 us (10%)
    ppermute x2, starting transfers between devices, swap(): return lax.ppermute(a, axis, pairs)  26 us
    ppermute x4, waiting for transfers between devices, around(): return lax.ppermute(a, axis, [(i, (i + by) % count) for i in range(count)])  10.1 us
    ppermute x3, starting transfers between devices, to_next(): return lax.ppermute(a, axis, [(i, i + 1) for i in range(count - 1)])  9.78 us
    ppermute x3, starting transfers between devices, to_previous(): return lax.ppermute(a, axis, [(i + 1, i) for i in range(count - 1)])  8.96 us
    pallas_call x9, Pallas kernels, call(): pl.pallas_call(kernel, out_shape=[jax.ShapeDtypeStruct(s, F32) for s in o...  7.68 us
    ppermute x3, waiting for transfers between devices, to_next(): return lax.ppermute(a, axis, [(i, i + 1) for i in range(count - 1)])  7.61 us
    ppermute x2, waiting for transfers between devices, swap(): return lax.ppermute(a, axis, pairs)  4.01 us
  transfers between devices with their start and end apart: 12, of which 5 were waited for; matrix products, arithmetic and copies ran while one was open for 0% of the time, Pallas kernels for 1%

profile of v7, /device:TPU:134, one launch (start us, length us, event | category | flops | bytes accessed | tf_op | source)
XLA Modules:
  0.0 75.5 jit_solution(17221719535032143224)
XLA Ops:
  0.0 0.1 add_add_fusion
  0.1 0.1 broadcast.7.place
  0.2 1.3 %shard_map.37 = (f32[11,8,8,128]{3,2,1,0:T(8,128)S(1)}, f32[16,8,128]{2,1,0:T(8,128)S(1)}, f32[11,8,128]{2,1,0:T(8,128)S(1)}) custom-call(s32[4,8,128]{2,1,0:T(8,128)S(1)} %broadcast.7.place, f32[4,8,8,128]{3,2,1,0:T(8,128)} %iterate.1, f32[4,8,8,128]{3,2,1,0:T(8,128)} %forcing.1, f32[3,8,8,128]{3,2,1,0:T(8,128)} %viscosity.1), custom_call_target="tpu_custom_call" | custom-call | tf_op jit(solution)/shard_map/pallas_call | solution.py:24
  1.5 24.1 %collective-permute-start = (f32[16,8,128]{2,1,0:T(8,128)S(1)}, f32[16,8,128]{2,1,0:T(8,128)S(1)}, u32[]{:S(2)}, u32[]{:S(2)}) collective-permute-start(f32[16,8,128]{2,1,0:T(8,128)S(1)} %get-tuple-element.28), channel_id=1, source_target_pairs={{1,2},{2,1},{3,4},{4,3},{5,6},{6,5},{9,10},{10,9},{11,12},{12,11},... | collective-permute-start | bytes 196616 | tf_op jit(solution)/shard_map/ppermute | solution.py:639
  25.6 2.9 %collective-permute-start.2 = (f32[32,8,128]{2,1,0:T(8,128)S(1)}, f32[32,8,128]{2,1,0:T(8,128)S(1)}, u32[]{:S(2)}, u32[]{:S(2)}) collective-permute-start(f32[32,8,128]{2,1,0:T(8,128)S(1)} %get-tuple-element.30), channel_id=1, source_target_pairs={{0,64},{64,128},{128,192},{192,256},{256,320},{320,384},{384,448},... | collective-permute-start | bytes 393224 | tf_op jit(solution)/shard_map/ppermute | solution.py:645
  28.5 4.1 %collective-permute-start.3 = (f32[32,8,128]{2,1,0:T(8,128)S(1)}, f32[32,8,128]{2,1,0:T(8,128)S(1)}, u32[]{:S(2)}, u32[]{:S(2)}) collective-permute-start(f32[32,8,128]{2,1,0:T(8,128)S(1)} %get-tuple-element.31), channel_id=1, source_target_pairs={{64,0},{128,64},{192,128},{256,192},{320,256},{384,320},{448,384},... | collective-permute-start | bytes 393224 | tf_op jit(solution)/shard_map/ppermute | solution.py:648
  32.6 1.9 %collective-permute-start.1 = (f32[11,8,128]{2,1,0:T(8,128)S(1)}, f32[11,8,128]{2,1,0:T(8,128)S(1)}, u32[]{:S(2)}, u32[]{:S(2)}) collective-permute-start(f32[11,8,128]{2,1,0:T(8,128)S(1)} %get-tuple-element.29), channel_id=1, source_target_pairs={{0,1},{1,0},{2,3},{3,2},{4,5},{5,4},{6,7},{7,6},{8,9},{9,8},{10,11... | collective-permute-start | bytes 135176 | tf_op jit(solution)/shard_map/ppermute | solution.py:639
  34.6 4.0 %collective-permute-done.1.second = f32[11,8,128]{2,1,0:T(8,128)S(1)} collective-permute-done((f32[11,8,128]{2,1,0:T(8,128)S(1)}, f32[11,8,128]{2,1,0:T(8,128)S(1)}, u32[]{:S(2)}, u32[]{:S(2)}) %collective-permute-start.1) | collective-permute-done | bytes 45088 | tf_op jit(solution)/shard_map/ppermute | solution.py:639
  38.6 0.1 shard_map.39
  38.7 2.9 %collective-permute-start.5 = (f32[19,8,128]{2,1,0:T(8,128)S(1)}, f32[19,8,128]{2,1,0:T(8,128)S(1)}, u32[]{:S(2)}, u32[]{:S(2)}) collective-permute-start(f32[19,8,128]{2,1,0:T(8,128)S(1)} %get-tuple-element.33), channel_id=1, source_target_pairs={{64,0},{128,64},{192,128},{256,192},{320,256},{384,320},{448,384},... | collective-permute-start | bytes 233480 | tf_op jit(solution)/shard_map/ppermute | solution.py:648
  41.6 2.9 %collective-permute-start.4 = (f32[11,8,128]{2,1,0:T(8,128)S(1)}, f32[11,8,128]{2,1,0:T(8,128)S(1)}, u32[]{:S(2)}, u32[]{:S(2)}) collective-permute-start(f32[11,8,128]{2,1,0:T(8,128)S(1)} %get-tuple-element.32), channel_id=1, source_target_pairs={{0,64},{64,128},{128,192},{192,256},{256,320},{320,384},{384,448},... | collective-permute-start | bytes 135176 | tf_op jit(solution)/shard_map/ppermute | solution.py:645
  44.5 4.2 %collective-permute-done.4.low_late = f32[11,8,128]{2,1,0:T(8,128)S(1)} collective-permute-done((f32[11,8,128]{2,1,0:T(8,128)S(1)}, f32[11,8,128]{2,1,0:T(8,128)S(1)}, u32[]{:S(2)}, u32[]{:S(2)}) %collective-permute-start.4) | collective-permute-done | bytes 45088 | tf_op jit(solution)/shard_map/ppermute | solution.py:645
  48.8 0.1 shard_map.41
  48.9 0.5 collective-permute-start.6
  49.4 0.3 shard_map.40.half
  49.8 5.2 %collective-permute-done.6.y_low = f32[304,128]{1,0:T(8,128)S(1)} collective-permute-done((f32[304,128]{1,0:T(8,128)S(1)}, f32[304,128]{1,0:T(8,128)S(1)}, u32[]{:S(2)}, u32[]{:S(2)}) %collective-permute-start.6) | collective-permute-done | bytes 155680 | tf_op jit(solution)/shard_map/ppermute | solution.py:642
  54.9 3.1 %shard_map.42 = (f32[11,14,16,256]{3,2,1,0:T(8,128)S(1)}, f32[4,14,16,256]{3,2,1,0:T(8,128)S(1)}, f32[7,4,8,128]{3,2,1,0:T(8,128)S(1)}, f32[160,128]{1,0:T(8,128)S(1)}, f32[120,128]{1,0:T(8,128)S(1)}) custom-call(s32[4,8,128]{2,1,0:T(8,128)S(1)} %broadcast.7.place, f32[11,14,8,256]{3,2,1,0:T(8,128)S(1)} %shard_map.40.half, ...), custom_call_target="tpu_custom_call" | custom-call | tf_op jit(solution)/shard_map/pallas_call | solution.py:24
  58.0 1.9 %collective-permute-start.9 = (f32[160,128]{1,0:T(8,128)S(1)}, f32[160,128]{1,0:T(8,128)S(1)}, u32[]{:S(2)}, u32[]{:S(2)}) collective-permute-start(f32[160,128]{1,0:T(8,128)S(1)} %get-tuple-element.45), channel_id=1, source_target_pairs={{64,0},{128,64},{192,128},{256,192},{320,256},{384,320},{448,384},... | collective-permute-start | bytes 245768 | tf_op jit(solution)/shard_map/ppermute | solution.py:648
  59.9 3.9 %collective-permute-start.8 = (f32[120,128]{1,0:T(8,128)S(1)}, f32[120,128]{1,0:T(8,128)S(1)}, u32[]{:S(2)}, u32[]{:S(2)}) collective-permute-start(f32[120,128]{1,0:T(8,128)S(1)} %get-tuple-element.44), channel_id=1, source_target_pairs={{0,64},{64,128},{128,192},{192,256},{256,320},{320,384},{384,448},... | collective-permute-start | bytes 184328 | tf_op jit(solution)/shard_map/ppermute | solution.py:645
  63.9 3.4 %collective-permute-done.8.from_low = f32[120,128]{1,0:T(8,128)S(1)} collective-permute-done((f32[120,128]{1,0:T(8,128)S(1)}, f32[120,128]{1,0:T(8,128)S(1)}, u32[]{:S(2)}, u32[]{:S(2)}) %collective-permute-start.8) | collective-permute-done | bytes 61472 | tf_op jit(solution)/shard_map/ppermute | solution.py:645
  67.4 0.5 collective-permute-start.10
  67.9 0.4 shard_map.43
  68.3 4.9 %collective-permute-done.10.y_low = f32[296,128]{1,0:T(8,128)S(1)} collective-permute-done((f32[296,128]{1,0:T(8,128)S(1)}, f32[296,128]{1,0:T(8,128)S(1)}, u32[]{:S(2)}, u32[]{:S(2)}) %collective-permute-start.10) | collective-permute-done | bytes 151584 | tf_op jit(solution)/shard_map/ppermute | solution.py:642
  73.2 2.3 %shard_map.45 = f32[4,8,8,128]{3,2,1,0:T(8,128)} custom-call(s32[4,8,128]{2,1,0:T(8,128)S(1)} %broadcast.7.place, f32[3,6,9,16,256]{4,3,2,1,0:T(8,128)S(1)} %get-tuple-element.38.last_sums, f32[3,9,16,256]{3,2,1,0:T(8,128)S(1)} %get-tuple-element.39.base, f32[3,9,16,256]{3,2,1,0:T(8,128)S(1)} %get-tuple-element.40.inv, ...), custom_call_target="tpu_custom_call" | custom-call | tf_op jit(solution)/shard_map/pallas_call | solution.py:24
  (11 shorter events, 0.1 us)
Async XLA Ops:
  1.5 37.1 %collective-permute-start = (f32[16,8,128]{2,1,0:T(8,128)S(1)}, f32[16,8,128]{2,1,0:T(8,128)S(1)}, u32[]{:S(2)}, u32[]{:S(2)}) collective-permute-start(f32[16,8,128]{2,1,0:T(8,128)S(1)} %get-tuple-element.28), channel_id=1, source_target_pairs={{1,2},{2,1},{3,4},{4,3},{5,6},{6,5},{9,10},{10,9},{11,12},{12,11},... | collective-permute-start | bytes 196616 | tf_op jit(solution)/shard_map/ppermute | solution.py:639
  25.6 23.2 %collective-permute-start.2 = (f32[32,8,128]{2,1,0:T(8,128)S(1)}, f32[32,8,128]{2,1,0:T(8,128)S(1)}, u32[]{:S(2)}, u32[]{:S(2)}) collective-permute-start(f32[32,8,128]{2,1,0:T(8,128)S(1)} %get-tuple-element.30), channel_id=1, source_target_pairs={{0,64},{64,128},{128,192},{192,256},{256,320},{320,384},{384,448},... | collective-permute-start | bytes 393224 | tf_op jit(solution)/shard_map/ppermute | solution.py:645
  28.5 20.3 %collective-permute-start.3 = (f32[32,8,128]{2,1,0:T(8,128)S(1)}, f32[32,8,128]{2,1,0:T(8,128)S(1)}, u32[]{:S(2)}, u32[]{:S(2)}) collective-permute-start(f32[32,8,128]{2,1,0:T(8,128)S(1)} %get-tuple-element.31), channel_id=1, source_target_pairs={{64,0},{128,64},{192,128},{256,192},{320,256},{384,320},{448,384},... | collective-permute-start | bytes 393224 | tf_op jit(solution)/shard_map/ppermute | solution.py:648
  32.6 5.9 %collective-permute-start.1 = (f32[11,8,128]{2,1,0:T(8,128)S(1)}, f32[11,8,128]{2,1,0:T(8,128)S(1)}, u32[]{:S(2)}, u32[]{:S(2)}) collective-permute-start(f32[11,8,128]{2,1,0:T(8,128)S(1)} %get-tuple-element.29), channel_id=1, source_target_pairs={{0,1},{1,0},{2,3},{3,2},{4,5},{5,4},{6,7},{7,6},{8,9},{9,8},{10,11... | collective-permute-start | bytes 135176 | tf_op jit(solution)/shard_map/ppermute | solution.py:639
  38.7 10.1 %collective-permute-start.5 = (f32[19,8,128]{2,1,0:T(8,128)S(1)}, f32[19,8,128]{2,1,0:T(8,128)S(1)}, u32[]{:S(2)}, u32[]{:S(2)}) collective-permute-start(f32[19,8,128]{2,1,0:T(8,128)S(1)} %get-tuple-element.33), channel_id=1, source_target_pairs={{64,0},{128,64},{192,128},{256,192},{320,256},{384,320},{448,384},... | collective-permute-start | bytes 233480 | tf_op jit(solution)/shard_map/ppermute | solution.py:648
  41.6 7.2 %collective-permute-start.4 = (f32[11,8,128]{2,1,0:T(8,128)S(1)}, f32[11,8,128]{2,1,0:T(8,128)S(1)}, u32[]{:S(2)}, u32[]{:S(2)}) collective-permute-start(f32[11,8,128]{2,1,0:T(8,128)S(1)} %get-tuple-element.32), channel_id=1, source_target_pairs={{0,64},{64,128},{128,192},{192,256},{256,320},{320,384},{384,448},... | collective-permute-start | bytes 135176 | tf_op jit(solution)/shard_map/ppermute | solution.py:645
  48.9 6.1 %collective-permute-start.7 = (f32[536,128]{1,0:T(8,128)S(1)}, f32[536,128]{1,0:T(8,128)S(1)}, u32[]{:S(2)}, u32[]{:S(2)}) collective-permute-start(f32[536,128]{1,0:T(8,128)S(1)} %get-tuple-element.35), channel_id=1, source_target_pairs={{0,56},{8,0},{16,8},{24,16},{32,24},{40,32},{48,40},{56,48},{1,57}... | collective-permute-start | bytes 823304 | tf_op jit(solution)/shard_map/ppermute | solution.py:642
  48.9 6.0 %collective-permute-start.6 = (f32[304,128]{1,0:T(8,128)S(1)}, f32[304,128]{1,0:T(8,128)S(1)}, u32[]{:S(2)}, u32[]{:S(2)}) collective-permute-start(f32[304,128]{1,0:T(8,128)S(1)} %get-tuple-element.34), channel_id=1, source_target_pairs={{0,8},{8,16},{16,24},{24,32},{32,40},{40,48},{48,56},{56,0},{1,9},... | collective-permute-start | bytes 466952 | tf_op jit(solution)/shard_map/ppermute | solution.py:642
  58.0 9.3 %collective-permute-start.9 = (f32[160,128]{1,0:T(8,128)S(1)}, f32[160,128]{1,0:T(8,128)S(1)}, u32[]{:S(2)}, u32[]{:S(2)}) collective-permute-start(f32[160,128]{1,0:T(8,128)S(1)} %get-tuple-element.45), channel_id=1, source_target_pairs={{64,0},{128,64},{192,128},{256,192},{320,256},{384,320},{448,384},... | collective-permute-start | bytes 245768 | tf_op jit(solution)/shard_map/ppermute | solution.py:648
  59.9 7.3 %collective-permute-start.8 = (f32[120,128]{1,0:T(8,128)S(1)}, f32[120,128]{1,0:T(8,128)S(1)}, u32[]{:S(2)}, u32[]{:S(2)}) collective-permute-start(f32[120,128]{1,0:T(8,128)S(1)} %get-tuple-element.44), channel_id=1, source_target_pairs={{0,64},{64,128},{128,192},{192,256},{256,320},{320,384},{384,448},... | collective-permute-start | bytes 184328 | tf_op jit(solution)/shard_map/ppermute | solution.py:645
  67.3 5.9 %collective-permute-start.11 = (f32[408,128]{1,0:T(8,128)S(1)}, f32[408,128]{1,0:T(8,128)S(1)}, u32[]{:S(2)}, u32[]{:S(2)}) collective-permute-start(f32[408,128]{1,0:T(8,128)S(1)} %get-tuple-element.48), channel_id=1, source_target_pairs={{0,56},{8,0},{16,8},{24,16},{32,24},{40,32},{48,40},{56,48},{1,57}... | collective-permute-start | bytes 626696 | tf_op jit(solution)/shard_map/ppermute | solution.py:642
  67.4 5.8 %collective-permute-start.10 = (f32[296,128]{1,0:T(8,128)S(1)}, f32[296,128]{1,0:T(8,128)S(1)}, u32[]{:S(2)}, u32[]{:S(2)}) collective-permute-start(f32[296,128]{1,0:T(8,128)S(1)} %get-tuple-element.47), channel_id=1, source_target_pairs={{0,8},{8,16},{16,24},{24,32},{32,40},{40,48},{48,56},{56,0},{1,9},... | collective-permute-start | bytes 454664 | tf_op jit(solution)/shard_map/ppermute | solution.py:642

commit v8 on v5

--- a/solution.py
+++ b/solution.py
@@ -96,6 +96,9 @@
 MY_DOWN, MY_DOWN_ROWS = offsets([((f, l), mid_above(f, 1)) for f in MID for l in MID_LAYERS[f]])
 
 
+NEAR_TILES = 16
+
+
 def pack_z(place, iterate, forcing, viscosity, own, first, second, sems):
     parts = ((iterate, 0, 4), (forcing, 4, 4), (viscosity, 8, 3))
     copies = [
@@ -105,6 +108,8 @@
     for copy in copies:
         copy.start()
     lane = iota((BY, BZ), 1) // 16
+    for f in range(11, NEAR_TILES):
+        second[f] = jnp.zeros((BY, BZ), F32)
     odd = place[3] == 1
     for copy, (_, at, count) in zip(copies, parts):
         copy.wait()
@@ -631,7 +636,7 @@
     )
     tile = (BY, BZ)
     own, first, second = call(
-        pack_z, [(11, BX) + tile, (11,) + tile, (11,) + tile], [pltpu.SemaphoreType.DMA((3,))],
+        pack_z, [(11, BX) + tile, (11,) + tile, (NEAR_TILES,) + tile], [pltpu.SemaphoreType.DMA((3,))],
         place, iterate, forcing, viscosity, space=HBM,
     )
     first = swap(first, "gz", nz, 1)

time: 72.7 us -> 75.6 us (1.040)
  the two profiles are of different devices: /device:TPU:641 before, /device:TPU:38 now
where the time goes in v8:
time: 75.6 us; the launch traced here: 75.3 us
  starting transfers between devices  46.2 us (61%)
  waiting for transfers between devices  21.1 us (28%)
  Pallas kernels  7.65 us (10%)
    ppermute x2, starting transfers between devices, swap(): return lax.ppermute(a, axis, pairs)  31.4 us
    ppermute x4, waiting for transfers between devices, around(): return lax.ppermute(a, axis, [(i, (i + by) % count) for i in range(count)])  10.4 us
    pallas_call x8, Pallas kernels, call(): pl.pallas_call(kernel, out_shape=[jax.ShapeDtypeStruct(s, F32) for s in o...  7.65 us
    ppermute x2, waiting for transfers between devices, to_next(): return lax.ppermute(a, axis, [(i, i + 1) for i in range(count - 1)])  7.55 us
    ppermute x2, starting transfers between devices, to_previous(): return lax.ppermute(a, axis, [(i + 1, i) for i in range(count - 1)])  6.28 us
    ppermute x2, starting transfers between devices, to_next(): return lax.ppermute(a, axis, [(i, i + 1) for i in range(count - 1)])  5.41 us
    ppermute x4, starting transfers between devices, around(): return lax.ppermute(a, axis, [(i, (i + by) % count) for i in range(count)])  3.16 us
    ppermute x2, waiting for transfers between devices, swap(): return lax.ppermute(a, axis, pairs)  2.38 us
  transfers between devices with their start and end apart: 10, of which 6 were waited for; matrix products, arithmetic and copies ran while one was open for 0% of the time, Pallas kernels for 1%

profile of v8, /device:TPU:38, one launch (start us, length us, event | category | flops | bytes accessed | tf_op | source)
XLA Modules:
  0.0 75.3 jit_solution(8069120944440103267)
XLA Ops:
  0.0 0.1 add_add_fusion
  0.1 0.1 broadcast.7.place
  0.2 1.3 %shard_map.37 = (f32[11,8,8,128]{3,2,1,0:T(8,128)S(1)}, f32[11,8,128]{2,1,0:T(8,128)S(1)}, f32[16,8,128]{2,1,0:T(8,128)S(1)}) custom-call(s32[4,8,128]{2,1,0:T(8,128)S(1)} %broadcast.7.place, f32[4,8,8,128]{3,2,1,0:T(8,128)} %iterate.1, f32[4,8,8,128]{3,2,1,0:T(8,128)} %forcing.1, f32[3,8,8,128]{3,2,1,0:T(8,128)} %viscosity.1), custom_call_target="tpu_custom_call" | custom-call | tf_op jit(solution)/shard_map/pallas_call | solution.py:24
  1.5 2.7 %collective-permute-start.1 = (f32[16,8,128]{2,1,0:T(8,128)S(1)}, f32[16,8,128]{2,1,0:T(8,128)S(1)}, u32[]{:S(2)}, u32[]{:S(2)}) collective-permute-start(f32[16,8,128]{2,1,0:T(8,128)S(1)} %get-tuple-element.27), channel_id=1, source_target_pairs={{0,1},{1,0},{2,3},{3,2},{4,5},{5,4},{6,7},{7,6},{8,9},{9,8},{10,11... | collective-permute-start | bytes 196616 | tf_op jit(solution)/shard_map/ppermute | solution.py:623
  4.2 28.7 %collective-permute-start = (f32[11,8,128]{2,1,0:T(8,128)S(1)}, f32[11,8,128]{2,1,0:T(8,128)S(1)}, u32[]{:S(2)}, u32[]{:S(2)}) collective-permute-start(f32[11,8,128]{2,1,0:T(8,128)S(1)} %get-tuple-element.26), channel_id=1, source_target_pairs={{1,2},{2,1},{3,4},{4,3},{5,6},{6,5},{9,10},{10,9},{11,12},{12,11},... | collective-permute-start | bytes 135176 | tf_op jit(solution)/shard_map/ppermute | solution.py:623
  32.9 2.4 %collective-permute-done.first = f32[11,8,128]{2,1,0:T(8,128)S(1)} collective-permute-done((f32[11,8,128]{2,1,0:T(8,128)S(1)}, f32[11,8,128]{2,1,0:T(8,128)S(1)}, u32[]{:S(2)}, u32[]{:S(2)}) %collective-permute-start) | collective-permute-done | bytes 45088 | tf_op jit(solution)/shard_map/ppermute | solution.py:623
  35.2 0.1 shard_map.38
  35.3 2.8 %collective-permute-start.3 = (f32[48,8,128]{2,1,0:T(8,128)S(1)}, f32[48,8,128]{2,1,0:T(8,128)S(1)}, u32[]{:S(2)}, u32[]{:S(2)}) collective-permute-start(f32[48,8,128]{2,1,0:T(8,128)S(1)} %get-tuple-element.29), channel_id=1, source_target_pairs={{64,0},{128,64},{192,128},{256,192},{320,256},{384,320},{448,384},... | collective-permute-start | bytes 589832 | tf_op jit(solution)/shard_map/ppermute | solution.py:632
  38.2 3.0 %collective-permute-start.2 = (f32[32,8,128]{2,1,0:T(8,128)S(1)}, f32[32,8,128]{2,1,0:T(8,128)S(1)}, u32[]{:S(2)}, u32[]{:S(2)}) collective-permute-start(f32[32,8,128]{2,1,0:T(8,128)S(1)} %get-tuple-element.28), channel_id=1, source_target_pairs={{0,64},{64,128},{128,192},{192,256},{256,320},{320,384},{384,448},... | collective-permute-start | bytes 393224 | tf_op jit(solution)/shard_map/ppermute | solution.py:629
  41.2 3.9 %collective-permute-done.2.from_low = f32[32,8,128]{2,1,0:T(8,128)S(1)} collective-permute-done((f32[32,8,128]{2,1,0:T(8,128)S(1)}, f32[32,8,128]{2,1,0:T(8,128)S(1)}, u32[]{:S(2)}, u32[]{:S(2)}) %collective-permute-start.2) | collective-permute-done | bytes 131104 | tf_op jit(solution)/shard_map/ppermute | solution.py:629
  45.1 0.8 %collective-permute-done.3.from_high = f32[48,8,128]{2,1,0:T(8,128)S(1)} collective-permute-done((f32[48,8,128]{2,1,0:T(8,128)S(1)}, f32[48,8,128]{2,1,0:T(8,128)S(1)}, u32[]{:S(2)}, u32[]{:S(2)}) %collective-permute-start.3) | collective-permute-done | bytes 196640 | tf_op jit(solution)/shard_map/ppermute | solution.py:632
  45.9 0.1 shard_map.40
  46.0 2.6 %collective-permute-start.5 = (f32[536,128]{1,0:T(8,128)S(1)}, f32[536,128]{1,0:T(8,128)S(1)}, u32[]{:S(2)}, u32[]{:S(2)}) collective-permute-start(f32[536,128]{1,0:T(8,128)S(1)} %get-tuple-element.31), channel_id=1, source_target_pairs={{0,56},{8,0},{16,8},{24,16},{32,24},{40,32},{48,40},{56,48},{1,57}... | collective-permute-start | bytes 823304 | tf_op jit(solution)/shard_map/ppermute | solution.py:626
  48.6 0.4 shard_map.39.half
  49.0 5.5 %collective-permute-done.4.y_low = f32[304,128]{1,0:T(8,128)S(1)} collective-permute-done((f32[304,128]{1,0:T(8,128)S(1)}, f32[304,128]{1,0:T(8,128)S(1)}, u32[]{:S(2)}, u32[]{:S(2)}) %collective-permute-start.4) | collective-permute-done | bytes 155680 | tf_op jit(solution)/shard_map/ppermute | solution.py:626
  54.5 3.1 %shard_map.41 = (f32[11,14,16,256]{3,2,1,0:T(8,128)S(1)}, f32[4,14,16,256]{3,2,1,0:T(8,128)S(1)}, f32[7,4,8,128]{3,2,1,0:T(8,128)S(1)}, f32[160,128]{1,0:T(8,128)S(1)}, f32[120,128]{1,0:T(8,128)S(1)}) custom-call(s32[4,8,128]{2,1,0:T(8,128)S(1)} %broadcast.7.place, f32[11,14,8,256]{3,2,1,0:T(8,128)S(1)} %shard_map.39.half, ...), custom_call_target="tpu_custom_call" | custom-call | tf_op jit(solution)/shard_map/pallas_call | solution.py:24
  57.5 3.4 %collective-permute-start.7 = (f32[160,128]{1,0:T(8,128)S(1)}, f32[160,128]{1,0:T(8,128)S(1)}, u32[]{:S(2)}, u32[]{:S(2)}) collective-permute-start(f32[160,128]{1,0:T(8,128)S(1)} %get-tuple-element.41), channel_id=1, source_target_pairs={{64,0},{128,64},{192,128},{256,192},{320,256},{384,320},{448,384},... | collective-permute-start | bytes 245768 | tf_op jit(solution)/shard_map/ppermute | solution.py:632
  61.0 2.4 %collective-permute-start.6 = (f32[120,128]{1,0:T(8,128)S(1)}, f32[120,128]{1,0:T(8,128)S(1)}, u32[]{:S(2)}, u32[]{:S(2)}) collective-permute-start(f32[120,128]{1,0:T(8,128)S(1)} %get-tuple-element.40), channel_id=1, source_target_pairs={{0,64},{64,128},{128,192},{192,256},{256,320},{320,384},{384,448},... | collective-permute-start | bytes 184328 | tf_op jit(solution)/shard_map/ppermute | solution.py:629
  63.4 3.7 %collective-permute-done.6.from_low = f32[120,128]{1,0:T(8,128)S(1)} collective-permute-done((f32[120,128]{1,0:T(8,128)S(1)}, f32[120,128]{1,0:T(8,128)S(1)}, u32[]{:S(2)}, u32[]{:S(2)}) %collective-permute-start.6) | collective-permute-done | bytes 61472 | tf_op jit(solution)/shard_map/ppermute | solution.py:629
  67.1 0.1 shard_map.43
  67.2 0.5 collective-permute-start.8
  67.7 0.4 shard_map.42
  68.1 4.9 %collective-permute-done.8.y_low = f32[296,128]{1,0:T(8,128)S(1)} collective-permute-done((f32[296,128]{1,0:T(8,128)S(1)}, f32[296,128]{1,0:T(8,128)S(1)}, u32[]{:S(2)}, u32[]{:S(2)}) %collective-permute-start.8) | collective-permute-done | bytes 151584 | tf_op jit(solution)/shard_map/ppermute | solution.py:626
  73.0 2.2 %shard_map.44 = f32[4,8,8,128]{3,2,1,0:T(8,128)} custom-call(s32[4,8,128]{2,1,0:T(8,128)S(1)} %broadcast.7.place, f32[3,6,9,16,256]{4,3,2,1,0:T(8,128)S(1)} %get-tuple-element.34.last_sums, f32[3,9,16,256]{3,2,1,0:T(8,128)S(1)} %get-tuple-element.35.base, f32[3,9,16,256]{3,2,1,0:T(8,128)S(1)} %get-tuple-element.36.inv, ...), custom_call_target="tpu_custom_call" | custom-call | tf_op jit(solution)/shard_map/pallas_call | solution.py:24
  (6 shorter events, 0.0 us)
Async XLA Ops:
  1.5 33.8 %collective-permute-start.1 = (f32[16,8,128]{2,1,0:T(8,128)S(1)}, f32[16,8,128]{2,1,0:T(8,128)S(1)}, u32[]{:S(2)}, u32[]{:S(2)}) collective-permute-start(f32[16,8,128]{2,1,0:T(8,128)S(1)} %get-tuple-element.27), channel_id=1, source_target_pairs={{0,1},{1,0},{2,3},{3,2},{4,5},{5,4},{6,7},{7,6},{8,9},{9,8},{10,11... | collective-permute-start | bytes 196616 | tf_op jit(solution)/shard_map/ppermute | solution.py:623
  4.2 31.0 %collective-permute-start = (f32[11,8,128]{2,1,0:T(8,128)S(1)}, f32[11,8,128]{2,1,0:T(8,128)S(1)}, u32[]{:S(2)}, u32[]{:S(2)}) collective-permute-start(f32[11,8,128]{2,1,0:T(8,128)S(1)} %get-tuple-element.26), channel_id=1, source_target_pairs={{1,2},{2,1},{3,4},{4,3},{5,6},{6,5},{9,10},{10,9},{11,12},{12,11},... | collective-permute-start | bytes 135176 | tf_op jit(solution)/shard_map/ppermute | solution.py:623
  35.3 10.5 %collective-permute-start.3 = (f32[48,8,128]{2,1,0:T(8,128)S(1)}, f32[48,8,128]{2,1,0:T(8,128)S(1)}, u32[]{:S(2)}, u32[]{:S(2)}) collective-permute-start(f32[48,8,128]{2,1,0:T(8,128)S(1)} %get-tuple-element.29), channel_id=1, source_target_pairs={{64,0},{128,64},{192,128},{256,192},{320,256},{384,320},{448,384},... | collective-permute-start | bytes 589832 | tf_op jit(solution)/shard_map/ppermute | solution.py:632
  38.2 6.9 %collective-permute-start.2 = (f32[32,8,128]{2,1,0:T(8,128)S(1)}, f32[32,8,128]{2,1,0:T(8,128)S(1)}, u32[]{:S(2)}, u32[]{:S(2)}) collective-permute-start(f32[32,8,128]{2,1,0:T(8,128)S(1)} %get-tuple-element.28), channel_id=1, source_target_pairs={{0,64},{64,128},{128,192},{192,256},{256,320},{320,384},{384,448},... | collective-permute-start | bytes 393224 | tf_op jit(solution)/shard_map/ppermute | solution.py:629
  46.0 8.5 %collective-permute-start.5 = (f32[536,128]{1,0:T(8,128)S(1)}, f32[536,128]{1,0:T(8,128)S(1)}, u32[]{:S(2)}, u32[]{:S(2)}) collective-permute-start(f32[536,128]{1,0:T(8,128)S(1)} %get-tuple-element.31), channel_id=1, source_target_pairs={{0,56},{8,0},{16,8},{24,16},{32,24},{40,32},{48,40},{56,48},{1,57}... | collective-permute-start | bytes 823304 | tf_op jit(solution)/shard_map/ppermute | solution.py:626
  48.6 5.9 %collective-permute-start.4 = (f32[304,128]{1,0:T(8,128)S(1)}, f32[304,128]{1,0:T(8,128)S(1)}, u32[]{:S(2)}, u32[]{:S(2)}) collective-permute-start(f32[304,128]{1,0:T(8,128)S(1)} %get-tuple-element.30), channel_id=1, source_target_pairs={{0,8},{8,16},{16,24},{24,32},{32,40},{40,48},{48,56},{56,0},{1,9},... | collective-permute-start | bytes 466952 | tf_op jit(solution)/shard_map/ppermute | solution.py:626
  57.5 9.6 %collective-permute-start.7 = (f32[160,128]{1,0:T(8,128)S(1)}, f32[160,128]{1,0:T(8,128)S(1)}, u32[]{:S(2)}, u32[]{:S(2)}) collective-permute-start(f32[160,128]{1,0:T(8,128)S(1)} %get-tuple-element.41), channel_id=1, source_target_pairs={{64,0},{128,64},{192,128},{256,192},{320,256},{384,320},{448,384},... | collective-permute-start | bytes 245768 | tf_op jit(solution)/shard_map/ppermute | solution.py:632
  61.0 6.1 %collective-permute-start.6 = (f32[120,128]{1,0:T(8,128)S(1)}, f32[120,128]{1,0:T(8,128)S(1)}, u32[]{:S(2)}, u32[]{:S(2)}) collective-permute-start(f32[120,128]{1,0:T(8,128)S(1)} %get-tuple-element.40), channel_id=1, source_target_pairs={{0,64},{64,128},{128,192},{192,256},{256,320},{320,384},{384,448},... | collective-permute-start | bytes 184328 | tf_op jit(solution)/shard_map/ppermute | solution.py:629
  67.2 5.9 %collective-permute-start.9 = (f32[408,128]{1,0:T(8,128)S(1)}, f32[408,128]{1,0:T(8,128)S(1)}, u32[]{:S(2)}, u32[]{:S(2)}) collective-permute-start(f32[408,128]{1,0:T(8,128)S(1)} %get-tuple-element.44), channel_id=1, source_target_pairs={{0,56},{8,0},{16,8},{24,16},{32,24},{40,32},{48,40},{56,48},{1,57}... | collective-permute-start | bytes 626696 | tf_op jit(solution)/shard_map/ppermute | solution.py:626
  67.2 5.8 %collective-permute-start.8 = (f32[296,128]{1,0:T(8,128)S(1)}, f32[296,128]{1,0:T(8,128)S(1)}, u32[]{:S(2)}, u32[]{:S(2)}) collective-permute-start(f32[296,128]{1,0:T(8,128)S(1)} %get-tuple-element.43), channel_id=1, source_target_pairs={{0,8},{8,16},{16,24},{24,32},{32,40},{40,48},{48,56},{56,0},{1,9},... | collective-permute-start | bytes 454664 | tf_op jit(solution)/shard_map/ppermute | solution.py:626

commit v9 on v5

--- a/solution.py
+++ b/solution.py
@@ -97,18 +97,16 @@
 
 
 def pack_z(place, iterate, forcing, viscosity, own, first, second, sems):
-    parts = ((iterate, 0, 4), (forcing, 4, 4), (viscosity, 8, 3))
-    copies = [
-        pltpu.make_async_copy(source, own.at[at : at + count], sems.at[i])
-        for i, (source, at, count) in enumerate(parts)
-    ]
+    parts = [(iterate, f, f) for f in range(4)] + [(forcing, f, 4 + f) for f in range(4)]
+    parts += [(viscosity, f, 8 + f) for f in range(3)]
+    copies = [pltpu.make_async_copy(source.at[f], own.at[at], sems.at[at]) for source, f, at in parts]
     for copy in copies:
         copy.start()
     lane = iota((BY, BZ), 1) // 16
     odd = place[3] == 1
-    for copy, (_, at, count) in zip(copies, parts):
+    for copy, (_, _, at) in zip(copies, parts):
         copy.wait()
-        for f in range(at, at + count):
+        for f in (at,):
             low = jnp.zeros((BY, BZ), F32)
             high = jnp.zeros((BY, BZ), F32)
             for x in range(BX):
@@ -631,7 +629,7 @@
     )
     tile = (BY, BZ)
     own, first, second = call(
-        pack_z, [(11, BX) + tile, (11,) + tile, (11,) + tile], [pltpu.SemaphoreType.DMA((3,))],
+        pack_z, [(11, BX) + tile, (11,) + tile, (11,) + tile], [pltpu.SemaphoreType.DMA((11,))],
         place, iterate, forcing, viscosity, space=HBM,
     )
     first = swap(first, "gz", nz, 1)

time: 72.7 us -> 73.2 us (level)
  no operation moved by 1% of the time
where the time goes in v9:
time: 73.2 us; the launch traced here: 71.7 us
  waiting for transfers between devices  34.3 us (47%)
  starting transfers between devices  29.1 us (40%)
  Pallas kernels  8.13 us (11%)
    ppermute x2, waiting for transfers between devices, swap(): return lax.ppermute(a, axis, pairs)  19.1 us
    ppermute x4, starting transfers between devices, around(): return lax.ppermute(a, axis, [(i, (i + by) % count) for i in range(count)])  11.9 us
    pallas_call x8, Pallas kernels, call(): pl.pallas_call(kernel, out_shape=[jax.ShapeDtypeStruct(s, F32) for s in o...  8.13 us
    ppermute x2, waiting for transfers between devices, to_next(): return lax.ppermute(a, axis, [(i, i + 1) for i in range(count - 1)])  7.8 us
    ppermute x4, waiting for transfers between devices, around(): return lax.ppermute(a, axis, [(i, (i + by) % count) for i in range(count)])  7.41 us
    ppermute x2, starting transfers between devices, swap(): return lax.ppermute(a, axis, pairs)  6.24 us
    ppermute x2, starting transfers between devices, to_previous(): return lax.ppermute(a, axis, [(i + 1, i) for i in range(count - 1)])  5.7 us
    ppermute x2, starting transfers between devices, to_next(): return lax.ppermute(a, axis, [(i, i + 1) for i in range(count - 1)])  5.28 us
  transfers between devices with their start and end apart: 10, of which 7 were waited for; matrix products, arithmetic and copies ran while one was open for 0% of the time, Pallas kernels for 1%

profile of v9, /device:TPU:641, one launch (start us, length us, event | category | flops | bytes accessed | tf_op | source)
XLA Modules:
  0.0 71.7 jit_solution(14952202110525377655)
XLA Ops:
  0.2 1.8 %shard_map.37 = (f32[11,8,8,128]{3,2,1,0:T(8,128)S(1)}, f32[11,8,128]{2,1,0:T(8,128)S(1)}, f32[11,8,128]{2,1,0:T(8,128)S(1)}) custom-call(s32[4,8,128]{2,1,0:T(8,128)S(1)} %broadcast.7.place, f32[4,8,8,128]{3,2,1,0:T(8,128)} %iterate.1, f32[4,8,8,128]{3,2,1,0:T(8,128)} %forcing.1, f32[3,8,8,128]{3,2,1,0:T(8,128)} %viscosity.1), custom_call_target="tpu_custom_call" | custom-call | tf_op jit(solution)/shard_map/pallas_call | solution.py:24
  1.9 1.9 %collective-permute-start = (f32[11,8,128]{2,1,0:T(8,128)S(1)}, f32[11,8,128]{2,1,0:T(8,128)S(1)}, u32[]{:S(2)}, u32[]{:S(2)}) collective-permute-start(f32[11,8,128]{2,1,0:T(8,128)S(1)} %get-tuple-element.26), channel_id=1, source_target_pairs={{1,2},{2,1},{3,4},{4,3},{5,6},{6,5},{9,10},{10,9},{11,12},{12,11},... | collective-permute-start | bytes 135176 | tf_op jit(solution)/shard_map/ppermute | solution.py:616
  3.9 4.3 %collective-permute-start.1 = (f32[11,8,128]{2,1,0:T(8,128)S(1)}, f32[11,8,128]{2,1,0:T(8,128)S(1)}, u32[]{:S(2)}, u32[]{:S(2)}) collective-permute-start(f32[11,8,128]{2,1,0:T(8,128)S(1)} %get-tuple-element.27), channel_id=1, source_target_pairs={{0,1},{1,0},{2,3},{3,2},{4,5},{5,4},{6,7},{7,6},{8,9},{9,8},{10,11... | collective-permute-start | bytes 135176 | tf_op jit(solution)/shard_map/ppermute | solution.py:616
  8.2 19.1 %collective-permute-done.first = f32[11,8,128]{2,1,0:T(8,128)S(1)} collective-permute-done((f32[11,8,128]{2,1,0:T(8,128)S(1)}, f32[11,8,128]{2,1,0:T(8,128)S(1)}, u32[]{:S(2)}, u32[]{:S(2)}) %collective-permute-start) | collective-permute-done | bytes 45088 | tf_op jit(solution)/shard_map/ppermute | solution.py:616
  27.3 0.1 shard_map.38
  27.4 3.8 %collective-permute-start.3 = (f32[48,8,128]{2,1,0:T(8,128)S(1)}, f32[48,8,128]{2,1,0:T(8,128)S(1)}, u32[]{:S(2)}, u32[]{:S(2)}) collective-permute-start(f32[48,8,128]{2,1,0:T(8,128)S(1)} %get-tuple-element.29), channel_id=1, source_target_pairs={{64,0},{128,64},{192,128},{256,192},{320,256},{384,320},{448,384},... | collective-permute-start | bytes 589832 | tf_op jit(solution)/shard_map/ppermute | solution.py:625
  31.1 1.9 %collective-permute-start.2 = (f32[32,8,128]{2,1,0:T(8,128)S(1)}, f32[32,8,128]{2,1,0:T(8,128)S(1)}, u32[]{:S(2)}, u32[]{:S(2)}) collective-permute-start(f32[32,8,128]{2,1,0:T(8,128)S(1)} %get-tuple-element.28), channel_id=1, source_target_pairs={{0,64},{64,128},{128,192},{192,256},{256,320},{320,384},{384,448},... | collective-permute-start | bytes 393224 | tf_op jit(solution)/shard_map/ppermute | solution.py:622
  33.1 5.0 %collective-permute-done.2.from_low = f32[32,8,128]{2,1,0:T(8,128)S(1)} collective-permute-done((f32[32,8,128]{2,1,0:T(8,128)S(1)}, f32[32,8,128]{2,1,0:T(8,128)S(1)}, u32[]{:S(2)}, u32[]{:S(2)}) %collective-permute-start.2) | collective-permute-done | bytes 131104 | tf_op jit(solution)/shard_map/ppermute | solution.py:622
  38.1 0.1 shard_map.40
  38.2 8.8 %collective-permute-start.5 = (f32[536,128]{1,0:T(8,128)S(1)}, f32[536,128]{1,0:T(8,128)S(1)}, u32[]{:S(2)}, u32[]{:S(2)}) collective-permute-start(f32[536,128]{1,0:T(8,128)S(1)} %get-tuple-element.31), channel_id=1, source_target_pairs={{0,56},{8,0},{16,8},{24,16},{32,24},{40,32},{48,40},{56,48},{1,57}... | collective-permute-start | bytes 823304 | tf_op jit(solution)/shard_map/ppermute | solution.py:619
  47.0 1.2 %collective-permute-start.4 = (f32[304,128]{1,0:T(8,128)S(1)}, f32[304,128]{1,0:T(8,128)S(1)}, u32[]{:S(2)}, u32[]{:S(2)}) collective-permute-start(f32[304,128]{1,0:T(8,128)S(1)} %get-tuple-element.30), channel_id=1, source_target_pairs={{0,8},{8,16},{16,24},{24,32},{32,40},{40,48},{48,56},{56,0},{1,9},... | collective-permute-start | bytes 466952 | tf_op jit(solution)/shard_map/ppermute | solution.py:619
  48.2 0.4 shard_map.39.half
  48.6 1.8 %collective-permute-done.4.y_low = f32[304,128]{1,0:T(8,128)S(1)} collective-permute-done((f32[304,128]{1,0:T(8,128)S(1)}, f32[304,128]{1,0:T(8,128)S(1)}, u32[]{:S(2)}, u32[]{:S(2)}) %collective-permute-start.4) | collective-permute-done | bytes 155680 | tf_op jit(solution)/shard_map/ppermute | solution.py:619
  50.4 2.3 %collective-permute-done.5.y_high = f32[536,128]{1,0:T(8,128)S(1)} collective-permute-done((f32[536,128]{1,0:T(8,128)S(1)}, f32[536,128]{1,0:T(8,128)S(1)}, u32[]{:S(2)}, u32[]{:S(2)}) %collective-permute-start.5) | collective-permute-done | bytes 274464 | tf_op jit(solution)/shard_map/ppermute | solution.py:619
  52.6 3.1 %shard_map.41 = (f32[11,14,16,256]{3,2,1,0:T(8,128)S(1)}, f32[4,14,16,256]{3,2,1,0:T(8,128)S(1)}, f32[7,4,8,128]{3,2,1,0:T(8,128)S(1)}, f32[160,128]{1,0:T(8,128)S(1)}, f32[120,128]{1,0:T(8,128)S(1)}) custom-call(s32[4,8,128]{2,1,0:T(8,128)S(1)} %broadcast.7.place, f32[11,14,8,256]{3,2,1,0:T(8,128)S(1)} %shard_map.39.half, ...), custom_call_target="tpu_custom_call" | custom-call | tf_op jit(solution)/shard_map/pallas_call | solution.py:24
  55.7 1.9 %collective-permute-start.7 = (f32[160,128]{1,0:T(8,128)S(1)}, f32[160,128]{1,0:T(8,128)S(1)}, u32[]{:S(2)}, u32[]{:S(2)}) collective-permute-start(f32[160,128]{1,0:T(8,128)S(1)} %get-tuple-element.41), channel_id=1, source_target_pairs={{64,0},{128,64},{192,128},{256,192},{320,256},{384,320},{448,384},... | collective-permute-start | bytes 245768 | tf_op jit(solution)/shard_map/ppermute | solution.py:625
  57.6 3.4 %collective-permute-start.6 = (f32[120,128]{1,0:T(8,128)S(1)}, f32[120,128]{1,0:T(8,128)S(1)}, u32[]{:S(2)}, u32[]{:S(2)}) collective-permute-start(f32[120,128]{1,0:T(8,128)S(1)} %get-tuple-element.40), channel_id=1, source_target_pairs={{0,64},{64,128},{128,192},{192,256},{256,320},{320,384},{384,448},... | collective-permute-start | bytes 184328 | tf_op jit(solution)/shard_map/ppermute | solution.py:622
  61.0 2.8 %collective-permute-done.6.from_low = f32[120,128]{1,0:T(8,128)S(1)} collective-permute-done((f32[120,128]{1,0:T(8,128)S(1)}, f32[120,128]{1,0:T(8,128)S(1)}, u32[]{:S(2)}, u32[]{:S(2)}) %collective-permute-start.6) | collective-permute-done | bytes 61472 | tf_op jit(solution)/shard_map/ppermute | solution.py:622
  63.9 1.6 %collective-permute-start.9 = (f32[408,128]{1,0:T(8,128)S(1)}, f32[408,128]{1,0:T(8,128)S(1)}, u32[]{:S(2)}, u32[]{:S(2)}) collective-permute-start(f32[408,128]{1,0:T(8,128)S(1)} %get-tuple-element.44), channel_id=1, source_target_pairs={{0,56},{8,0},{16,8},{24,16},{32,24},{40,32},{48,40},{56,48},{1,57}... | collective-permute-start | bytes 626696 | tf_op jit(solution)/shard_map/ppermute | solution.py:619
  65.5 0.3 collective-permute-start.8
  65.7 0.4 shard_map.42
  66.2 1.7 %collective-permute-done.8.y_low = f32[296,128]{1,0:T(8,128)S(1)} collective-permute-done((f32[296,128]{1,0:T(8,128)S(1)}, f32[296,128]{1,0:T(8,128)S(1)}, u32[]{:S(2)}, u32[]{:S(2)}) %collective-permute-start.8) | collective-permute-done | bytes 151584 | tf_op jit(solution)/shard_map/ppermute | solution.py:619
  67.9 1.6 %collective-permute-done.9.y_high = f32[408,128]{1,0:T(8,128)S(1)} collective-permute-done((f32[408,128]{1,0:T(8,128)S(1)}, f32[408,128]{1,0:T(8,128)S(1)}, u32[]{:S(2)}, u32[]{:S(2)}) %collective-permute-start.9) | collective-permute-done | bytes 208928 | tf_op jit(solution)/shard_map/ppermute | solution.py:619
  69.5 2.2 %shard_map.44 = f32[4,8,8,128]{3,2,1,0:T(8,128)} custom-call(s32[4,8,128]{2,1,0:T(8,128)S(1)} %broadcast.7.place, f32[3,6,9,16,256]{4,3,2,1,0:T(8,128)S(1)} %get-tuple-element.34.last_sums, f32[3,9,16,256]{3,2,1,0:T(8,128)S(1)} %get-tuple-element.35.base, f32[3,9,16,256]{3,2,1,0:T(8,128)S(1)} %get-tuple-element.36.inv, ...), custom_call_target="tpu_custom_call" | custom-call | tf_op jit(solution)/shard_map/pallas_call | solution.py:24
  (6 shorter events, 0.2 us)
Async XLA Ops:
  1.9 25.3 %collective-permute-start = (f32[11,8,128]{2,1,0:T(8,128)S(1)}, f32[11,8,128]{2,1,0:T(8,128)S(1)}, u32[]{:S(2)}, u32[]{:S(2)}) collective-permute-start(f32[11,8,128]{2,1,0:T(8,128)S(1)} %get-tuple-element.26), channel_id=1, source_target_pairs={{1,2},{2,1},{3,4},{4,3},{5,6},{6,5},{9,10},{10,9},{11,12},{12,11},... | collective-permute-start | bytes 135176 | tf_op jit(solution)/shard_map/ppermute | solution.py:616
  3.9 23.4 %collective-permute-start.1 = (f32[11,8,128]{2,1,0:T(8,128)S(1)}, f32[11,8,128]{2,1,0:T(8,128)S(1)}, u32[]{:S(2)}, u32[]{:S(2)}) collective-permute-start(f32[11,8,128]{2,1,0:T(8,128)S(1)} %get-tuple-element.27), channel_id=1, source_target_pairs={{0,1},{1,0},{2,3},{3,2},{4,5},{5,4},{6,7},{7,6},{8,9},{9,8},{10,11... | collective-permute-start | bytes 135176 | tf_op jit(solution)/shard_map/ppermute | solution.py:616
  27.4 10.7 %collective-permute-start.3 = (f32[48,8,128]{2,1,0:T(8,128)S(1)}, f32[48,8,128]{2,1,0:T(8,128)S(1)}, u32[]{:S(2)}, u32[]{:S(2)}) collective-permute-start(f32[48,8,128]{2,1,0:T(8,128)S(1)} %get-tuple-element.29), channel_id=1, source_target_pairs={{64,0},{128,64},{192,128},{256,192},{320,256},{384,320},{448,384},... | collective-permute-start | bytes 589832 | tf_op jit(solution)/shard_map/ppermute | solution.py:625
  31.1 6.9 %collective-permute-start.2 = (f32[32,8,128]{2,1,0:T(8,128)S(1)}, f32[32,8,128]{2,1,0:T(8,128)S(1)}, u32[]{:S(2)}, u32[]{:S(2)}) collective-permute-start(f32[32,8,128]{2,1,0:T(8,128)S(1)} %get-tuple-element.28), channel_id=1, source_target_pairs={{0,64},{64,128},{128,192},{192,256},{256,320},{320,384},{384,448},... | collective-permute-start | bytes 393224 | tf_op jit(solution)/shard_map/ppermute | solution.py:622
  38.2 14.5 %collective-permute-start.5 = (f32[536,128]{1,0:T(8,128)S(1)}, f32[536,128]{1,0:T(8,128)S(1)}, u32[]{:S(2)}, u32[]{:S(2)}) collective-permute-start(f32[536,128]{1,0:T(8,128)S(1)} %get-tuple-element.31), channel_id=1, source_target_pairs={{0,56},{8,0},{16,8},{24,16},{32,24},{40,32},{48,40},{56,48},{1,57}... | collective-permute-start | bytes 823304 | tf_op jit(solution)/shard_map/ppermute | solution.py:619
  47.0 3.4 %collective-permute-start.4 = (f32[304,128]{1,0:T(8,128)S(1)}, f32[304,128]{1,0:T(8,128)S(1)}, u32[]{:S(2)}, u32[]{:S(2)}) collective-permute-start(f32[304,128]{1,0:T(8,128)S(1)} %get-tuple-element.30), channel_id=1, source_target_pairs={{0,8},{8,16},{16,24},{24,32},{32,40},{40,48},{48,56},{56,0},{1,9},... | collective-permute-start | bytes 466952 | tf_op jit(solution)/shard_map/ppermute | solution.py:619
  55.7 8.1 %collective-permute-start.7 = (f32[160,128]{1,0:T(8,128)S(1)}, f32[160,128]{1,0:T(8,128)S(1)}, u32[]{:S(2)}, u32[]{:S(2)}) collective-permute-start(f32[160,128]{1,0:T(8,128)S(1)} %get-tuple-element.41), channel_id=1, source_target_pairs={{64,0},{128,64},{192,128},{256,192},{320,256},{384,320},{448,384},... | collective-permute-start | bytes 245768 | tf_op jit(solution)/shard_map/ppermute | solution.py:625
  57.6 6.2 %collective-permute-start.6 = (f32[120,128]{1,0:T(8,128)S(1)}, f32[120,128]{1,0:T(8,128)S(1)}, u32[]{:S(2)}, u32[]{:S(2)}) collective-permute-start(f32[120,128]{1,0:T(8,128)S(1)} %get-tuple-element.40), channel_id=1, source_target_pairs={{0,64},{64,128},{128,192},{192,256},{256,320},{320,384},{384,448},... | collective-permute-start | bytes 184328 | tf_op jit(solution)/shard_map/ppermute | solution.py:622
  63.9 5.6 %collective-permute-start.9 = (f32[408,128]{1,0:T(8,128)S(1)}, f32[408,128]{1,0:T(8,128)S(1)}, u32[]{:S(2)}, u32[]{:S(2)}) collective-permute-start(f32[408,128]{1,0:T(8,128)S(1)} %get-tuple-element.44), channel_id=1, source_target_pairs={{0,56},{8,0},{16,8},{24,16},{32,24},{40,32},{48,40},{56,48},{1,57}... | collective-permute-start | bytes 626696 | tf_op jit(solution)/shard_map/ppermute | solution.py:619
  65.5 2.4 %collective-permute-start.8 = (f32[296,128]{1,0:T(8,128)S(1)}, f32[296,128]{1,0:T(8,128)S(1)}, u32[]{:S(2)}, u32[]{:S(2)}) collective-permute-start(f32[296,128]{1,0:T(8,128)S(1)} %get-tuple-element.43), channel_id=1, source_target_pairs={{0,8},{8,16},{16,24},{24,32},{32,40},{40,48},{48,56},{56,0},{1,9},... | collective-permute-start | bytes 454664 | tf_op jit(solution)/shard_map/ppermute | solution.py:619
